TPU v7x, 32 devices: a whole 2x2x4 slice. The times are simulated.
32 devices in a mesh: parts: 1, var: 8 (over z, core), patch: 4 (over y, x).
Axes of the slice: x: 2, y: 2, z: 4, core: 2. Of those that a mesh axis runs over, the one named last changes fastest.
Arguments:
- tokens: bfloat16 [256, 24, 768], P('patch', ('parts', 'var')), may hold values from -6 to 6
- patch_mask: int32 [256, 24], P('patch', ('parts', 'var')), may hold values 0 or 1
- group_ids: int32 [24], P('parts'), may hold values from 0 to 7, never falling along the last dimension, each value on 1 to 6 neighbouring positions
- time_gain: float32 [768], replicated, may hold values from 0.1 to 1.9
- time_qkv: bfloat16 [768, 3, 768], P(None, None, 'patch'), may hold values from -0.21875 to 0.21875
- time_out: bfloat16 [768, 768], P('patch'), may hold values from -0.21875 to 0.21875
- space_gain: float32 [768], replicated, may hold values from 0.1 to 1.9
- space_qkv: bfloat16 [768, 3, 768], P(None, None, 'patch'), may hold values from -0.21875 to 0.21875
- space_out: bfloat16 [768, 768], P('patch'), may hold values from -0.21875 to 0.21875
Outputs:
- panel_out: bfloat16 [256, 24, 768], P('patch', ('parts', 'var'))
Inputs may be any that keep to these rules, and one draw needn't show every extreme that they name: group_ids never falls along the variates; each group is a run of 1 to 6 consecutive variates.
All inputs are finite; a program needn't handle non-finite values. No bound on the sum of `patch_mask` on one device may be relied on, other than what follows from the above.
Results may differ from a plain program's by a relative error of at most 0.017.
Values may be sent and summed in bfloat16 or wider, within the bound.
No kernel may reach another device: no remote copies, remote signals or barrier semaphores. Data moves between devices by JAX's collectives and lax.ppermute only.
A program may use at most 64 MiB of HBM per device.

v0:
```python
import jax
import jax.numpy as jnp
from jax import lax
from jax.sharding import PartitionSpec as P

HD = 64


epsilon = 1e-06


def passed_along(block, axis, distance):
    devices = range(lax.axis_size(axis))
    route = [(i - distance, i) for i in devices if i - distance in devices]
    return lax.ppermute(block, axis, route)


def norm_rows(block_rows, gain):
    floats = block_rows.astype(jnp.float32)
    scaled = floats * lax.rsqrt(jnp.mean(floats * floats, axis=-1, keepdims=True) + epsilon)
    return (scaled * gain).astype(jnp.bfloat16)


def soft_weights(scores, allowed):
    masked = jnp.where(allowed, scores, -jnp.inf)
    highest = jnp.max(masked, axis=-1, keepdims=True)
    raised = jnp.exp(masked - highest)
    return (raised / jnp.sum(raised, axis=-1, keepdims=True)).astype(jnp.bfloat16)


def make_term(attended, out_weight):
    return jnp.einsum("pvk,kd->pvd", attended, out_weight, preferred_element_type=jnp.float32)


def time_attend(normed, labels, weight):
    patch_count, var_count = (normed.shape[0], normed.shape[1])
    head_width = weight.shape[2]
    head_count = head_width // HD
    projected = jnp.einsum(
        "pvd,dtk->pvtk", normed, weight, preferred_element_type=jnp.float32
    ).astype(jnp.bfloat16)
    queries = projected[:, :, 0].reshape(patch_count, var_count, head_count, HD)
    key_rows = projected[:, :, 1].reshape(patch_count, var_count, head_count, HD)
    value_rows = projected[:, :, 2].reshape(patch_count, var_count, head_count, HD)
    scores = jnp.einsum(
        "qvhe,kvhe->vhqk", queries, key_rows, preferred_element_type=jnp.float32
    ) * HD ** (-0.5)
    query_pos = jnp.arange(patch_count)[:, None]
    key_pos = jnp.arange(patch_count)[None, :]
    observed = (labels.T > 0.5)[:, None, None, :]
    allowed = (key_pos <= query_pos)[None, None] & (observed | (key_pos == query_pos)[None, None])
    weights = soft_weights(scores, allowed)
    attended = jnp.einsum(
        "vhqk,kvhe->qvhe", weights, value_rows, preferred_element_type=jnp.float32
    ).astype(jnp.bfloat16)
    return attended.reshape(patch_count, var_count, head_width)


def space_attend(normed, group_ids, weight):
    patch_count, var_count = (normed.shape[0], normed.shape[1])
    head_width = weight.shape[2]
    head_count = head_width // HD
    projected = jnp.einsum(
        "pvd,dtk->pvtk", normed, weight, preferred_element_type=jnp.float32
    ).astype(jnp.bfloat16)
    queries = projected[:, :, 0].reshape(patch_count, var_count, head_count, HD)
    paired = projected[:, :, 1:3].reshape(patch_count, var_count, 2 * head_width)
    lower_list = []
    upper_list = []
    moving = paired
    for repeat in range(2):
        moving = passed_along(moving, "var", 1)
        lower_list.insert(0, moving)
    moving = paired
    for repeat in range(2):
        moving = passed_along(moving, "var", -1)
        upper_list.append(moving)
    window = jnp.concatenate(lower_list + [paired] + upper_list, axis=1)
    window_count = window.shape[1]
    key_window = window[:, :, :head_width].reshape(patch_count, window_count, head_count, HD)
    value_window = window[:, :, head_width:].reshape(patch_count, window_count, head_count, HD)
    device_index = lax.axis_index("var")
    outside = jnp.full((2 * var_count,), -1, jnp.int32)
    padded_ids = jnp.concatenate([outside, group_ids, outside])
    key_ids = lax.dynamic_slice_in_dim(padded_ids, device_index * var_count, window_count)
    query_ids = lax.dynamic_slice_in_dim(group_ids, device_index * var_count, var_count)
    scores = jnp.einsum(
        "pqhe,pkhe->phqk", queries, key_window, preferred_element_type=jnp.float32
    ) * HD ** (-0.5)
    allowed = (query_ids[:, None] == key_ids[None, :])[None, None]
    weights = soft_weights(scores, allowed)
    attended = jnp.einsum(
        "phqk,pkhe->pqhe", weights, value_window, preferred_element_type=jnp.float32
    ).astype(jnp.bfloat16)
    return attended.reshape(patch_count, var_count, head_width)


def on_device(
    tokens, patch_mask, group_ids, time_gain, time_qkv, time_out, space_gain, space_qkv, space_out
):
    mark_rows = patch_mask.astype(jnp.bfloat16)
    own_normed = norm_rows(tokens, time_gain)
    gathered, labels = (
        lax.all_gather(own_normed, "patch", axis=0, tiled=True),
        lax.all_gather(mark_rows, "patch", axis=0, tiled=True),
    )
    attended = time_attend(gathered, labels, time_qkv)
    summed = lax.psum_scatter(
        make_term(attended, time_out).astype(jnp.bfloat16), "patch", scatter_dimension=0, tiled=True
    ).astype(jnp.float32)
    residual = (tokens.astype(jnp.float32) + summed).astype(jnp.bfloat16)
    space_normed = lax.all_gather(norm_rows(residual, space_gain), "patch", axis=0, tiled=True)
    space_result = space_attend(space_normed, group_ids, space_qkv)
    space_summed = lax.psum_scatter(
        make_term(space_result, space_out).astype(jnp.bfloat16),
        "patch",
        scatter_dimension=0,
        tiled=True,
    ).astype(jnp.float32)
    return (residual.astype(jnp.float32) + space_summed).astype(jnp.bfloat16)


def solution(mesh):
    in_specs = (
        P("patch", ("parts", "var"), None),
        P("patch", ("parts", "var")),
        P("parts"),
        P(),
        P(None, None, "patch"),
        P("patch", None),
        P(),
        P(None, None, "patch"),
        P("patch", None),
    )
    out_specs = P("patch", ("parts", "var"), None)
    return jax.shard_map(
        on_device, mesh=mesh, in_specs=in_specs, out_specs=out_specs, check_vma=False
    )
```

profile of v0, /device:TPU:9, one launch (start us, length us, event | category | flops | bytes accessed | tf_op | source)
XLA Modules:
  0.0 194.5 jit_solution(7199102504552056548)
XLA Ops:
  6.5 0.0 copy-start
  6.5 0.0 all-gather.4.cloned.1.call-start
  6.5 1.2 fusion.14
  7.7 1.8 fusion.16
  9.5 0.0 all-gather.4.cloned.1.call-update
  9.6 0.0 reduce-scatter.3.cloned.1.call-start
  9.6 0.7 convert_bitcast_fusion
  10.3 6.0 %all-gather = bf16[4,64,3]{1,2,0:T(4,128)(2,1)S(1)} all-gather(bf16[1,64,3]{1,2,0:T(4,128)(2,1)S(1)} %convert_bitcast_fusion), channel_id=1, replica_groups=mesh['parts'=1,'var'=8,'patch'=4] {'patch'}, dimensions={0}, use_global_device_ids=true | all-gather | bytes 1920 | tf_op jit(solution)/shard_map/all_gather | solution.py:105
  16.4 0.1 reshape.108
  16.5 0.2 or_and_fusion
  16.7 21.9 %all-gather.4.cloned.1.call-done = bf16[256,3,768]{2,0,1:T(8,128)(2,1)} async-done(((bf16[64,3,768]{2,0,1:T(8,128)(2,1)}), bf16[256,3,768]{2,0,1:T(8,128)(2,1)}) %all-gather.4.cloned.1.call-update) | async-done | bytes 1179664 | tf_op jit(solution)/shard_map/all_gather | solution.py:104
  38.6 0.0 copy-done
  38.6 2.2 %convolution_convert_fusion.3 = bf16[256,3,3,192]{0,3,2,1:T(8,128)(2,1)S(1)} fusion(bf16[256,3,768]{2,0,1:T(8,128)(2,1)} %all-gather.4.cloned.1.call-done, bf16[768,3,192]{0,2,1:T(8,128)(2,1)S(1)} %copy-done), kind=kOutput, calls=%fused_computation.13 | convolution fusion | flops 679919616 | bytes 2949120 | tf_op jit(solution)/shard_map/pvd,dtk->pvtk/dot_general | solution.py:39
  40.8 0.1 fusion.29
  40.9 2.4 %fusion.30 = (f32[3,3,256]{2,1,0:T(4,128)S(1)}, f32[3,3,256,256]{2,3,1,0:T(8,128)}) fusion(pred[3,256,256]{1,2,0:T(8,128)(4,1)S(1)} %or_and_fusion, bf16[256,3,3,64]{0,3,2,1:T(8,128)(2,1)S(1)} %bitcast.57, bf16[256,3,3,64]{0,3,2,1:T(8,128)(2,1)S(1)} %bitcast.56), kind=kOutput, calls=%fused_computation.60 | convolution fusion | flops 77857024 | bytes 3154944 | tf_op jit(solution)/shard_map/sub | solution.py:27
  43.2 2.0 %convolution_convert_fusion.5 = bf16[3,3,64,256]{3,2,1,0:T(8,128)(2,1)S(1)} fusion(bf16[256,3,3,64]{0,3,2,1:T(8,128)(2,1)S(1)} %bitcast.55, f32[3,3,256,256]{2,3,1,0:T(8,128)} %get-tuple-element.11, f32[3,3,256]{2,1,0:T(4,128)S(1)} %get-tuple-element.10), kind=kOutput, calls=%fused_computation.16 | convolution fusion | flops 76824576 | bytes 2958336 | tf_op jit(solution)/shard_map/vhqk,kvhe->qvhe/dot_general | solution.py:53
  45.3 0.0 copy-start.1
  45.3 0.0 copy-start.5
  45.3 0.0 copy-done.3
  45.3 1.5 convolution_convert_fusion.1
  46.9 0.0 reduce-scatter.3.cloned.1.call-update
  46.9 0.0 all-gather.6.cloned.1.call-start
  46.9 28.6 %reduce-scatter.3.cloned.1.call-done = bf16[64,3,768]{2,0,1:T(8,128)(2,1)} async-done(((bf16[256,3,768]{2,0,1:T(8,128)(2,1)}), bf16[64,3,768]{2,0,1:T(8,128)(2,1)}) %reduce-scatter.3.cloned.1.call-update) | async-done | bytes 294928 | tf_op jit(solution)/shard_map/reduce_scatter | solution.py:108
  75.6 0.0 copy-done.1
  75.6 1.1 fusion.18
  76.7 0.0 copy-done.5
  76.7 1.8 fusion.20
  78.5 0.0 all-gather.6.cloned.1.call-update
  78.6 0.0 copy-start.6
  78.6 0.0 reduce-scatter.5.cloned.1.call-start
  78.6 27.8 %all-gather.6.cloned.1.call-done = bf16[256,3,768]{2,0,1:T(8,128)(2,1)} async-done(((bf16[64,3,768]{2,0,1:T(8,128)(2,1)}), bf16[256,3,768]{2,0,1:T(8,128)(2,1)}) %all-gather.6.cloned.1.call-update) | async-done | bytes 1179664 | tf_op jit(solution)/shard_map/all_gather | solution.py:112
  106.4 2.4 %convolution_convert_fusion.2 = bf16[256,3,3,192]{0,3,2,1:T(8,128)(2,1)S(1)} fusion(bf16[256,3,768]{2,0,1:T(8,128)(2,1)} %all-gather.6.cloned.1.call-done, bf16[768,3,192]{0,2,1:T(8,128)(2,1)} %param.16), kind=kOutput, calls=%fused_computation.12 | convolution fusion | flops 679919616 | bytes 2949120 | tf_op jit(solution)/shard_map/pvd,dtk->pvtk/dot_general | solution.py:63
  108.9 3.7 %collective-permute-start = (bf16[256,3,384]{0,2,1:T(8,128)(2,1)S(1)}, bf16[256,3,384]{0,2,1:T(8,128)(2,1)}, u32[]{:S(2)}, u32[]{:S(2)}) collective-permute-start(bf16[256,3,384]{0,2,1:T(8,128)(2,1)S(1)} %bitcast.50), channel_id=1, source_target_pairs={{0,4},{4,8},{8,12},{12,16},{16,20},{20,24},{24,28},{1,5},{5,9},{9,... | collective-permute-start | bytes 1769480 | tf_op jit(solution)/shard_map/ppermute | solution.py:15
  112.6 1.9 collective-permute-start.2
  114.5 4.9 %collective-permute-done = bf16[256,3,384]{0,2,1:T(8,128)(2,1)} collective-permute-done((bf16[256,3,384]{0,2,1:T(8,128)(2,1)S(1)}, bf16[256,3,384]{0,2,1:T(8,128)(2,1)}, u32[]{:S(2)}, u32[]{:S(2)}) %collective-permute-start) | collective-permute-done | bytes 589856 | tf_op jit(solution)/shard_map/ppermute | solution.py:15
  119.4 4.5 %collective-permute-start.1 = (bf16[256,3,384]{0,2,1:T(8,128)(2,1)}, bf16[256,3,384]{0,2,1:T(8,128)(2,1)}, u32[]{:S(2)}, u32[]{:S(2)}) collective-permute-start(bf16[256,3,384]{0,2,1:T(8,128)(2,1)} %collective-permute-done), channel_id=1, source_target_pairs={{0,4},{4,8},{8,12},{12,16},{16,20},{20,24},{24,28},{1,5},{5,9},{9,... | collective-permute-start | bytes 1769480 | tf_op jit(solution)/shard_map/ppermute | solution.py:15
  123.9 0.0 copy-done.6
  123.9 0.1 dynamic_slice.6
  124.0 0.1 pad_add_fusion
  124.0 0.1 dynamic_slice.7
  124.1 0.0 collective-permute-done.2
  124.1 1.9 collective-permute-start.3
  126.0 0.1 broadcast_compare_fusion
  126.1 0.6 copy.26
  126.7 4.3 %collective-permute-done.1 = bf16[256,3,384]{0,2,1:T(8,128)(2,1)} collective-permute-done((bf16[256,3,384]{0,2,1:T(8,128)(2,1)}, bf16[256,3,384]{0,2,1:T(8,128)(2,1)}, u32[]{:S(2)}, u32[]{:S(2)}) %collective-permute-start.1) | collective-permute-done | bytes 589856 | tf_op jit(solution)/shard_map/ppermute | solution.py:15
  131.0 1.1 constant_dynamic-update-slice_fusion.4
  132.1 1.1 constant_dynamic-update-slice_fusion.3
  133.3 1.1 constant_dynamic-update-slice_fusion.1
  134.4 1.3 collective-permute-done.3
  135.6 1.1 constant_dynamic-update-slice_fusion
  136.7 1.4 fusion.28
  138.1 5.2 %copy.27 = bf16[256,15,3,64]{3,1,2,0:T(8,128)(2,1)} copy(bf16[256,15,3,64]{0,3,2,1:T(8,128)(2,1)} %bitcast.49) | data formatting | bytes 2949120 | tf_op jit(solution)/shard_map/reshape | solution.py:80
  143.3 3.9 %copy.28 = bf16[256,15,3,64]{3,1,2,0:T(8,128)(2,1)} copy(bf16[256,15,3,64]{0,3,2,1:T(8,128)(2,1)S(1)} %bitcast.48) | data formatting | bytes 2949120 | tf_op jit(solution)/shard_map/reshape | solution.py:81
  147.3 5.0 %fusion.31 = (f32[256,3,3]{2,1,0:T(4,128)S(1)}, f32[256,3,3,15]{3,2,1,0:T(4,128)}) fusion(bf16[256,3,3,64]{3,1,2,0:T(4,128)(2,1)S(1)} %copy.26, bf16[256,15,3,64]{3,1,2,0:T(8,128)(2,1)} %copy.27, pred[3,15]{1,0:T(4,128)(4,1)S(1)} %broadcast_compare_fusion), kind=kOutput, calls=%fused_computation.61 | convolution fusion | flops 4561934 | bytes 1916973 | tf_op jit(solution)/shard_map/sub | solution.py:27
  152.3 0.0 copy-start.4
  152.3 3.6 %fusion.5 = bf16[256,3,3,64]{3,1,2,0:T(4,128)(2,1)S(1)} fusion(bf16[256,15,3,64]{3,1,2,0:T(8,128)(2,1)} %copy.28, f32[256,3,3,15]{3,2,1,0:T(4,128)} %get-tuple-element.13, f32[256,3,3]{2,1,0:T(4,128)S(1)} %get-tuple-element.12), kind=kOutput, calls=%fused_computation.15 | convolution fusion | flops 4640256 | bytes 1916928 | tf_op jit(solution)/shard_map/phqk,pkhe->pqhe/dot_general | solution.py:92
  155.9 0.0 copy-start.2
  155.9 0.5 copy.29
  156.5 0.0 copy-done.4
  156.5 1.5 convolution_convert_fusion
  158.0 0.0 reduce-scatter.5.cloned.1.call-update
  158.0 28.2 %reduce-scatter.5.cloned.1.call-done = bf16[64,3,768]{2,0,1:T(8,128)(2,1)} async-done(((bf16[256,3,768]{2,0,1:T(8,128)(2,1)}), bf16[64,3,768]{2,0,1:T(8,128)(2,1)}) %reduce-scatter.5.cloned.1.call-update) | async-done | bytes 294928 | tf_op jit(solution)/shard_map/reduce_scatter | solution.py:114
  186.2 0.0 copy-done.2
  186.2 1.8 fusion.21
  (9 shorter events, 0.2 us)
Async XLA Ops:
  6.5 32.1 %copy-start = (bf16[768,3,192]{0,2,1:T(8,128)(2,1)S(1)}, bf16[768,3,192]{0,2,1:T(8,128)(2,1)}, u32[]{:S(2)}) copy-start(bf16[768,3,192]{0,2,1:T(8,128)(2,1)} %param.13) | copy-start | bytes 2654212
  6.5 32.1 %all-gather.4.cloned.1.call-start = ((), (), s32[]{:S(2)}) async-start(), calls=%async_computation.2 | async-start | bytes 1474560 | tf_op jit(solution)/shard_map/all_gather | solution.py:104
  9.6 66.0 %reduce-scatter.3.cloned.1.call-start = ((), (), s32[]{:S(2)}) async-start(), calls=%async_computation.3 | async-start | bytes 1474560 | tf_op jit(solution)/shard_map/reduce_scatter | solution.py:108
  43.2 2.1 %copy-start.3 = (bf16[192,768]{1,0:T(8,128)(2,1)S(1)}, bf16[192,768]{1,0:T(8,128)(2,1)}, u32[]{:S(2)}) copy-start(bf16[192,768]{1,0:T(8,128)(2,1)} %param.14) | copy-start | bytes 884740
  45.3 30.3 %copy-start.1 = (bf16[64,3,768]{2,0,1:T(8,128)(2,1)S(1)}, bf16[64,3,768]{2,0,1:T(8,128)(2,1)}, u32[]{:S(2)}) copy-start(bf16[64,3,768]{2,0,1:T(8,128)(2,1)} %param.9) | copy-start | bytes 884740
  45.3 31.4 %copy-start.5 = (f32[768]{0:T(1024)S(1)}, f32[768]{0:T(1024)}, u32[]{:S(2)}) copy-start(f32[768]{0:T(1024)} %param.15) | copy-start | bytes 9220
  46.9 59.6 %all-gather.6.cloned.1.call-start = ((), (), s32[]{:S(2)}) async-start(), calls=%async_computation.4 | async-start | bytes 1474560 | tf_op jit(solution)/shard_map/all_gather | solution.py:112
  78.6 45.3 %copy-start.6 = (s32[24]{0:T(128)S(1)}, s32[24]{0:T(128)}, u32[]{:S(2)}) copy-start(s32[24]{0:T(128)} %param.11) | copy-start | bytes 292
  78.6 107.6 %reduce-scatter.5.cloned.1.call-start = ((), (), s32[]{:S(2)}) async-start(), calls=%async_computation.5 | async-start | bytes 1474560 | tf_op jit(solution)/shard_map/reduce_scatter | solution.py:114
  108.9 10.5 %collective-permute-start = (bf16[256,3,384]{0,2,1:T(8,128)(2,1)S(1)}, bf16[256,3,384]{0,2,1:T(8,128)(2,1)}, u32[]{:S(2)}, u32[]{:S(2)}) collective-permute-start(bf16[256,3,384]{0,2,1:T(8,128)(2,1)S(1)} %bitcast.50), channel_id=1, source_target_pairs={{0,4},{4,8},{8,12},{12,16},{16,20},{20,24},{24,28},{1,5},{5,9},{9,... | collective-permute-start | bytes 1769480 | tf_op jit(solution)/shard_map/ppermute | solution.py:15
  112.6 11.6 %collective-permute-start.2 = (bf16[256,3,384]{0,2,1:T(8,128)(2,1)S(1)}, bf16[256,3,384]{0,2,1:T(8,128)(2,1)}, u32[]{:S(2)}, u32[]{:S(2)}) collective-permute-start(bf16[256,3,384]{0,2,1:T(8,128)(2,1)S(1)} %bitcast.51), channel_id=1, source_target_pairs={{4,0},{8,4},{12,8},{16,12},{20,16},{24,20},{28,24},{5,1},{9,5},{13... | collective-permute-start | bytes 1769480 | tf_op jit(solution)/shard_map/ppermute | solution.py:15
  119.4 11.6 %collective-permute-start.1 = (bf16[256,3,384]{0,2,1:T(8,128)(2,1)}, bf16[256,3,384]{0,2,1:T(8,128)(2,1)}, u32[]{:S(2)}, u32[]{:S(2)}) collective-permute-start(bf16[256,3,384]{0,2,1:T(8,128)(2,1)} %collective-permute-done), channel_id=1, source_target_pairs={{0,4},{4,8},{8,12},{12,16},{16,20},{20,24},{24,28},{1,5},{5,9},{9,... | collective-permute-start | bytes 1769480 | tf_op jit(solution)/shard_map/ppermute | solution.py:15
  124.1 11.5 %collective-permute-start.3 = (bf16[256,3,384]{0,2,1:T(8,128)(2,1)}, bf16[256,3,384]{0,2,1:T(8,128)(2,1)}, u32[]{:S(2)}, u32[]{:S(2)}) collective-permute-start(bf16[256,3,384]{0,2,1:T(8,128)(2,1)} %collective-permute-done.2), channel_id=1, source_target_pairs={{4,0},{8,4},{12,8},{16,12},{20,16},{24,20},{28,24},{5,1},{9,5},{13... | collective-permute-start | bytes 1769480 | tf_op jit(solution)/shard_map/ppermute | solution.py:15
  152.3 4.2 %copy-start.4 = (bf16[192,768]{1,0:T(8,128)(2,1)S(1)}, bf16[192,768]{1,0:T(8,128)(2,1)}, u32[]{:S(2)}) copy-start(bf16[192,768]{1,0:T(8,128)(2,1)} %param.17) | copy-start | bytes 884740
  155.9 30.3 %copy-start.2 = (bf16[64,3,768]{2,0,1:T(8,128)(2,1)S(1)}, bf16[64,3,768]{2,0,1:T(8,128)(2,1)}, u32[]{:S(2)}) copy-start(bf16[64,3,768]{2,0,1:T(8,128)(2,1)} %reduce-scatter.3.cloned.1.call-done) | copy-start | bytes 884740
Sparse Core Ops, SparseCore 0:
  9.7 28.8 all-gather.3
  47.0 28.5 reduce-scatter.2
  78.7 27.7 all-gather.5
  158.2 27.9 reduce-scatter.4
where the time goes:
time: 197 us; the launch traced here: 195 us
  waiting for transfers between devices  117 us (59%)
  matrix products  20.7 us (11%)
  local copies, waits for them, and re-layouts  16.5 us (8%)
  between operations  13.3 us (7%)
  starting transfers between devices  12.1 us (6%)
  other arithmetic  8.81 us (4%)
  blocking collectives  6.04 us (3%)
    reduce_scatter x1, waiting for transfers between devices, on_device(): lax.psum_scatter(make_term(attended, time_out).astype(jnp.bfloat16), 'pat...  28.6 us
    reduce_scatter x1, waiting for transfers between devices, on_device(): lax.psum_scatter(make_term(space_result, space_out).astype(jnp.bfloat16),...  28.2 us
    all_gather x1, waiting for transfers between devices, on_device(): lax.all_gather(norm_rows(residual, space_gain), 'patch', axis=0, tiled=True)  27.8 us
    all_gather x1, waiting for transfers between devices, on_device(): lax.all_gather(own_normed, 'patch', axis=0, tiled=True)  21.9 us
    ppermute x4, starting transfers between devices, passed_along(): return lax.ppermute(block, axis, route)  12 us
    ppermute x4, waiting for transfers between devices, passed_along(): return lax.ppermute(block, axis, route)  10.4 us
    sub x2, matrix products, soft_weights(): raised = jnp.exp(masked - highest)  7.41 us
    all_gather x1, blocking collectives, on_device(): lax.all_gather(mark_rows, 'patch', axis=0, tiled=True)  6.04 us
  transfers between devices with their start and end apart: 8, of which 7 were waited for; matrix products, arithmetic and copies ran while one was open for 3% of the time, Pallas kernels for 0%

commit v1 on v0

v1 whole, which is shorter than its diff:
```python
import functools

import jax
import jax.numpy as jnp
from jax import lax
from jax.experimental import pallas as pl
from jax.experimental.pallas import tpu as pltpu
from jax.sharding import PartitionSpec as P

HD = 64
epsilon = 1e-06
NT = (((1,), (1,)), ((), ()))
VM = pl.BlockSpec(memory_space=pltpu.VMEM)
SM = pl.BlockSpec(memory_space=pltpu.SMEM)


def params():
    return pltpu.CompilerParams(vmem_limit_bytes=28 * 1024 * 1024)


def cost(flops, size):
    return pl.CostEstimate(flops=flops, bytes_accessed=size, transcendentals=0)


def normed(floats, gain):
    mean = jnp.mean(floats * floats, axis=-1, keepdims=True)
    return (floats * lax.rsqrt(mean + epsilon) * gain).astype(jnp.bfloat16)


def dot_nt(a, b):
    return lax.dot_general(a, b, NT, preferred_element_type=jnp.float32)


def time_kernel(base_ref, t0, t1, t2, t3, mask_ref, gain_ref, w_ref, o0, o1, o2, o3):
    tokens, outs = (t0, t1, t2, t3), (o0, o1, o2, o3)
    var_count, rows, depth = t0.shape
    width = w_ref.shape[0] // 3
    total = rows * len(tokens)
    row = lax.broadcasted_iota(jnp.int32, (total, total), 0)
    col = lax.broadcasted_iota(jnp.int32, (total, total), 1)

    def positions(index):
        where = index + base_ref[0]
        for block in range(1, len(tokens)):
            shift = base_ref[block] - block * rows
            where = jnp.where(index >= block * rows, index + shift, where)
        return where

    query_pos, key_pos = positions(row), positions(col)
    causal, same = key_pos <= query_pos, key_pos == query_pos
    head_of = lax.broadcasted_iota(jnp.int32, (1, width), 1) // HD
    gain = gain_ref[...]
    weight = w_ref[...]
    for v in range(var_count):
        raw = jnp.concatenate([t[v] for t in tokens], axis=0).astype(jnp.float32)
        x = normed(raw, gain)
        projected = dot_nt(x, weight)
        queries = (projected[:, :width].astype(jnp.bfloat16)).astype(jnp.float32) * HD ** (-0.5)
        queries = queries.astype(jnp.bfloat16)
        keys = projected[:, width : 2 * width].astype(jnp.bfloat16)
        values = projected[:, 2 * width :].astype(jnp.bfloat16)
        observed = mask_ref[v : v + 1, :] > 0
        bias = jnp.where(causal & (observed | same), 0.0, -jnp.inf)
        attended = jnp.zeros((total, width), jnp.float32)
        for head in range(width // HD):
            mine = head_of == head
            scores = dot_nt(jnp.where(mine, queries, 0), keys) + bias
            raised = jnp.exp(scores - jnp.max(scores, axis=-1, keepdims=True))
            share = 1.0 / jnp.sum(raised, axis=-1, keepdims=True)
            weights = (raised * share).astype(jnp.bfloat16)
            mixed = jnp.dot(weights, values, preferred_element_type=jnp.float32)
            attended = jnp.where(mine, mixed, attended)
        attended = attended.astype(jnp.bfloat16)
        for block, out in enumerate(outs):
            out[v] = attended[block * rows : (block + 1) * rows]


def mid_kernel(
    place_ref, a0, a1, a2, a3, w0, w1, w2, wa, wb, tok_ref, gain_ref, mid_ref, x_ref, f1_ref, f2_ref, last
):
    half = wa.shape[0]
    core = place_ref[0]
    last[pl.ds(pl.multiple_of(core * half, 32), half), :] = wa[...]
    last[pl.ds(pl.multiple_of((1 - core) * half, 32), half), :] = wb[...]
    var_count, rows, depth = tok_ref.shape
    gain = gain_ref[...]
    for v in range(var_count):
        summed = jnp.dot(a0[v], w0[...], preferred_element_type=jnp.float32)
        for a, w in ((a1, w1), (a2, w2), (a3, last)):
            summed = summed + jnp.dot(a[v], w[...], preferred_element_type=jnp.float32)
        mid = (tok_ref[v].astype(jnp.float32) + summed).astype(jnp.bfloat16)
        mid_ref[v] = mid
        x_ref[v] = normed(mid.astype(jnp.float32), gain)
    far = f1_ref.shape[0]
    f1_ref[...] = x_ref[pl.ds(place_ref[1], far)]
    f2_ref[...] = x_ref[pl.ds(place_ref[2], far)]


def space_kernel(
    place_ref, ids_ref,
    x0, xs, xo, f1, f2, mid_ref,
    w0, w1, w2, wa, wb, u0, u1, u2, ua, ub,
    out_ref,
    far, wall, uall, qbuf, kbuf, vbuf, prob, att,
):
    var_count, rows, depth = x0.shape
    far_count = f1.shape[0]
    kind, width, _ = w0.shape
    half = wa.shape[1]
    core = place_ref[0]
    far[pl.ds(place_ref[3] * far_count, far_count)] = f1[...]
    far[pl.ds(place_ref[4] * far_count, far_count)] = f2[...]
    low = 3 * width
    for group, (w, u) in enumerate(((w0, u0), (w1, u1), (w2, u2))):
        wall[:, group * width : (group + 1) * width, :] = w[...]
        uall[group * width : (group + 1) * width, :] = u[...]
    own_at = pl.multiple_of(low + core * half, 32)
    other_at = pl.multiple_of(low + (1 - core) * half, 32)
    wall[:, pl.ds(own_at, half), :] = wa[...]
    wall[:, pl.ds(other_at, half), :] = wb[...]
    uall[pl.ds(own_at, half), :] = ua[...]
    uall[pl.ds(other_at, half), :] = ub[...]
    inner = wall.shape[1]
    heads = inner // HD

    window = [x0[v] for v in range(var_count)] + [xs[v] for v in range(var_count)]
    window += [xo[v] for v in range(var_count)] + [far[v] for v in range(2 * far_count)]
    count = len(window)
    x_own = jnp.concatenate(window[:var_count], axis=0)
    scaled = dot_nt(x_own, wall[0]).astype(jnp.bfloat16).astype(jnp.float32) * HD ** (-0.5)
    qbuf[...] = scaled.astype(jnp.bfloat16)
    x_all = jnp.concatenate(window, axis=0)
    kbuf[...] = dot_nt(x_all, wall[1]).astype(jnp.bfloat16)
    vbuf[...] = dot_nt(x_all, wall[2]).astype(jnp.bfloat16)

    def needed(u, w):
        if w < 3 * var_count:
            return True
        w -= 3 * var_count
        if w < far_count:
            offset = u + 2 * var_count - (var_count - far_count) - w
        else:
            offset = 2 * var_count + (w - far_count) - u
        return offset <= 2 * var_count - 1

    lanes = 128
    lane = lax.broadcasted_iota(jnp.int32, (1, lanes), 1)
    lane_u = lane // heads
    sum_row = lax.broadcasted_iota(jnp.int32, (inner, lanes), 0) // HD
    sum_col = lax.broadcasted_iota(jnp.int32, (inner, lanes), 1)
    spread_row = lax.broadcasted_iota(jnp.int32, (lanes, inner), 0)
    spread_col = lax.broadcasted_iota(jnp.int32, (lanes, inner), 1) // HD
    collect = [(sum_row + u * heads == sum_col).astype(jnp.bfloat16) for u in range(var_count)]
    spread = [(spread_col + u * heads == spread_row).astype(jnp.bfloat16) for u in range(var_count)]
    own_id = jnp.full((1, lanes), -2, jnp.int32)
    for u in range(var_count):
        own_id = jnp.where(lane_u == u, ids_ref[u], own_id)
    scores = []
    for w in range(count):
        keys = kbuf[w * rows : (w + 1) * rows, :]
        score = None
        for u in range(var_count):
            if needed(u, w):
                part = jnp.dot(
                    qbuf[u * rows : (u + 1) * rows, :] * keys, collect[u], preferred_element_type=jnp.float32
                )
                score = part if score is None else score + part
        scores.append(jnp.where(own_id == ids_ref[w], score, -jnp.inf))
    highest = functools.reduce(jnp.maximum, scores)
    highest = jnp.where(lane_u < var_count, highest, 0.0)
    raised = [jnp.exp(score - highest) for score in scores]
    total = functools.reduce(lambda a, b: a + b, raised)
    share = 1.0 / jnp.where(lane_u < var_count, total, 1.0)
    for w in range(count):
        prob[w * rows : (w + 1) * rows, :] = (raised[w] * share).astype(jnp.bfloat16)
    for u in range(var_count):
        mixed = None
        for w in range(count):
            if needed(u, w):
                each = jnp.dot(
                    prob[w * rows : (w + 1) * rows, :], spread[u], preferred_element_type=jnp.float32
                )
                term = each * vbuf[w * rows : (w + 1) * rows, :].astype(jnp.float32)
                mixed = term if mixed is None else mixed + term
        att[u * rows : (u + 1) * rows, :] = mixed.astype(jnp.bfloat16)
    summed = jnp.dot(att[...], uall[...], preferred_element_type=jnp.float32)
    for u in range(var_count):
        out_ref[u] = (
            mid_ref[u].astype(jnp.float32) + summed[u * rows : (u + 1) * rows]
        ).astype(jnp.bfloat16)


def routes(var_size, patch_size):
    def route(even, odd):
        pairs = []
        for v in range(var_size):
            for p in range(patch_size):
                step = odd if v % 2 else even
                pairs.append((v * patch_size + p, v * patch_size + (p ^ step)))
        return pairs
    return route(1, 2), route(2, 1), route(3, 3)


def pairs_of(size, partner):
    return [(i, partner(i)) for i in range(size) if 0 <= partner(i) < size]


def on_device(
    tokens, patch_mask, group_ids, time_gain, time_qkv, time_out, space_gain, space_qkv, space_out
):
    var_size, patch_size = lax.axis_size("var"), lax.axis_size("patch")
    var_index, patch_index = lax.axis_index("var"), lax.axis_index("patch")
    core, level = var_index % 2, (var_index // 2) % 2
    both = ("var", "patch")
    first, second, third = routes(var_size, patch_size)
    swap = pairs_of(var_size, lambda i: i ^ 1)

    def send(block, route):
        return lax.ppermute(block, both, route)

    def partner(block):
        return lax.ppermute(block, "var", swap)

    tok = jnp.transpose(tokens, (1, 0, 2))
    mask = jnp.transpose(patch_mask)
    qkv_t = jnp.transpose(time_qkv, (1, 2, 0))
    qkv_s = jnp.transpose(space_qkv, (1, 2, 0))
    var_count, rows, depth = tok.shape
    kind, width, _ = qkv_t.shape
    half = width // 2

    tok1, tok2 = send(tok, first), send(tok, second)
    mask1, mask2, mask3 = send(mask, first), send(mask, second), send(mask, third)
    tok3 = send(tok1, second)

    def spread_weight(weight, after):
        weight, _ = lax.optimization_barrier((weight, after))
        got1 = send(weight, first)
        got2 = partner(got1)
        axis = weight.ndim - 2
        mine = lax.dynamic_slice_in_dim(got1, core * half, half, axis)
        mine = send(mine, second)
        return weight, got1, got2, mine, partner(mine)

    tout = spread_weight(time_out, (tok1, tok2))
    sqkv = spread_weight(qkv_s, (tok1, tok2))
    sout = spread_weight(space_out, (tok1, tok2))

    near, far_step = jnp.where(core == 0, 1, 2), jnp.where(core == 0, 2, 1)
    bases = jnp.stack(
        [patch_index, patch_index ^ near, patch_index ^ far_step, patch_index ^ 3]
    ).astype(jnp.int32) * rows
    marks = jnp.concatenate([mask, mask1, mask2, mask3], axis=1)
    block = jax.ShapeDtypeStruct((var_count, rows, width), jnp.bfloat16)
    att = pl.pallas_call(
        time_kernel,
        out_shape=[block] * 4,
        in_specs=[SM] + [VM] * 7,
        out_specs=[VM] * 4,
        compiler_params=params(),
        cost_estimate=cost(2_000_000_000, 4_000_000),
        name="time",
    )(bases, tok, tok1, tok2, tok3, marks, time_gain[None], qkv_t.reshape(kind * width, depth))
    att0 = att[0]
    att1, att2, att3 = send(att[1], first), send(att[2], second), send(att[3], third)

    far_count = var_count - 1
    place = jnp.stack([
        core, jnp.where(level == 0, 1, 0), jnp.where(level == 0, 0, 1),
        jnp.where(level == 0, 1, 0), jnp.where(level == 0, 0, 1),
    ]).astype(jnp.int32)
    whole = jax.ShapeDtypeStruct((var_count, rows, depth), jnp.bfloat16)
    part = jax.ShapeDtypeStruct((far_count, rows, depth), jnp.bfloat16)
    mid, x_own, far1, far2 = pl.pallas_call(
        mid_kernel,
        out_shape=[whole, whole, part, part],
        in_specs=[SM] + [VM] * 11,
        out_specs=[VM] * 4,
        scratch_shapes=[pltpu.VMEM((width, depth), jnp.bfloat16)],
        compiler_params=params(),
        cost_estimate=cost(300_000_000, 3_000_000),
        name="mid",
    )(place, att0, att1, att2, att3, *tout, tok, space_gain[None])

    x_swap = partner(x_own)
    x_other = lax.ppermute(x_own, "var", pairs_of(var_size, lambda i: i + 1 if i % 2 else i - 1))
    far1 = lax.ppermute(far1, "var", pairs_of(var_size, lambda i: i ^ 2))
    far2 = lax.ppermute(
        far2, "var", pairs_of(var_size, lambda i: i + 2 if (i // 2) % 2 else i - 2)
    )

    outside = jnp.full((2 * var_count,), -1, jnp.int32)
    padded = jnp.concatenate([outside, group_ids, outside])

    def ids_at(index, skip, size):
        return lax.dynamic_slice_in_dim(padded, (index + 2) * var_count + skip, size)

    ids = jnp.concatenate([
        ids_at(var_index, 0, var_count),
        ids_at(var_index + 1 - 2 * core, 0, var_count),
        ids_at(var_index - 1 + 2 * core, 0, var_count),
        ids_at(var_index - 2, 1, far_count),
        ids_at(var_index + 2, 0, far_count),
    ])
    inner = 4 * width
    count = 3 * var_count + 2 * far_count
    bf = jnp.bfloat16
    out = pl.pallas_call(
        space_kernel,
        out_shape=whole,
        in_specs=[SM] * 2 + [VM] * 16,
        out_specs=VM,
        scratch_shapes=[
            pltpu.VMEM((2 * far_count, rows, depth), bf),
            pltpu.VMEM((kind, inner, depth), bf),
            pltpu.VMEM((inner, depth), bf),
            pltpu.VMEM((var_count * rows, inner), bf),
            pltpu.VMEM((count * rows, inner), bf),
            pltpu.VMEM((count * rows, inner), bf),
            pltpu.VMEM((count * rows, 128), bf),
            pltpu.VMEM((var_count * rows, inner), bf),
        ],
        compiler_params=params(),
        cost_estimate=cost(4_000_000_000, 8_000_000),
        name="space",
    )(place, ids, x_own, x_swap, x_other, far1, far2, mid, *sqkv, *sout)
    return jnp.transpose(out, (1, 0, 2))


def solution(mesh):
    in_specs = (
        P("patch", ("parts", "var"), None),
        P("patch", ("parts", "var")),
        P("parts"),
        P(),
        P(None, None, "patch"),
        P("patch", None),
        P(),
        P(None, None, "patch"),
        P("patch", None),
    )
    out_specs = P("patch", ("parts", "var"), None)
    return jax.shard_map(
        on_device, mesh=mesh, in_specs=in_specs, out_specs=out_specs, check_vma=False
    )
```

time: 197 us -> 92.6 us (0.47)
  the two profiles are of different devices: /device:TPU:9 before, /device:TPU:16 now
where the time goes in v1:
time: 92.6 us; the launch traced here: 92.2 us
  waiting for transfers between devices  42 us (45%)
  starting transfers between devices  25 us (27%)
  Pallas kernels  14.3 us (15%)
  local copies, waits for them, and re-layouts  9.84 us (11%)
    ppermute x15, waiting for transfers between devices, send(): return lax.ppermute(block, both, route)  33.3 us
    ppermute x15, starting transfers between devices, send(): return lax.ppermute(block, both, route)  17 us
    unnamed x24, local copies, waits for them, and re-layouts  8 us
    pallas_call x1, Pallas kernels, on_device(): pl.pallas_call(space_kernel, out_shape=whole, in_specs=[SM] * 2 + [VM] *...  7.45 us
    ppermute x1, waiting for transfers between devices, on_device(): lax.ppermute(far2, 'var', pairs_of(var_size, lambda i: i + 2 if i // 2 %...  5.58 us
    pallas_call x1, Pallas kernels, on_device(): pl.pallas_call(time_kernel, out_shape=[block] * 4, in_specs=[SM] + [VM] *...  4.68 us
    ppermute x1, waiting for transfers between devices, on_device(): far1 = lax.ppermute(far1, 'var', pairs_of(var_size, lambda i: i ^ 2))  3.16 us
    ppermute x1, starting transfers between devices, on_device(): lax.ppermute(far2, 'var', pairs_of(var_size, lambda i: i + 2 if i // 2 %...  2.76 us
  transfers between devices with their start and end apart: 25, of which 7 were waited for; matrix products, arithmetic and copies ran while one was open for 3% of the time, Pallas kernels for 7%

profile of v1, /device:TPU:16, one launch (start us, length us, event | category | flops | bytes accessed | tf_op | source)
XLA Modules:
  0.0 92.2 jit_solution(3569425983371225571)
XLA Ops:
  0.0 1.5 %collective-permute-start.1 = (bf16[3,64,768]{2,1,0:T(8,128)(2,1)}, bf16[3,64,768]{2,1,0:T(8,128)(2,1)S(1)}, u32[]{:S(2)}, u32[]{:S(2)}) collective-permute-start(bf16[3,64,768]{2,1,0:T(8,128)(2,1)} %bitcast.14), channel_id=1, source_target_pairs={{0,2},{1,3},{2,0},{3,1},{4,5},{5,4},{6,7},{7,6},{8,10},{9,11},{10,... | collective-permute-start | bytes 884744 | tf_op jit(solution)/shard_map/ppermute | solution.py:219
  1.5 1.5 %collective-permute-start = (bf16[3,64,768]{2,1,0:T(8,128)(2,1)}, bf16[3,64,768]{2,1,0:T(8,128)(2,1)S(1)}, u32[]{:S(2)}, u32[]{:S(2)}) collective-permute-start(bf16[3,64,768]{2,1,0:T(8,128)(2,1)} %bitcast.15), channel_id=1, source_target_pairs={{0,1},{1,0},{2,3},{3,2},{4,6},{5,7},{6,4},{7,5},{8,9},{9,8},{10,11... | collective-permute-start | bytes 884744 | tf_op jit(solution)/shard_map/ppermute | solution.py:219
  3.0 7.0 %collective-permute-done.1.t2 = bf16[3,64,768]{2,1,0:T(8,128)(2,1)S(1)} collective-permute-done((bf16[3,64,768]{2,1,0:T(8,128)(2,1)}, bf16[3,64,768]{2,1,0:T(8,128)(2,1)S(1)}, u32[]{:S(2)}, u32[]{:S(2)}) %collective-permute-start.1) | collective-permute-done | bytes 294944 | tf_op jit(solution)/shard_map/ppermute | solution.py:219
  10.0 0.0 collective-permute-done.t1
  10.0 0.7 collective-permute-start.17
  10.7 1.3 %collective-permute-start.9 = (bf16[192,768]{1,0:T(8,128)(2,1)}, bf16[192,768]{1,0:T(8,128)(2,1)S(1)}, u32[]{:S(2)}, u32[]{:S(2)}) collective-permute-start(bf16[192,768]{1,0:T(8,128)(2,1)} %w0), channel_id=1, source_target_pairs={{0,1},{1,0},{2,3},{3,2},{4,6},{5,7},{6,4},{7,5},{8,9},{9,8},{10,11... | collective-permute-start | bytes 884744 | tf_op jit(solution)/shard_map/ppermute | solution.py:219
  12.1 1.6 %collective-permute-start.5 = (s32[3,64]{1,0:T(4,128)}, s32[3,64]{1,0:T(4,128)S(1)}, u32[]{:S(2)}, u32[]{:S(2)}) collective-permute-start(s32[3,64]{1,0:T(4,128)} %bitcast.21), channel_id=1, source_target_pairs={{0,3},{1,2},{2,1},{3,0},{4,7},{5,6},{6,5},{7,4},{8,11},{9,10},{10,... | collective-permute-start | bytes 2312 | tf_op jit(solution)/shard_map/ppermute | solution.py:219
  13.7 0.5 collective-permute-start.4
  14.2 1.3 %collective-permute-start.3 = (s32[3,64]{1,0:T(4,128)}, s32[3,64]{1,0:T(4,128)S(1)}, u32[]{:S(2)}, u32[]{:S(2)}) collective-permute-start(s32[3,64]{1,0:T(4,128)} %bitcast.23), channel_id=1, source_target_pairs={{0,1},{1,0},{2,3},{3,2},{4,6},{5,7},{6,4},{7,5},{8,9},{9,8},{10,11... | collective-permute-start | bytes 2312 | tf_op jit(solution)/shard_map/ppermute | solution.py:219
  15.5 15.3 %collective-permute-done.5 = s32[3,64]{1,0:T(4,128)S(1)} collective-permute-done((s32[3,64]{1,0:T(4,128)}, s32[3,64]{1,0:T(4,128)S(1)}, u32[]{:S(2)}, u32[]{:S(2)}) %collective-permute-start.5) | collective-permute-done | bytes 800 | tf_op jit(solution)/shard_map/ppermute | solution.py:219
  30.8 0.4 collective-permute-start.2
  31.2 0.1 add_multiply_fusion.base_ref
  31.3 0.7 broadcast_in_dim.6.gain_ref
  32.0 0.0 collective-permute-done.3
  32.0 0.8 pad_add_fusion.mask_ref
  32.8 0.7 collective-permute-start.21
  33.5 2.1 %collective-permute-start.11 = (bf16[96,768]{1,0:T(8,128)(2,1)S(1)}, bf16[96,768]{1,0:T(8,128)(2,1)S(1)}, u32[]{:S(2)}, u32[]{:S(2)}) collective-permute-start(bf16[96,768]{1,0:T(8,128)(2,1)S(1)} %constant_dynamic-slice_fusion.2), channel_id=1, source_target_pairs={{0,2},{1,3},{2,0},{3,1},{4,5},{5,4},{6,7},{7,6},{8,10},{9,11},{10,... | collective-permute-start | bytes 442376 | tf_op jit(solution)/shard_map/ppermute | solution.py:219
  35.5 3.0 %collective-permute-done.2.t3 = bf16[3,64,768]{2,1,0:T(8,128)(2,1)S(1)} collective-permute-done((bf16[3,64,768]{2,1,0:T(8,128)(2,1)S(1)}, bf16[3,64,768]{2,1,0:T(8,128)(2,1)S(1)}, u32[]{:S(2)}, u32[]{:S(2)}) %collective-permute-start.2) | collective-permute-done | bytes 294944 | tf_op jit(solution)/shard_map/ppermute | solution.py:219
  38.6 1.2 %copy-done.2 = bf16[768,3,192]{0,2,1:T(8,128)(2,1)S(1)} copy-done((bf16[768,3,192]{0,2,1:T(8,128)(2,1)S(1)}, bf16[768,3,192]{0,2,1:T(8,128)(2,1)}, u32[]{:S(2)}) %copy-start.2) | copy-done | bytes 884760
  39.7 4.7 %time.1 = (bf16[3,64,192]{2,1,0:T(8,128)(2,1)S(1)}, bf16[3,64,192]{2,1,0:T(8,128)(2,1)S(1)}, bf16[3,64,192]{2,1,0:T(8,128)(2,1)S(1)}, bf16[3,64,192]{2,1,0:T(8,128)(2,1)S(1)}) custom-call(s32[4]{0:T(128)S(1)} %add_multiply_fusion.base_ref, bf16[3,64,768]{2,1,0:T(8,128)(2,1)S(1)} %bitcast.16, bf16[3,64,768]{2,1,0:T(8,128)(2,1)S(1)} %collective-permute-done.t1, ...), custom_call_target="tpu_custom_call" | custom-call | flops 2000000000 | bytes 4000000 | tf_op jit(solution)/shard_map/time/pallas_call | solution.py:255
  44.4 0.5 collective-permute-start.6
  45.0 3.0 %collective-permute-start.8 = (bf16[3,64,192]{2,1,0:T(8,128)(2,1)S(1)}, bf16[3,64,192]{2,1,0:T(8,128)(2,1)S(1)}, u32[]{:S(2)}, u32[]{:S(2)}) collective-permute-start(bf16[3,64,192]{2,1,0:T(8,128)(2,1)S(1)} %get-tuple-element.19), channel_id=1, source_target_pairs={{0,3},{1,2},{2,1},{3,0},{4,7},{5,6},{6,5},{7,4},{8,11},{9,10},{10,... | collective-permute-start | bytes 221192 | tf_op jit(solution)/shard_map/ppermute | solution.py:219
  48.0 0.8 constant_dynamic-slice_fusion.1
  48.8 0.0 collective-permute-done.21.u1
  48.8 0.4 collective-permute-start.19
  49.2 0.0 collective-permute-done.6.a1
  49.2 0.0 collective-permute-start.18
  49.2 0.4 collective-permute-done.7.a2
  49.6 1.3 %collective-permute-start.23 = (bf16[96,768]{1,0:T(8,128)(2,1)S(1)}, bf16[96,768]{1,0:T(8,128)(2,1)}, u32[]{:S(2)}, u32[]{:S(2)}) collective-permute-start(bf16[96,768]{1,0:T(8,128)(2,1)S(1)} %constant_dynamic-slice_fusion), channel_id=1, source_target_pairs={{0,2},{1,3},{2,0},{3,1},{4,5},{5,4},{6,7},{7,6},{8,10},{9,11},{10,... | collective-permute-start | bytes 442376 | tf_op jit(solution)/shard_map/ppermute | solution.py:219
  50.9 0.0 collective-permute-done.8.a3
  50.9 0.0 collective-permute-start.10
  50.9 0.5 collective-permute-start.12
  51.4 7.6 %collective-permute-done.23.ua = bf16[96,768]{1,0:T(8,128)(2,1)} collective-permute-done((bf16[96,768]{1,0:T(8,128)(2,1)S(1)}, bf16[96,768]{1,0:T(8,128)(2,1)}, u32[]{:S(2)}, u32[]{:S(2)}) %collective-permute-start.23) | collective-permute-done | bytes 147488 | tf_op jit(solution)/shard_map/ppermute | solution.py:219
  59.0 0.0 collective-permute-start.22
  59.0 0.0 collective-permute-done.12.wb
  59.0 0.5 collective-permute-start.24
  59.5 0.7 copy-done.10
  60.2 0.1 stack.32.place_ref
  60.3 0.0 collective-permute-done.19.wa
  60.3 0.0 collective-permute-start.20
  60.3 2.1 %mid.1 = (bf16[3,64,768]{2,1,0:T(8,128)(2,1)S(1)}, bf16[3,64,768]{2,1,0:T(8,128)(2,1)S(1)}, bf16[2,64,768]{2,1,0:T(8,128)(2,1)}, bf16[2,64,768]{2,1,0:T(8,128)(2,1)S(1)}) custom-call(s32[5]{0:T(128)S(1)} %stack.32.place_ref, bf16[3,64,192]{2,1,0:T(8,128)(2,1)S(1)} %get-tuple-element.16.a0, bf16[3,64,192]{2,1,0:T(8,128)(2,1)S(1)} %collective-permute-done.6.a1, ...), custom_call_target="tpu_custom_call" | custom-call | flops 300000000 | bytes 3000000 | tf_op jit(solution)/shard_map/mid/pallas_call | solution.py:274
  62.5 0.7 copy-done.5
  63.2 0.7 copy-done.7
  63.9 0.7 copy-done.9
  64.5 1.6 %collective-permute-start.15 = (bf16[2,64,768]{2,1,0:T(8,128)(2,1)}, bf16[2,64,768]{2,1,0:T(8,128)(2,1)S(1)}, u32[]{:S(2)}, u32[]{:S(2)}) collective-permute-start(bf16[2,64,768]{2,1,0:T(8,128)(2,1)} %get-tuple-element.22), channel_id=1, source_target_pairs={{0,8},{4,12},{8,0},{12,4},{16,24},{20,28},{24,16},{28,20},{1,9},{5... | collective-permute-start | bytes 589832 | tf_op jit(solution)/shard_map/ppermute | solution.py:287
  66.1 0.0 collective-permute-done.24.ub
  66.1 2.0 %collective-permute-start.14 = (bf16[3,64,768]{2,1,0:T(8,128)(2,1)}, bf16[3,64,768]{2,1,0:T(8,128)(2,1)S(1)}, u32[]{:S(2)}, u32[]{:S(2)}) collective-permute-start(bf16[3,64,768]{2,1,0:T(8,128)(2,1)} %copy-done.7), channel_id=1, source_target_pairs={{4,8},{8,4},{12,16},{16,12},{20,24},{24,20},{5,9},{9,5},{13,17},{1... | collective-permute-start | bytes 884744 | tf_op jit(solution)/shard_map/ppermute | solution.py:286
  68.2 0.0 collective-permute-done.22.u2
  68.2 0.6 collective-permute-start.13
  68.8 0.1 pad_add_fusion.1
  68.9 3.2 %collective-permute-done.15.f1 = bf16[2,64,768]{2,1,0:T(8,128)(2,1)S(1)} collective-permute-done((bf16[2,64,768]{2,1,0:T(8,128)(2,1)}, bf16[2,64,768]{2,1,0:T(8,128)(2,1)S(1)}, u32[]{:S(2)}, u32[]{:S(2)}) %collective-permute-start.15) | collective-permute-done | bytes 196640 | tf_op jit(solution)/shard_map/ppermute | solution.py:287
  72.0 2.8 %collective-permute-start.16 = (bf16[2,64,768]{2,1,0:T(8,128)(2,1)}, bf16[2,64,768]{2,1,0:T(8,128)(2,1)S(1)}, u32[]{:S(2)}, u32[]{:S(2)}) collective-permute-start(bf16[2,64,768]{2,1,0:T(8,128)(2,1)} %copy-done.9), channel_id=1, source_target_pairs={{8,16},{12,20},{16,8},{20,12},{9,17},{13,21},{17,9},{21,13},{10,18... | collective-permute-start | bytes 589832 | tf_op jit(solution)/shard_map/ppermute | solution.py:288
  74.8 0.1 fusion
  74.9 0.1 fusion.1
  75.0 0.1 concatenate.10.ids_ref
  75.1 5.6 %collective-permute-done.16.f2 = bf16[2,64,768]{2,1,0:T(8,128)(2,1)S(1)} collective-permute-done((bf16[2,64,768]{2,1,0:T(8,128)(2,1)}, bf16[2,64,768]{2,1,0:T(8,128)(2,1)S(1)}, u32[]{:S(2)}, u32[]{:S(2)}) %collective-permute-start.16) | collective-permute-done | bytes 196640 | tf_op jit(solution)/shard_map/ppermute | solution.py:288
  80.6 0.0 collective-permute-done.14.xo
  80.6 0.0 collective-permute-done.13.xs
  80.7 0.0 copy-start.3
  80.7 1.2 %copy-done.3 = bf16[768,3,192]{0,2,1:T(8,128)(2,1)S(1)} copy-done((bf16[768,3,192]{0,2,1:T(8,128)(2,1)S(1)}, bf16[768,3,192]{0,2,1:T(8,128)(2,1)}, u32[]{:S(2)}) %copy-start.3) | copy-done | bytes 884760
  81.8 1.0 %copy-done.4 = bf16[192,768]{1,0:T(8,128)(2,1)S(1)} copy-done((bf16[192,768]{1,0:T(8,128)(2,1)S(1)}, bf16[192,768]{1,0:T(8,128)(2,1)}, u32[]{:S(2)}) %copy-start.4) | copy-done | bytes 294936
  82.8 1.0 %copy-done.6 = bf16[3,64,768]{2,1,0:T(8,128)(2,1)S(1)} copy-done((bf16[3,64,768]{2,1,0:T(8,128)(2,1)S(1)}, bf16[3,64,768]{2,1,0:T(8,128)(2,1)}, u32[]{:S(2)}) %copy-start.6) | copy-done | bytes 294936
  83.8 1.0 %copy-done.8 = bf16[3,64,768]{2,1,0:T(8,128)(2,1)S(1)} copy-done((bf16[3,64,768]{2,1,0:T(8,128)(2,1)S(1)}, bf16[3,64,768]{2,1,0:T(8,128)(2,1)}, u32[]{:S(2)}) %copy-start.8) | copy-done | bytes 294936
  84.7 7.4 %space.1 = bf16[3,64,768]{2,1,0:T(8,128)(2,1)} custom-call(s32[5]{0:T(128)S(1)} %stack.32.place_ref, s32[13]{0:T(128)S(1)} %concatenate.10.ids_ref, bf16[3,64,768]{2,1,0:T(8,128)(2,1)S(1)} %copy-done.8, bf16[3,64,768]{2,1,0:T(8,128)(2,1)S(1)} %collective-permute-done.13.xs, bf16[3,64,768]{2,1,0:T(8,128)(2,1)S(1)} %collective-permute-done.14.xo, ...), custom_call_target="tpu_custom_call" | custom-call | flops 4000000000 | bytes 8000000 | tf_op jit(solution)/shard_map/space/pallas_call | solution.py:308
  (26 shorter events, 0.1 us)
Async XLA Ops:
  0.0 38.6 %copy-start = (bf16[64,3,768]{2,0,1:T(8,128)(2,1)S(1)}, bf16[64,3,768]{2,0,1:T(8,128)(2,1)}, u32[]{:S(2)}) copy-start(bf16[64,3,768]{2,0,1:T(8,128)(2,1)} %param.9) | copy-start | bytes 884740
  0.0 10.0 %collective-permute-start.1 = (bf16[3,64,768]{2,1,0:T(8,128)(2,1)}, bf16[3,64,768]{2,1,0:T(8,128)(2,1)S(1)}, u32[]{:S(2)}, u32[]{:S(2)}) collective-permute-start(bf16[3,64,768]{2,1,0:T(8,128)(2,1)} %bitcast.14), channel_id=1, source_target_pairs={{0,2},{1,3},{2,0},{3,1},{4,5},{5,4},{6,7},{7,6},{8,10},{9,11},{10,... | collective-permute-start | bytes 884744 | tf_op jit(solution)/shard_map/ppermute | solution.py:219
  1.5 8.5 %collective-permute-start = (bf16[3,64,768]{2,1,0:T(8,128)(2,1)}, bf16[3,64,768]{2,1,0:T(8,128)(2,1)S(1)}, u32[]{:S(2)}, u32[]{:S(2)}) collective-permute-start(bf16[3,64,768]{2,1,0:T(8,128)(2,1)} %bitcast.15), channel_id=1, source_target_pairs={{0,1},{1,0},{2,3},{3,2},{4,6},{5,7},{6,4},{7,5},{8,9},{9,8},{10,11... | collective-permute-start | bytes 884744 | tf_op jit(solution)/shard_map/ppermute | solution.py:219
  10.0 34.9 %collective-permute-start.17 = (bf16[3,192,768]{2,1,0:T(8,128)(2,1)}, bf16[3,192,768]{2,1,0:T(8,128)(2,1)S(1)}, u32[]{:S(2)}, u32[]{:S(2)}) collective-permute-start(bf16[3,192,768]{2,1,0:T(8,128)(2,1)} %bitcast.19), channel_id=1, source_target_pairs={{0,1},{1,0},{2,3},{3,2},{4,6},{5,7},{6,4},{7,5},{8,9},{9,8},{10,11... | collective-permute-start | bytes 2654216 | tf_op jit(solution)/shard_map/ppermute | solution.py:219
  10.7 22.7 %collective-permute-start.9 = (bf16[192,768]{1,0:T(8,128)(2,1)}, bf16[192,768]{1,0:T(8,128)(2,1)S(1)}, u32[]{:S(2)}, u32[]{:S(2)}) collective-permute-start(bf16[192,768]{1,0:T(8,128)(2,1)} %w0), channel_id=1, source_target_pairs={{0,1},{1,0},{2,3},{3,2},{4,6},{5,7},{6,4},{7,5},{8,9},{9,8},{10,11... | collective-permute-start | bytes 884744 | tf_op jit(solution)/shard_map/ppermute | solution.py:219
  12.1 18.7 %collective-permute-start.5 = (s32[3,64]{1,0:T(4,128)}, s32[3,64]{1,0:T(4,128)S(1)}, u32[]{:S(2)}, u32[]{:S(2)}) collective-permute-start(s32[3,64]{1,0:T(4,128)} %bitcast.21), channel_id=1, source_target_pairs={{0,3},{1,2},{2,1},{3,0},{4,7},{5,6},{6,5},{7,4},{8,11},{9,10},{10,... | collective-permute-start | bytes 2312 | tf_op jit(solution)/shard_map/ppermute | solution.py:219
  13.7 18.3 %collective-permute-start.4 = (s32[3,64]{1,0:T(4,128)}, s32[3,64]{1,0:T(4,128)S(1)}, u32[]{:S(2)}, u32[]{:S(2)}) collective-permute-start(s32[3,64]{1,0:T(4,128)} %bitcast.22), channel_id=1, source_target_pairs={{0,2},{1,3},{2,0},{3,1},{4,5},{5,4},{6,7},{7,6},{8,10},{9,11},{10,... | collective-permute-start | bytes 2312 | tf_op jit(solution)/shard_map/ppermute | solution.py:219
  14.2 17.8 %collective-permute-start.3 = (s32[3,64]{1,0:T(4,128)}, s32[3,64]{1,0:T(4,128)S(1)}, u32[]{:S(2)}, u32[]{:S(2)}) collective-permute-start(s32[3,64]{1,0:T(4,128)} %bitcast.23), channel_id=1, source_target_pairs={{0,1},{1,0},{2,3},{3,2},{4,6},{5,7},{6,4},{7,5},{8,9},{9,8},{10,11... | collective-permute-start | bytes 2312 | tf_op jit(solution)/shard_map/ppermute | solution.py:219
  30.8 7.8 %collective-permute-start.2 = (bf16[3,64,768]{2,1,0:T(8,128)(2,1)S(1)}, bf16[3,64,768]{2,1,0:T(8,128)(2,1)S(1)}, u32[]{:S(2)}, u32[]{:S(2)}) collective-permute-start(bf16[3,64,768]{2,1,0:T(8,128)(2,1)S(1)} %collective-permute-done.t1), channel_id=1, source_target_pairs={{0,2},{1,3},{2,0},{3,1},{4,5},{5,4},{6,7},{7,6},{8,10},{9,11},{10,... | collective-permute-start | bytes 884744 | tf_op jit(solution)/shard_map/ppermute | solution.py:219
  32.8 16.0 %collective-permute-start.21 = (bf16[192,768]{1,0:T(8,128)(2,1)}, bf16[192,768]{1,0:T(8,128)(2,1)S(1)}, u32[]{:S(2)}, u32[]{:S(2)}) collective-permute-start(bf16[192,768]{1,0:T(8,128)(2,1)} %u0), channel_id=1, source_target_pairs={{0,1},{1,0},{2,3},{3,2},{4,6},{5,7},{6,4},{7,5},{8,9},{9,8},{10,11... | collective-permute-start | bytes 884744 | tf_op jit(solution)/shard_map/ppermute | solution.py:219
  33.5 17.4 %collective-permute-start.11 = (bf16[96,768]{1,0:T(8,128)(2,1)S(1)}, bf16[96,768]{1,0:T(8,128)(2,1)S(1)}, u32[]{:S(2)}, u32[]{:S(2)}) collective-permute-start(bf16[96,768]{1,0:T(8,128)(2,1)S(1)} %constant_dynamic-slice_fusion.2), channel_id=1, source_target_pairs={{0,2},{1,3},{2,0},{3,1},{4,5},{5,4},{6,7},{7,6},{8,10},{9,11},{10,... | collective-permute-start | bytes 442376 | tf_op jit(solution)/shard_map/ppermute | solution.py:219
  38.6 1.2 %copy-start.2 = (bf16[768,3,192]{0,2,1:T(8,128)(2,1)S(1)}, bf16[768,3,192]{0,2,1:T(8,128)(2,1)}, u32[]{:S(2)}) copy-start(bf16[768,3,192]{0,2,1:T(8,128)(2,1)} %param.13) | copy-start | bytes 2654212
  44.4 4.7 %collective-permute-start.6 = (bf16[3,64,192]{2,1,0:T(8,128)(2,1)S(1)}, bf16[3,64,192]{2,1,0:T(8,128)(2,1)S(1)}, u32[]{:S(2)}, u32[]{:S(2)}) collective-permute-start(bf16[3,64,192]{2,1,0:T(8,128)(2,1)S(1)} %get-tuple-element.17), channel_id=1, source_target_pairs={{0,1},{1,0},{2,3},{3,2},{4,6},{5,7},{6,4},{7,5},{8,9},{9,8},{10,11... | collective-permute-start | bytes 221192 | tf_op jit(solution)/shard_map/ppermute | solution.py:219
  45.0 4.6 %collective-permute-start.7 = (bf16[3,64,192]{2,1,0:T(8,128)(2,1)S(1)}, bf16[3,64,192]{2,1,0:T(8,128)(2,1)S(1)}, u32[]{:S(2)}, u32[]{:S(2)}) collective-permute-start(bf16[3,64,192]{2,1,0:T(8,128)(2,1)S(1)} %get-tuple-element.18), channel_id=1, source_target_pairs={{0,2},{1,3},{2,0},{3,1},{4,5},{5,4},{6,7},{7,6},{8,10},{9,11},{10,... | collective-permute-start | bytes 221192 | tf_op jit(solution)/shard_map/ppermute | solution.py:219
  45.0 5.9 %collective-permute-start.8 = (bf16[3,64,192]{2,1,0:T(8,128)(2,1)S(1)}, bf16[3,64,192]{2,1,0:T(8,128)(2,1)S(1)}, u32[]{:S(2)}, u32[]{:S(2)}) collective-permute-start(bf16[3,64,192]{2,1,0:T(8,128)(2,1)S(1)} %get-tuple-element.19), channel_id=1, source_target_pairs={{0,3},{1,2},{2,1},{3,0},{4,7},{5,6},{6,5},{7,4},{8,11},{9,10},{10,... | collective-permute-start | bytes 221192 | tf_op jit(solution)/shard_map/ppermute | solution.py:219
  48.8 11.5 %copy-start.1 = (bf16[192,768]{1,0:T(8,128)(2,1)S(1)}, bf16[192,768]{1,0:T(8,128)(2,1)}, u32[]{:S(2)}) copy-start(bf16[192,768]{1,0:T(8,128)(2,1)} %w0) | copy-start | bytes 884740
  48.8 11.5 %collective-permute-start.19 = (bf16[3,96,768]{2,1,0:T(8,128)(2,1)}, bf16[3,96,768]{2,1,0:T(8,128)(2,1)S(1)}, u32[]{:S(2)}, u32[]{:S(2)}) collective-permute-start(bf16[3,96,768]{2,1,0:T(8,128)(2,1)} %constant_dynamic-slice_fusion.1), channel_id=1, source_target_pairs={{0,2},{1,3},{2,0},{3,1},{4,5},{5,4},{6,7},{7,6},{8,10},{9,11},{10,... | collective-permute-start | bytes 1327112 | tf_op jit(solution)/shard_map/ppermute | solution.py:219
  49.2 31.5 %collective-permute-start.18 = (bf16[3,192,768]{2,1,0:T(8,128)(2,1)S(1)}, bf16[3,192,768]{2,1,0:T(8,128)(2,1)}, u32[]{:S(2)}, u32[]{:S(2)}) collective-permute-start(bf16[3,192,768]{2,1,0:T(8,128)(2,1)S(1)} %collective-permute-done.17.w1), channel_id=1, source_target_pairs={{0,4},{4,0},{8,12},{12,8},{16,20},{20,16},{24,28},{28,24},{1,5},{5... | collective-permute-start | bytes 2654216 | tf_op jit(solution)/shard_map/ppermute | solution.py:222
  49.6 9.4 %collective-permute-start.23 = (bf16[96,768]{1,0:T(8,128)(2,1)S(1)}, bf16[96,768]{1,0:T(8,128)(2,1)}, u32[]{:S(2)}, u32[]{:S(2)}) collective-permute-start(bf16[96,768]{1,0:T(8,128)(2,1)S(1)} %constant_dynamic-slice_fusion), channel_id=1, source_target_pairs={{0,2},{1,3},{2,0},{3,1},{4,5},{5,4},{6,7},{7,6},{8,10},{9,11},{10,... | collective-permute-start | bytes 442376 | tf_op jit(solution)/shard_map/ppermute | solution.py:219
  50.9 9.4 %collective-permute-start.10 = (bf16[192,768]{1,0:T(8,128)(2,1)S(1)}, bf16[192,768]{1,0:T(8,128)(2,1)S(1)}, u32[]{:S(2)}, u32[]{:S(2)}) collective-permute-start(bf16[192,768]{1,0:T(8,128)(2,1)S(1)} %collective-permute-done.9.w1), channel_id=1, source_target_pairs={{0,4},{4,0},{8,12},{12,8},{16,20},{20,16},{24,28},{28,24},{1,5},{5... | collective-permute-start | bytes 884744 | tf_op jit(solution)/shard_map/ppermute | solution.py:222
  50.9 8.1 %collective-permute-start.12 = (bf16[96,768]{1,0:T(8,128)(2,1)S(1)}, bf16[96,768]{1,0:T(8,128)(2,1)S(1)}, u32[]{:S(2)}, u32[]{:S(2)}) collective-permute-start(bf16[96,768]{1,0:T(8,128)(2,1)S(1)} %collective-permute-done.11.wa), channel_id=1, source_target_pairs={{0,4},{4,0},{8,12},{12,8},{16,20},{20,16},{24,28},{28,24},{1,5},{5... | collective-permute-start | bytes 442376 | tf_op jit(solution)/shard_map/ppermute | solution.py:222
  59.0 9.2 %collective-permute-start.22 = (bf16[192,768]{1,0:T(8,128)(2,1)S(1)}, bf16[192,768]{1,0:T(8,128)(2,1)}, u32[]{:S(2)}, u32[]{:S(2)}) collective-permute-start(bf16[192,768]{1,0:T(8,128)(2,1)S(1)} %collective-permute-done.21.u1), channel_id=1, source_target_pairs={{0,4},{4,0},{8,12},{12,8},{16,20},{20,16},{24,28},{28,24},{1,5},{5... | collective-permute-start | bytes 884744 | tf_op jit(solution)/shard_map/ppermute | solution.py:222
  59.0 7.1 %collective-permute-start.24 = (bf16[96,768]{1,0:T(8,128)(2,1)}, bf16[96,768]{1,0:T(8,128)(2,1)}, u32[]{:S(2)}, u32[]{:S(2)}) collective-permute-start(bf16[96,768]{1,0:T(8,128)(2,1)} %collective-permute-done.23.ua), channel_id=1, source_target_pairs={{0,4},{4,0},{8,12},{12,8},{16,20},{20,16},{24,28},{28,24},{1,5},{5... | collective-permute-start | bytes 442376 | tf_op jit(solution)/shard_map/ppermute | solution.py:222
  59.5 0.7 copy-start.10
  60.3 20.4 %collective-permute-start.20 = (bf16[3,96,768]{2,1,0:T(8,128)(2,1)S(1)}, bf16[3,96,768]{2,1,0:T(8,128)(2,1)}, u32[]{:S(2)}, u32[]{:S(2)}) collective-permute-start(bf16[3,96,768]{2,1,0:T(8,128)(2,1)S(1)} %collective-permute-done.19.wa), channel_id=1, source_target_pairs={{0,4},{4,0},{8,12},{12,8},{16,20},{20,16},{24,28},{28,24},{1,5},{5... | collective-permute-start | bytes 1327112 | tf_op jit(solution)/shard_map/ppermute | solution.py:222
  62.5 0.7 copy-start.5
  63.2 0.7 copy-start.7
  63.9 0.7 copy-start.9
  64.5 7.5 %collective-permute-start.15 = (bf16[2,64,768]{2,1,0:T(8,128)(2,1)}, bf16[2,64,768]{2,1,0:T(8,128)(2,1)S(1)}, u32[]{:S(2)}, u32[]{:S(2)}) collective-permute-start(bf16[2,64,768]{2,1,0:T(8,128)(2,1)} %get-tuple-element.22), channel_id=1, source_target_pairs={{0,8},{4,12},{8,0},{12,4},{16,24},{20,28},{24,16},{28,20},{1,9},{5... | collective-permute-start | bytes 589832 | tf_op jit(solution)/shard_map/ppermute | solution.py:287
  66.1 2.7 %copy-start.11 = (s32[24]{0:T(128)S(1)}, s32[24]{0:T(128)}, u32[]{:S(2)}) copy-start(s32[24]{0:T(128)} %param.11) | copy-start | bytes 292
  66.1 14.5 %collective-permute-start.14 = (bf16[3,64,768]{2,1,0:T(8,128)(2,1)}, bf16[3,64,768]{2,1,0:T(8,128)(2,1)S(1)}, u32[]{:S(2)}, u32[]{:S(2)}) collective-permute-start(bf16[3,64,768]{2,1,0:T(8,128)(2,1)} %copy-done.7), channel_id=1, source_target_pairs={{4,8},{8,4},{12,16},{16,12},{20,24},{24,20},{5,9},{9,5},{13,17},{1... | collective-permute-start | bytes 884744 | tf_op jit(solution)/shard_map/ppermute | solution.py:286
  68.2 12.5 %collective-permute-start.13 = (bf16[3,64,768]{2,1,0:T(8,128)(2,1)}, bf16[3,64,768]{2,1,0:T(8,128)(2,1)S(1)}, u32[]{:S(2)}, u32[]{:S(2)}) collective-permute-start(bf16[3,64,768]{2,1,0:T(8,128)(2,1)} %copy-done.7), channel_id=1, source_target_pairs={{0,4},{4,0},{8,12},{12,8},{16,20},{20,16},{24,28},{28,24},{1,5},{5... | collective-permute-start | bytes 884744 | tf_op jit(solution)/shard_map/ppermute | solution.py:222
  72.0 8.6 %collective-permute-start.16 = (bf16[2,64,768]{2,1,0:T(8,128)(2,1)}, bf16[2,64,768]{2,1,0:T(8,128)(2,1)S(1)}, u32[]{:S(2)}, u32[]{:S(2)}) collective-permute-start(bf16[2,64,768]{2,1,0:T(8,128)(2,1)} %copy-done.9), channel_id=1, source_target_pairs={{8,16},{12,20},{16,8},{20,12},{9,17},{13,21},{17,9},{21,13},{10,18... | collective-permute-start | bytes 589832 | tf_op jit(solution)/shard_map/ppermute | solution.py:288
  80.7 1.2 %copy-start.3 = (bf16[768,3,192]{0,2,1:T(8,128)(2,1)S(1)}, bf16[768,3,192]{0,2,1:T(8,128)(2,1)}, u32[]{:S(2)}) copy-start(bf16[768,3,192]{0,2,1:T(8,128)(2,1)} %param.16) | copy-start | bytes 2654212
  81.8 1.0 %copy-start.4 = (bf16[192,768]{1,0:T(8,128)(2,1)S(1)}, bf16[192,768]{1,0:T(8,128)(2,1)}, u32[]{:S(2)}) copy-start(bf16[192,768]{1,0:T(8,128)(2,1)} %u0) | copy-start | bytes 884740
  82.8 1.0 %copy-start.6 = (bf16[3,64,768]{2,1,0:T(8,128)(2,1)S(1)}, bf16[3,64,768]{2,1,0:T(8,128)(2,1)}, u32[]{:S(2)}) copy-start(bf16[3,64,768]{2,1,0:T(8,128)(2,1)} %copy-done.5) | copy-start | bytes 884740
  83.8 1.0 %copy-start.8 = (bf16[3,64,768]{2,1,0:T(8,128)(2,1)S(1)}, bf16[3,64,768]{2,1,0:T(8,128)(2,1)}, u32[]{:S(2)}) copy-start(bf16[3,64,768]{2,1,0:T(8,128)(2,1)} %copy-done.7) | copy-start | bytes 884740

commit v2 on v1

v2 whole, which is shorter than its diff:
```python
import functools

import jax
import jax.numpy as jnp
from jax import lax
from jax.experimental import pallas as pl
from jax.experimental.pallas import tpu as pltpu
from jax.sharding import PartitionSpec as P

HD = 64
SPACE_COST = 10_000_000_000
epsilon = 1e-06
NT = (((1,), (1,)), ((), ()))
VM = pl.BlockSpec(memory_space=pltpu.VMEM)
SM = pl.BlockSpec(memory_space=pltpu.SMEM)
HB = pl.BlockSpec(memory_space=pltpu.HBM)


def params(mib=20):
    return pltpu.CompilerParams(vmem_limit_bytes=mib * 1024 * 1024)


def cost(flops, size):
    return pl.CostEstimate(flops=flops, bytes_accessed=size, transcendentals=0)


def normed(floats, gain):
    mean = jnp.mean(floats * floats, axis=-1, keepdims=True)
    gain = gain.reshape(1, -1)
    return (floats * lax.rsqrt(mean + epsilon) * gain).astype(jnp.bfloat16)


def dot_nt(a, b):
    return lax.dot_general(a, b, NT, preferred_element_type=jnp.float32)


def project_kernel(t0, t1, t2, gain_ref, w_ref, out_ref):
    var_count, rows, depth = t0.shape
    gain = gain_ref[...]
    x = [normed(t[v].astype(jnp.float32), gain) for v in range(var_count) for t in (t0, t1, t2)]
    x = jnp.concatenate(x, axis=0)
    out_ref[...] = dot_nt(x, w_ref[...]).astype(jnp.bfloat16)


def time_kernel(
    base_ref, early_ref, t3, m0, m1, m2, m3, gain_ref, w_ref, o0, o1, o2, o3
):
    outs, masks = (o0, o1, o2, o3), (m0, m1, m2, m3)
    var_count, rows, depth = t3.shape
    width = w_ref.shape[0] // 3
    blocks = len(outs)
    total = rows * blocks
    gain = gain_ref[...]
    x = jnp.concatenate([normed(t3[v].astype(jnp.float32), gain) for v in range(var_count)], axis=0)
    late = dot_nt(x, w_ref[...]).astype(jnp.bfloat16)
    row = lax.broadcasted_iota(jnp.int32, (total, total), 0)
    col = lax.broadcasted_iota(jnp.int32, (total, total), 1)

    def positions(index):
        where = index + base_ref[0]
        for block in range(1, blocks):
            shift = base_ref[block] - block * rows
            where = jnp.where(index >= block * rows, index + shift, where)
        return where

    query_pos, key_pos = positions(row), positions(col)
    causal, same = key_pos <= query_pos, key_pos == query_pos
    head_of = lax.broadcasted_iota(jnp.int32, (1, width), 1) // HD
    marks = jnp.concatenate([m[...] for m in masks], axis=1)
    early = rows * (blocks - 1)
    for v in range(var_count):
        projected = jnp.concatenate(
            [early_ref[v * early : (v + 1) * early], late[v * rows : (v + 1) * rows]], axis=0
        )
        queries = projected[:, :width] * jnp.bfloat16(HD ** (-0.5))
        keys = projected[:, width : 2 * width]
        values = projected[:, 2 * width :]
        observed = marks[v : v + 1, :] > 0
        bias = jnp.where(causal & (observed | same), 0.0, -jnp.inf)
        attended = jnp.zeros((total, width), jnp.float32)
        for head in range(width // HD):
            mine = head_of == head
            scores = dot_nt(jnp.where(mine, queries, 0), keys) + bias
            raised = jnp.exp(scores - jnp.max(scores, axis=-1, keepdims=True))
            share = 1.0 / jnp.sum(raised, axis=-1, keepdims=True)
            weights = raised.astype(jnp.bfloat16)
            mixed = jnp.dot(weights, values, preferred_element_type=jnp.float32) * share
            attended = jnp.where(mine, mixed, attended)
        attended = attended.astype(jnp.bfloat16)
        for block, out in enumerate(outs):
            out[v] = attended[block * rows : (block + 1) * rows]


def mid_kernel(
    place_ref, a0, a1, a2, a3, w0, w1, w2, wa, wb, tok_ref, gain_ref,
    mid_ref, x_ref, f1_ref, f2_ref, last,
):
    half = wa.shape[1]
    core = place_ref[0]
    last[pl.ds(pl.multiple_of(core * half, 32), half), :] = wa[0]
    last[pl.ds(pl.multiple_of((1 - core) * half, 32), half), :] = wb[0]
    var_count, rows, depth = tok_ref.shape
    width = a0.shape[2]
    gain = gain_ref[...]
    summed = 0.0
    for a, w in ((a0, w0), (a1, w1.at[0]), (a2, w2.at[0]), (a3, last)):
        attended = a[...].reshape(var_count * rows, width)
        summed = summed + jnp.dot(attended, w[...], preferred_element_type=jnp.float32)
    mid = tok_ref[...].astype(jnp.float32).reshape(var_count * rows, depth) + summed
    mid = mid.astype(jnp.bfloat16)
    x_ref[...] = normed(mid.astype(jnp.float32), gain).reshape(tok_ref.shape)
    mid_ref[...] = mid.reshape(tok_ref.shape)
    far = f1_ref.shape[0]
    f1_ref[...] = x_ref[pl.ds(place_ref[1], far)]
    f2_ref[...] = x_ref[pl.ds(place_ref[2], far)]


def half_kernel(parts, place_ref, *refs):
    *sources, out, sems = refs
    half = out.shape[1]
    at = pl.multiple_of(place_ref[0] * half, 32)
    copies, kind = [], 0
    for source, (low, high) in zip(sources, parts):
        size = high - low
        cut = source.at[low:high, pl.ds(at, half)]
        copies.append(pltpu.make_async_copy(cut, out.at[kind : kind + size], sems.at[len(copies)]))
        copies[-1].start()
        kind += size
    for copy in copies:
        copy.wait()


def needed(u, w, var_count, far_count):
    if w < 3 * var_count:
        return True
    w -= 3 * var_count
    if w < far_count:
        offset = u + 2 * var_count - (var_count - far_count) - w
    else:
        offset = 2 * var_count + (w - far_count) - u
    return offset <= 2 * var_count - 1


def join_halves(place_ref, first, second, target, at):
    half = first.shape[0]
    core = place_ref[0]
    target[pl.ds(pl.multiple_of(at + core * half, 32), half), :] = first[...]
    target[pl.ds(pl.multiple_of(at + (1 - core) * half, 32), half), :] = second[...]


def window_kernel(place_ref, x0, xs, xo, f1, f2, xall):
    var_count, far_count = x0.shape[0], f1.shape[0]
    for block, x in enumerate((x0, xs, xo)):
        xall[block * var_count : (block + 1) * var_count] = x[...]
    xall[pl.ds(3 * var_count + place_ref[3] * far_count, far_count)] = f1[...]
    xall[pl.ds(3 * var_count + place_ref[4] * far_count, far_count)] = f2[...]


def out_kernel(place_ref, before, att, u0, u1, u2, ua, ub, mid_ref, out_ref, uall):
    width = u0.shape[0]
    for group, u in enumerate((u0, u1.at[0], u2.at[0])):
        uall[group * width : (group + 1) * width, :] = u[...]
    join_halves(place_ref, ua.at[3], ub.at[3], uall, 3 * width)
    summed, at = mid_ref[...].astype(jnp.float32).reshape(att.shape[0], -1), 0
    for attended in (before, att):
        size = attended.shape[1]
        summed = summed + jnp.dot(
            attended[...], uall[at : at + size, :], preferred_element_type=jnp.float32
        )
        at += size
    out_ref[...] = summed.astype(jnp.bfloat16).reshape(out_ref.shape)


def space_kernel(halves, var_count, place_ref, ids_ref, xall, *refs):
    *weights, out_ref, wall, qbuf, kbuf, vbuf = refs
    count, rows, depth = xall.shape
    far_count = var_count - 1
    inner = wall.shape[1]
    core = place_ref[0]
    for kind in range(3):
        if halves:
            join_halves(place_ref, weights[0].at[kind], weights[1].at[kind], wall.at[kind], 0)
        else:
            width = inner // len(weights)
            for group, weight in enumerate(weights):
                wall[kind, group * width : (group + 1) * width, :] = weight[kind]
    heads = inner // HD

    variate = place_ref[5] * var_count
    starts = (0, (1 - 2 * core) * var_count, (2 * core - 1) * var_count)
    offsets = [start + u for start in starts for u in range(var_count)]
    offsets += [u - var_count - far_count for u in range(far_count)]
    offsets += [u + 2 * var_count for u in range(far_count)]
    ids = []
    for offset in offsets:
        at = variate + offset
        inside = (at >= 0) & (at < ids_ref.shape[0])
        ids.append(jnp.where(inside, ids_ref[jnp.clip(at, 0, ids_ref.shape[0] - 1)], -1))

    scaled = dot_nt(xall[:var_count].reshape(var_count * rows, depth), wall[0]).astype(jnp.bfloat16)
    qbuf[...] = scaled * jnp.bfloat16(HD ** (-0.5))
    x_all = xall[...].reshape(count * rows, depth)
    kbuf[...] = dot_nt(x_all, wall[1]).astype(jnp.bfloat16)
    vbuf[...] = dot_nt(x_all, wall[2]).astype(jnp.bfloat16)

    lanes = 128
    lane = lax.broadcasted_iota(jnp.int32, (1, lanes), 1)
    lane_u = lane // heads
    sum_row = lax.broadcasted_iota(jnp.int32, (inner, lanes), 0) // HD
    sum_col = lax.broadcasted_iota(jnp.int32, (inner, lanes), 1)
    spread_row = lax.broadcasted_iota(jnp.int32, (lanes, inner), 0)
    spread_col = lax.broadcasted_iota(jnp.int32, (lanes, inner), 1) // HD
    collect = [(sum_row + u * heads == sum_col).astype(jnp.bfloat16) for u in range(var_count)]
    spread = [(spread_col + u * heads == spread_row).astype(jnp.bfloat16) for u in range(var_count)]
    own_id = jnp.full((1, lanes), -2, jnp.int32)
    for u in range(var_count):
        own_id = jnp.where(lane_u == u, ids[u], own_id)
    keys = kbuf[...].reshape(count, rows, inner)
    score = 0.0
    for u in range(var_count):
        product = keys * qbuf[u * rows : (u + 1) * rows, :][None]
        score = score + jnp.dot(
            product.reshape(count * rows, inner), collect[u], preferred_element_type=jnp.float32
        )
    scores = [
        jnp.where(own_id == ids[w], score[w * rows : (w + 1) * rows], -jnp.inf) for w in range(count)
    ]
    highest = functools.reduce(jnp.maximum, scores)
    highest = jnp.where(lane_u < var_count, highest, 0.0)
    raised = [jnp.exp(one - highest) for one in scores]
    total = functools.reduce(lambda a, b: a + b, raised)
    share = 1.0 / jnp.where(lane_u < var_count, total, 1.0)
    prob = jnp.concatenate([(one * share).astype(jnp.bfloat16) for one in raised], axis=0)
    for u in range(var_count):
        each = jnp.dot(prob, spread[u], preferred_element_type=jnp.float32)
        mixed = None
        for w in range(count):
            if needed(u, w, var_count, far_count):
                at = slice(w * rows, (w + 1) * rows)
                term = each[at] * vbuf[at, :].astype(jnp.float32)
                mixed = term if mixed is None else mixed + term
        out_ref[u * rows : (u + 1) * rows, :] = mixed.astype(jnp.bfloat16)


def routes(var_size, patch_size):
    def route(even, odd):
        pairs = []
        for v in range(var_size):
            for p in range(patch_size):
                step = odd if v % 2 else even
                pairs.append((v * patch_size + p, v * patch_size + (p ^ step)))
        return pairs
    return route(1, 2), route(2, 1), route(3, 3)


def tied(blocks, after):
    return lax.optimization_barrier((*blocks, after))


def pairs_of(size, partner):
    return [(i, partner(i)) for i in range(size) if 0 <= partner(i) < size]


def on_device(
    tokens, patch_mask, group_ids, time_gain, time_qkv, time_out, space_gain, space_qkv, space_out
):
    var_size, patch_size = lax.axis_size("var"), lax.axis_size("patch")
    var_index, patch_index = lax.axis_index("var"), lax.axis_index("patch")
    core, level = var_index % 2, (var_index // 2) % 2
    both = ("var", "patch")
    first, second, third = routes(var_size, patch_size)
    swap = pairs_of(var_size, lambda i: i ^ 1)

    def send(block, route):
        return lax.ppermute(block, both, route)

    def partner(block):
        return lax.ppermute(block, "var", swap)

    tok = jnp.transpose(tokens, (1, 0, 2))
    mask = jnp.transpose(patch_mask)
    qkv_t = jnp.transpose(time_qkv, (1, 2, 0))
    qkv_s = jnp.transpose(space_qkv, (1, 2, 0))
    var_count, rows, depth = tok.shape
    kind, width, _ = qkv_t.shape
    half = width // 2

    tok1, tok2 = send(tok, first), send(tok, second)
    mask1, mask2, mask3 = send(mask, first), send(mask, second), send(mask, third)
    tok1f, mask1, mask2, mask3 = lax.optimization_barrier((tok1, mask1, mask2, mask3))
    tok3 = send(tok1f, second)
    weight = qkv_t.reshape(kind * width, depth)
    bf = jnp.bfloat16
    early = pl.pallas_call(
        project_kernel,
        out_shape=jax.ShapeDtypeStruct((3 * var_count * rows, kind * width), bf),
        in_specs=[VM] * 5,
        out_specs=VM,
        compiler_params=params(),
        cost_estimate=cost(1000, 1000),
        name="project",
    )(tok, tok1f, tok2, time_gain, weight)

    def half_of(parts, *blocks, weight=1000):
        return pl.pallas_call(
            functools.partial(half_kernel, parts),
            out_shape=jax.ShapeDtypeStruct((sum(b - a for a, b in parts), half, depth), bf),
            in_specs=[SM] + [HB] * len(blocks),
            out_specs=HB,
            scratch_shapes=[pltpu.SemaphoreType.DMA((len(blocks),))],
            compiler_params=params(1),
            cost_estimate=cost(weight, 1000),
            name="half",
        )(place, *blocks)

    far_count = var_count - 1
    place = jnp.stack([
        core, jnp.where(level == 0, 1, 0), jnp.where(level == 0, 0, 1),
        jnp.where(level == 0, 1, 0), jnp.where(level == 0, 0, 1), var_index,
    ]).astype(jnp.int32)
    t_half = half_of(((0, 1),), time_out[None])
    t_own, t_half, early = lax.optimization_barrier((time_out[None], t_half, early))
    t1, ta = send(t_own, first), send(t_half, third)

    near, far_step = jnp.where(core == 0, 1, 2), jnp.where(core == 0, 2, 1)
    bases = jnp.stack(
        [patch_index, patch_index ^ near, patch_index ^ far_step, patch_index ^ 3]
    ).astype(jnp.int32) * rows
    block = jax.ShapeDtypeStruct((var_count, rows, width), bf)
    att = pl.pallas_call(
        time_kernel,
        out_shape=[block] * 4,
        in_specs=[SM] + [VM] * 8,
        out_specs=[VM] * 4,
        compiler_params=params(),
        cost_estimate=cost(1000, 1000),
        name="time",
    )(bases, early, tok3, mask, mask1, mask2, mask3, time_gain, weight)
    att0 = att[0]
    att1, att3, att2 = send(att[1], first), send(att[3], third), send(att[2], second)
    s_qkv, s_out, t1, ta, att1, att2, att3 = lax.optimization_barrier(
        (qkv_s, space_out[None], t1, ta, att1, att2, att3)
    )
    t2, tb = partner(t1), partner(ta)
    qkv1, u1 = send(s_qkv, first), send(s_out, first)

    whole = jax.ShapeDtypeStruct((var_count, rows, depth), jnp.bfloat16)
    part = jax.ShapeDtypeStruct((far_count, rows, depth), jnp.bfloat16)
    mid, x_own, far1, far2 = pl.pallas_call(
        mid_kernel,
        out_shape=[whole, whole, part, part],
        in_specs=[SM] + [VM] * 11,
        out_specs=[VM] * 4,
        scratch_shapes=[pltpu.VMEM((width, depth), bf)],
        compiler_params=params(),
        cost_estimate=cost(1000, 1000),
        name="mid",
    )(place, att0, att1, att2, att3, time_out, t1, t2, ta, tb, tok, space_gain)

    x_other = lax.ppermute(x_own, "var", pairs_of(var_size, lambda i: i + 1 if i % 2 else i - 1))
    x_swap = partner(x_own)
    far1 = lax.ppermute(far1, "var", pairs_of(var_size, lambda i: i ^ 2))
    far2 = lax.ppermute(
        far2, "var", pairs_of(var_size, lambda i: i + 2 if (i // 2) % 2 else i - 2)
    )
    count = 3 * var_count + 2 * far_count
    own_rows = var_count * rows
    window = pl.pallas_call(
        window_kernel,
        out_shape=jax.ShapeDtypeStruct((count, rows, depth), bf),
        in_specs=[SM] + [VM] * 5,
        out_specs=VM,
        compiler_params=params(8),
        cost_estimate=cost(1000, 1000),
        name="window",
    )(place, x_own, x_swap, x_other, far1, far2)
    qkv1, u1, window = lax.optimization_barrier((qkv1, u1, window))
    rest_a = send(half_of(((0, 3), (0, 1)), qkv1, u1), second)
    qkv2 = partner(qkv1)

    def attend(groups, *weights):
        inner = width * groups
        return pl.pallas_call(
            functools.partial(space_kernel, groups == 1, var_count),
            out_shape=jax.ShapeDtypeStruct((own_rows, inner), bf),
            in_specs=[SM] * 2 + [VM] * (1 + len(weights)),
            out_specs=VM,
            scratch_shapes=[
                pltpu.VMEM((kind, inner, depth), bf),
                pltpu.VMEM((own_rows, inner), bf),
                pltpu.VMEM((count * rows, inner), bf),
                pltpu.VMEM((count * rows, inner), bf),
            ],
            compiler_params=params(),
            cost_estimate=cost(1000 if groups == 1 else SPACE_COST, 1000),
            name="space_last" if groups == 1 else "space",
        )(place, group_ids, window, *weights)

    first_parts = attend(3, qkv_s, qkv1, qkv2)
    rest_a, u1, first_parts = lax.optimization_barrier((rest_a, u1, first_parts))
    rest_b, u2 = partner(rest_a), partner(u1)
    last_part = attend(1, rest_a, rest_b)
    out = pl.pallas_call(
        out_kernel,
        out_shape=whole,
        in_specs=[SM] + [VM] * 8,
        out_specs=VM,
        scratch_shapes=[pltpu.VMEM((4 * width, depth), bf)],
        compiler_params=params(),
        cost_estimate=cost(1000, 1000),
        name="out",
    )(place, first_parts, last_part, space_out, u1, u2, rest_a, rest_b, mid)
    return jnp.transpose(out, (1, 0, 2))


def solution(mesh):
    in_specs = (
        P("patch", ("parts", "var"), None),
        P("patch", ("parts", "var")),
        P("parts"),
        P(),
        P(None, None, "patch"),
        P("patch", None),
        P(),
        P(None, None, "patch"),
        P("patch", None),
    )
    out_specs = P("patch", ("parts", "var"), None)
    return jax.shard_map(
        on_device, mesh=mesh, in_specs=in_specs, out_specs=out_specs, check_vma=False
    )
```

time: 92.6 us -> 70 us (0.76)
  the two profiles are of different devices: /device:TPU:16 before, /device:TPU:9 now
where the time goes in v2:
time: 70 us; the launch traced here: 69.7 us
  starting transfers between devices  28.2 us (40%)
  waiting for transfers between devices  20.3 us (29%)
  Pallas kernels  17.1 us (24%)
  local copies, waits for them, and re-layouts  3.9 us (6%)
    ppermute x14, waiting for transfers between devices, send(): return lax.ppermute(block, both, route)  13.1 us
    ppermute x14, starting transfers between devices, send(): return lax.ppermute(block, both, route)  12.4 us
    pallas_call x2, Pallas kernels, attend(): pl.pallas_call(functools.partial(space_kernel, groups == 1, var_count), o...  8.4 us
    ppermute x6, starting transfers between devices, partner(): return lax.ppermute(block, 'var', swap)  8.06 us
    ppermute x1, starting transfers between devices, on_device(): lax.ppermute(x_own, 'var', pairs_of(var_size, lambda i: i + 1 if i % 2 el...  4.43 us
    unnamed x26, local copies, waits for them, and re-layouts  3.82 us
    ppermute x6, waiting for transfers between devices, partner(): return lax.ppermute(block, 'var', swap)  3.62 us
    ppermute x1, waiting for transfers between devices, on_device(): lax.ppermute(far2, 'var', pairs_of(var_size, lambda i: i + 2 if i // 2 %...  3.2 us
  transfers between devices with their start and end apart: 23, of which 12 were waited for; matrix products, arithmetic and copies ran while one was open for 0% of the time, Pallas kernels for 22%

profile of v2, /device:TPU:9, one launch (start us, length us, event | category | flops | bytes accessed | tf_op | source)
XLA Modules:
  0.0 69.7 jit_solution(1116008803128676233)
XLA Ops:
  0.0 1.2 %collective-permute-start = (bf16[3,64,768]{2,1,0:T(8,128)(2,1)}, bf16[3,64,768]{2,1,0:T(8,128)(2,1)S(1)}, u32[]{:S(2)}, u32[]{:S(2)}) collective-permute-start(bf16[3,64,768]{2,1,0:T(8,128)(2,1)} %bitcast.19), channel_id=1, source_target_pairs={{0,1},{1,0},{2,3},{3,2},{4,6},{5,7},{6,4},{7,5},{8,9},{9,8},{10,11... | collective-permute-start | bytes 884744 | tf_op jit(solution)/shard_map/ppermute | solution.py:275
  1.2 1.2 %collective-permute-start.4 = (bf16[3,64,768]{2,1,0:T(8,128)(2,1)}, bf16[3,64,768]{2,1,0:T(8,128)(2,1)S(1)}, u32[]{:S(2)}, u32[]{:S(2)}) collective-permute-start(bf16[3,64,768]{2,1,0:T(8,128)(2,1)} %bitcast.20), channel_id=1, source_target_pairs={{0,2},{1,3},{2,0},{3,1},{4,5},{5,4},{6,7},{7,6},{8,10},{9,11},{10,... | collective-permute-start | bytes 884744 | tf_op jit(solution)/shard_map/ppermute | solution.py:275
  2.5 0.2 collective-permute-start.1
  2.7 0.3 collective-permute-start.2
  2.9 2.2 %collective-permute-start.3 = (s32[3,64]{1,0:T(4,128)}, s32[3,64]{1,0:T(4,128)S(1)}, u32[]{:S(2)}, u32[]{:S(2)}) collective-permute-start(s32[3,64]{1,0:T(4,128)} %bitcast.28), channel_id=1, source_target_pairs={{0,3},{1,2},{2,1},{3,0},{4,7},{5,6},{6,5},{7,4},{8,11},{9,10},{10,... | collective-permute-start | bytes 2312 | tf_op jit(solution)/shard_map/ppermute | solution.py:275
  5.1 1.5 %collective-permute-done.1.m1 = s32[3,64]{1,0:T(4,128)S(1)} collective-permute-done((s32[3,64]{1,0:T(4,128)}, s32[3,64]{1,0:T(4,128)S(1)}, u32[]{:S(2)}, u32[]{:S(2)}) %collective-permute-start.1) | collective-permute-done | bytes 800 | tf_op jit(solution)/shard_map/ppermute | solution.py:275
  6.6 3.9 %collective-permute-done.2.m2 = s32[3,64]{1,0:T(4,128)S(1)} collective-permute-done((s32[3,64]{1,0:T(4,128)}, s32[3,64]{1,0:T(4,128)S(1)}, u32[]{:S(2)}, u32[]{:S(2)}) %collective-permute-start.2) | collective-permute-done | bytes 800 | tf_op jit(solution)/shard_map/ppermute | solution.py:275
  10.4 0.0 collective-permute-done.3.m3
  10.4 0.0 collective-permute-done.t1
  10.4 1.2 %collective-permute-start.7 = (bf16[3,64,768]{2,1,0:T(8,128)(2,1)S(1)}, bf16[3,64,768]{2,1,0:T(8,128)(2,1)S(1)}, u32[]{:S(2)}, u32[]{:S(2)}) collective-permute-start(bf16[3,64,768]{2,1,0:T(8,128)(2,1)S(1)} %collective-permute-done.t1), channel_id=1, source_target_pairs={{0,2},{1,3},{2,0},{3,1},{4,5},{5,4},{6,7},{7,6},{8,10},{9,11},{10,... | collective-permute-start | bytes 884744 | tf_op jit(solution)/shard_map/ppermute | solution.py:275
  11.7 0.1 stack.36.place_ref
  11.7 1.0 %copy-done.4 = bf16[192,768]{1,0:T(8,128)(2,1)S(1)} copy-done((bf16[192,768]{1,0:T(8,128)(2,1)S(1)}, bf16[192,768]{1,0:T(8,128)(2,1)}, u32[]{:S(2)}) %copy-start.4) | copy-done | bytes 294936
  12.7 0.7 %half.2 = bf16[1,96,768]{2,1,0:T(8,128)(2,1)S(1)} custom-call(s32[6]{0:T(128)S(1)} %stack.36.place_ref, bf16[1,192,768]{2,1,0:T(8,128)(2,1)S(1)} %bitcast.23), custom_call_target="tpu_custom_call" | custom-call | flops 1000 | bytes 1000 | tf_op jit(solution)/shard_map/half/pallas_call | solution.py:305
  13.5 0.0 collective-permute-done.4.t2
  13.5 0.0 copy-start
  13.5 1.2 %copy-done = bf16[768,3,192]{0,2,1:T(8,128)(2,1)S(1)} copy-done((bf16[768,3,192]{0,2,1:T(8,128)(2,1)S(1)}, bf16[768,3,192]{0,2,1:T(8,128)(2,1)}, u32[]{:S(2)}) %copy-start) | copy-done | bytes 884760
  14.7 1.0 %copy-done.2 = bf16[64,3,768]{2,0,1:T(8,128)(2,1)S(1)} copy-done((bf16[64,3,768]{2,0,1:T(8,128)(2,1)S(1)}, bf16[64,3,768]{2,0,1:T(8,128)(2,1)}, u32[]{:S(2)}) %copy-start.2) | copy-done | bytes 294936
  15.6 0.7 copy-done.7
  16.3 1.0 %project.1.early_ref = bf16[576,576]{1,0:T(8,128)(2,1)S(1)} custom-call(bf16[3,64,768]{2,1,0:T(8,128)(2,1)S(1)} %bitcast.21, bf16[3,64,768]{2,1,0:T(8,128)(2,1)S(1)} %collective-permute-done.t1, bf16[3,64,768]{2,1,0:T(8,128)(2,1)S(1)} %collective-permute-done.4.t2, f32[768]{0:T(1024)S(1)} %copy-done.7, bf16[576,768]{1,0:T(8,128)(2,1)S(1)} %bitcast.17), custom_call_target="tpu_custom_call" | custom-call | flops 1000 | bytes 1000 | tf_op jit(solution)/shard_map/project/pallas_call | solution.py:294
  17.3 0.0 copy-start.3
  17.3 0.0 copy-start.9
  17.3 1.2 %collective-permute-start.5 = (bf16[1,192,768]{2,1,0:T(8,128)(2,1)S(1)}, bf16[1,192,768]{2,1,0:T(8,128)(2,1)S(1)}, u32[]{:S(2)}, u32[]{:S(2)}) collective-permute-start(bf16[1,192,768]{2,1,0:T(8,128)(2,1)S(1)} %bitcast.24), channel_id=1, source_target_pairs={{0,1},{1,0},{2,3},{3,2},{4,6},{5,7},{6,4},{7,5},{8,9},{9,8},{10,11... | collective-permute-start | bytes 884744 | tf_op jit(solution)/shard_map/ppermute | solution.py:275
  18.5 0.3 collective-permute-start.6
  18.9 0.1 add_multiply_fusion.base_ref
  18.9 0.0 collective-permute-done.7.t3
  18.9 2.5 %time.1 = (bf16[3,64,192]{2,1,0:T(8,128)(2,1)S(1)}, bf16[3,64,192]{2,1,0:T(8,128)(2,1)S(1)}, bf16[3,64,192]{2,1,0:T(8,128)(2,1)S(1)}, bf16[3,64,192]{2,1,0:T(8,128)(2,1)S(1)}) custom-call(s32[4]{0:T(128)S(1)} %add_multiply_fusion.base_ref, bf16[576,576]{1,0:T(8,128)(2,1)S(1)} %project.1.early_ref, bf16[3,64,768]{2,1,0:T(8,128)(2,1)S(1)} %collective-permute-done.7.t3, ...), custom_call_target="tpu_custom_call" | custom-call | flops 1000 | bytes 1000 | tf_op jit(solution)/shard_map/time/pallas_call | solution.py:330
  21.4 0.0 copy-start.6
  21.5 2.1 %collective-permute-start.10 = (bf16[3,64,192]{2,1,0:T(8,128)(2,1)S(1)}, bf16[3,64,192]{2,1,0:T(8,128)(2,1)S(1)}, u32[]{:S(2)}, u32[]{:S(2)}) collective-permute-start(bf16[3,64,192]{2,1,0:T(8,128)(2,1)S(1)} %get-tuple-element.42), channel_id=1, source_target_pairs={{0,3},{1,2},{2,1},{3,0},{4,7},{5,6},{6,5},{7,4},{8,11},{9,10},{10,... | collective-permute-start | bytes 221192 | tf_op jit(solution)/shard_map/ppermute | solution.py:275
  23.5 0.4 collective-permute-start.8
  23.9 0.3 collective-permute-start.9
  24.2 0.8 %collective-permute-done.6.wa = bf16[1,96,768]{2,1,0:T(8,128)(2,1)S(1)} collective-permute-done((bf16[1,96,768]{2,1,0:T(8,128)(2,1)S(1)}, bf16[1,96,768]{2,1,0:T(8,128)(2,1)S(1)}, u32[]{:S(2)}, u32[]{:S(2)}) %collective-permute-start.6) | collective-permute-done | bytes 147488 | tf_op jit(solution)/shard_map/ppermute | solution.py:275
  24.9 0.0 collective-permute-done.5.w1
  24.9 2.4 %collective-permute-done.10.a3 = bf16[3,64,192]{2,1,0:T(8,128)(2,1)S(1)} collective-permute-done((bf16[3,64,192]{2,1,0:T(8,128)(2,1)S(1)}, bf16[3,64,192]{2,1,0:T(8,128)(2,1)S(1)}, u32[]{:S(2)}, u32[]{:S(2)}) %collective-permute-start.10) | collective-permute-done | bytes 73760 | tf_op jit(solution)/shard_map/ppermute | solution.py:275
  27.3 1.8 %collective-permute-done.8.a1 = bf16[3,64,192]{2,1,0:T(8,128)(2,1)S(1)} collective-permute-done((bf16[3,64,192]{2,1,0:T(8,128)(2,1)S(1)}, bf16[3,64,192]{2,1,0:T(8,128)(2,1)S(1)}, u32[]{:S(2)}, u32[]{:S(2)}) %collective-permute-start.8) | collective-permute-done | bytes 73760 | tf_op jit(solution)/shard_map/ppermute | solution.py:275
  29.2 0.1 collective-permute-done.9.a2
  29.3 0.6 collective-permute-start.11
  29.9 3.4 %collective-permute-start.13 = (bf16[1,192,768]{2,1,0:T(8,128)(2,1)S(1)}, bf16[1,192,768]{2,1,0:T(8,128)(2,1)S(1)}, u32[]{:S(2)}, u32[]{:S(2)}) collective-permute-start(bf16[1,192,768]{2,1,0:T(8,128)(2,1)S(1)} %collective-permute-done.5.w1), channel_id=1, source_target_pairs={{0,4},{4,0},{8,12},{12,8},{16,20},{20,16},{24,28},{28,24},{1,5},{5... | collective-permute-start | bytes 884744 | tf_op jit(solution)/shard_map/ppermute | solution.py:278
  33.3 0.0 collective-permute-start.14
  33.3 1.4 %collective-permute-done.14.wb = bf16[1,96,768]{2,1,0:T(8,128)(2,1)S(1)} collective-permute-done((bf16[1,96,768]{2,1,0:T(8,128)(2,1)S(1)}, bf16[1,96,768]{2,1,0:T(8,128)(2,1)S(1)}, u32[]{:S(2)}, u32[]{:S(2)}) %collective-permute-start.14) | collective-permute-done | bytes 147488 | tf_op jit(solution)/shard_map/ppermute | solution.py:278
  34.7 0.0 collective-permute-done.13.w2
  34.7 1.2 %mid.1 = (bf16[3,64,768]{2,1,0:T(8,128)(2,1)S(1)}, bf16[3,64,768]{2,1,0:T(8,128)(2,1)S(1)}, bf16[2,64,768]{2,1,0:T(8,128)(2,1)S(1)}, bf16[2,64,768]{2,1,0:T(8,128)(2,1)S(1)}) custom-call(s32[6]{0:T(128)S(1)} %stack.36.place_ref, bf16[3,64,192]{2,1,0:T(8,128)(2,1)S(1)} %get-tuple-element.45.a0, bf16[3,64,192]{2,1,0:T(8,128)(2,1)S(1)} %collective-permute-done.8.a1, ...), custom_call_target="tpu_custom_call" | custom-call | flops 1000 | bytes 1000 | tf_op jit(solution)/shard_map/mid/pallas_call | solution.py:349
  35.9 0.1 collective-permute-start.17
  36.0 0.6 collective-permute-start.15
  36.6 4.4 %collective-permute-start.16 = (bf16[3,64,768]{2,1,0:T(8,128)(2,1)S(1)}, bf16[3,64,768]{2,1,0:T(8,128)(2,1)S(1)}, u32[]{:S(2)}, u32[]{:S(2)}) collective-permute-start(bf16[3,64,768]{2,1,0:T(8,128)(2,1)S(1)} %get-tuple-element.51.x0), channel_id=1, source_target_pairs={{4,8},{8,4},{12,16},{16,12},{20,24},{24,20},{5,9},{9,5},{13,17},{1... | collective-permute-start | bytes 884744 | tf_op jit(solution)/shard_map/ppermute | solution.py:360
  41.0 0.7 collective-permute-start.12
  41.7 0.4 collective-permute-done.17.f1
  42.1 3.2 %collective-permute-start.18 = (bf16[2,64,768]{2,1,0:T(8,128)(2,1)S(1)}, bf16[2,64,768]{2,1,0:T(8,128)(2,1)S(1)}, u32[]{:S(2)}, u32[]{:S(2)}) collective-permute-start(bf16[2,64,768]{2,1,0:T(8,128)(2,1)S(1)} %get-tuple-element.53), channel_id=1, source_target_pairs={{8,16},{12,20},{16,8},{20,12},{9,17},{13,21},{17,9},{21,13},{10,18... | collective-permute-start | bytes 589832 | tf_op jit(solution)/shard_map/ppermute | solution.py:363
  45.3 3.2 %collective-permute-done.18.f2 = bf16[2,64,768]{2,1,0:T(8,128)(2,1)S(1)} collective-permute-done((bf16[2,64,768]{2,1,0:T(8,128)(2,1)S(1)}, bf16[2,64,768]{2,1,0:T(8,128)(2,1)S(1)}, u32[]{:S(2)}, u32[]{:S(2)}) %collective-permute-start.18) | collective-permute-done | bytes 196640 | tf_op jit(solution)/shard_map/ppermute | solution.py:363
  48.5 0.0 collective-permute-done.15.xs
  48.5 0.0 collective-permute-done.16.xo
  48.5 0.6 window.1.xall
  49.1 0.0 copy-start.11
  49.1 0.0 collective-permute-done.12.refs_1_.u1
  49.1 3.2 %collective-permute-start.20 = (bf16[3,192,768]{2,1,0:T(8,128)(2,1)S(1)}, bf16[3,192,768]{2,1,0:T(8,128)(2,1)S(1)}, u32[]{:S(2)}, u32[]{:S(2)}) collective-permute-start(bf16[3,192,768]{2,1,0:T(8,128)(2,1)S(1)} %collective-permute-done.11.refs_0_.refs_1_), channel_id=1, source_target_pairs={{0,4},{4,0},{8,12},{12,8},{16,20},{20,16},{24,28},{28,24},{1,5},{5... | collective-permute-start | bytes 2654216 | tf_op jit(solution)/shard_map/ppermute | solution.py:278
  52.4 0.8 %half.3 = bf16[4,96,768]{2,1,0:T(8,128)(2,1)S(1)} custom-call(s32[6]{0:T(128)S(1)} %stack.36.place_ref, bf16[3,192,768]{2,1,0:T(8,128)(2,1)S(1)} %collective-permute-done.11.refs_0_.refs_1_, bf16[1,192,768]{2,1,0:T(8,128)(2,1)S(1)} %collective-permute-done.12.refs_1_.u1), custom_call_target="tpu_custom_call" | custom-call | flops 1000 | bytes 1000 | tf_op jit(solution)/shard_map/half/pallas_call | solution.py:305
  53.2 0.6 collective-permute-start.19
  53.8 0.6 collective-permute-done.20.refs_2_
  54.4 5.3 %space.1.before = bf16[192,576]{1,0:T(8,128)(2,1)S(1)} custom-call(s32[6]{0:T(128)S(1)} %stack.36.place_ref, s32[24]{0:T(128)S(1)} %copy-done.11, bf16[13,64,768]{2,1,0:T(8,128)(2,1)S(1)} %window.1.xall, bf16[3,192,768]{2,1,0:T(8,128)(2,1)S(1)} %bitcast.31, bf16[3,192,768]{2,1,0:T(8,128)(2,1)S(1)} %collective-permute-done.11.refs_0_.refs_1_, ...), custom_call_target="tpu_custom_call" | custom-call | flops 10000000000 | bytes 1000 | tf_op jit(solution)/shard_map/space/pallas_call | solution.py:383
  59.7 2.6 %collective-permute-done.19.refs_0_.ua = bf16[4,96,768]{2,1,0:T(8,128)(2,1)S(1)} collective-permute-done((bf16[4,96,768]{2,1,0:T(8,128)(2,1)S(1)}, bf16[4,96,768]{2,1,0:T(8,128)(2,1)S(1)}, u32[]{:S(2)}, u32[]{:S(2)}) %collective-permute-start.19) | collective-permute-done | bytes 589856 | tf_op jit(solution)/shard_map/ppermute | solution.py:275
  62.3 0.9 %collective-permute-start.21 = (bf16[4,96,768]{2,1,0:T(8,128)(2,1)S(1)}, bf16[4,96,768]{2,1,0:T(8,128)(2,1)S(1)}, u32[]{:S(2)}, u32[]{:S(2)}) collective-permute-start(bf16[4,96,768]{2,1,0:T(8,128)(2,1)S(1)} %collective-permute-done.19.refs_0_.ua), channel_id=1, source_target_pairs={{0,4},{4,0},{8,12},{12,8},{16,20},{20,16},{24,28},{28,24},{1,5},{5... | collective-permute-start | bytes 1769480 | tf_op jit(solution)/shard_map/ppermute | solution.py:278
  63.2 0.0 collective-permute-start.22
  63.2 1.6 %collective-permute-done.21.refs_1_.ub = bf16[4,96,768]{2,1,0:T(8,128)(2,1)S(1)} collective-permute-done((bf16[4,96,768]{2,1,0:T(8,128)(2,1)S(1)}, bf16[4,96,768]{2,1,0:T(8,128)(2,1)S(1)}, u32[]{:S(2)}, u32[]{:S(2)}) %collective-permute-start.21) | collective-permute-done | bytes 589856 | tf_op jit(solution)/shard_map/ppermute | solution.py:278
  64.8 3.1 %space_last.1.att = bf16[192,192]{1,0:T(8,128)(2,1)S(1)} custom-call(s32[6]{0:T(128)S(1)} %stack.36.place_ref, s32[24]{0:T(128)S(1)} %copy-done.11, bf16[13,64,768]{2,1,0:T(8,128)(2,1)S(1)} %window.1.xall, bf16[4,96,768]{2,1,0:T(8,128)(2,1)S(1)} %collective-permute-done.19.refs_0_.ua, bf16[4,96,768]{2,1,0:T(8,128)(2,1)S(1)} %collective-permute-done.21.refs_1_.ub), custom_call_target="tpu_custom_call" | custom-call | flops 1000 | bytes 1000 | tf_op jit(solution)/shard_map/space_last/pallas_call | solution.py:383
  67.9 1.8 %out.1 = bf16[3,64,768]{2,1,0:T(8,128)(2,1)} custom-call(s32[6]{0:T(128)S(1)} %stack.36.place_ref, bf16[192,576]{1,0:T(8,128)(2,1)S(1)} %space.1.before, bf16[192,192]{1,0:T(8,128)(2,1)S(1)} %space_last.1.att, bf16[192,768]{1,0:T(8,128)(2,1)S(1)} %copy-done.6, bf16[1,192,768]{2,1,0:T(8,128)(2,1)S(1)} %collective-permute-done.12.refs_1_.u1, ...), custom_call_target="tpu_custom_call" | custom-call | flops 1000 | bytes 1000 | tf_op jit(solution)/shard_map/out/pallas_call | solution.py:403
  (19 shorter events, 0.0 us)
Async XLA Ops:
  0.0 10.4 %collective-permute-start = (bf16[3,64,768]{2,1,0:T(8,128)(2,1)}, bf16[3,64,768]{2,1,0:T(8,128)(2,1)S(1)}, u32[]{:S(2)}, u32[]{:S(2)}) collective-permute-start(bf16[3,64,768]{2,1,0:T(8,128)(2,1)} %bitcast.19), channel_id=1, source_target_pairs={{0,1},{1,0},{2,3},{3,2},{4,6},{5,7},{6,4},{7,5},{8,9},{9,8},{10,11... | collective-permute-start | bytes 884744 | tf_op jit(solution)/shard_map/ppermute | solution.py:275
  1.2 12.2 %collective-permute-start.4 = (bf16[3,64,768]{2,1,0:T(8,128)(2,1)}, bf16[3,64,768]{2,1,0:T(8,128)(2,1)S(1)}, u32[]{:S(2)}, u32[]{:S(2)}) collective-permute-start(bf16[3,64,768]{2,1,0:T(8,128)(2,1)} %bitcast.20), channel_id=1, source_target_pairs={{0,2},{1,3},{2,0},{3,1},{4,5},{5,4},{6,7},{7,6},{8,10},{9,11},{10,... | collective-permute-start | bytes 884744 | tf_op jit(solution)/shard_map/ppermute | solution.py:275
  2.5 4.1 %collective-permute-start.1 = (s32[3,64]{1,0:T(4,128)}, s32[3,64]{1,0:T(4,128)S(1)}, u32[]{:S(2)}, u32[]{:S(2)}) collective-permute-start(s32[3,64]{1,0:T(4,128)} %bitcast.26), channel_id=1, source_target_pairs={{0,1},{1,0},{2,3},{3,2},{4,6},{5,7},{6,4},{7,5},{8,9},{9,8},{10,11... | collective-permute-start | bytes 2312 | tf_op jit(solution)/shard_map/ppermute | solution.py:275
  2.7 7.8 %collective-permute-start.2 = (s32[3,64]{1,0:T(4,128)}, s32[3,64]{1,0:T(4,128)S(1)}, u32[]{:S(2)}, u32[]{:S(2)}) collective-permute-start(s32[3,64]{1,0:T(4,128)} %bitcast.27), channel_id=1, source_target_pairs={{0,2},{1,3},{2,0},{3,1},{4,5},{5,4},{6,7},{7,6},{8,10},{9,11},{10,... | collective-permute-start | bytes 2312 | tf_op jit(solution)/shard_map/ppermute | solution.py:275
  2.9 7.5 %collective-permute-start.3 = (s32[3,64]{1,0:T(4,128)}, s32[3,64]{1,0:T(4,128)S(1)}, u32[]{:S(2)}, u32[]{:S(2)}) collective-permute-start(s32[3,64]{1,0:T(4,128)} %bitcast.28), channel_id=1, source_target_pairs={{0,3},{1,2},{2,1},{3,0},{4,7},{5,6},{6,5},{7,4},{8,11},{9,10},{10,... | collective-permute-start | bytes 2312 | tf_op jit(solution)/shard_map/ppermute | solution.py:275
  10.4 8.5 %collective-permute-start.7 = (bf16[3,64,768]{2,1,0:T(8,128)(2,1)S(1)}, bf16[3,64,768]{2,1,0:T(8,128)(2,1)S(1)}, u32[]{:S(2)}, u32[]{:S(2)}) collective-permute-start(bf16[3,64,768]{2,1,0:T(8,128)(2,1)S(1)} %collective-permute-done.t1), channel_id=1, source_target_pairs={{0,2},{1,3},{2,0},{3,1},{4,5},{5,4},{6,7},{7,6},{8,10},{9,11},{10,... | collective-permute-start | bytes 884744 | tf_op jit(solution)/shard_map/ppermute | solution.py:275
  11.7 1.0 %copy-start.4 = (bf16[192,768]{1,0:T(8,128)(2,1)S(1)}, bf16[192,768]{1,0:T(8,128)(2,1)}, u32[]{:S(2)}) copy-start(bf16[192,768]{1,0:T(8,128)(2,1)} %w0.1) | copy-start | bytes 884740
  12.7 4.6 %copy-start.5 = (bf16[192,768]{1,0:T(8,128)(2,1)S(1)}, bf16[192,768]{1,0:T(8,128)(2,1)}, u32[]{:S(2)}) copy-start(bf16[192,768]{1,0:T(8,128)(2,1)} %w0.1) | copy-start | bytes 884740
  12.7 6.2 %copy-start.8 = (f32[768]{0:T(1024)S(1)}, f32[768]{0:T(1024)}, u32[]{:S(2)}) copy-start(f32[768]{0:T(1024)} %gain_ref.4) | copy-start | bytes 9220
  12.7 6.2 %copy-start.10 = (s32[64,3]{0,1:T(4,128)S(1)}, s32[64,3]{0,1:T(4,128)}, u32[]{:S(2)}) copy-start(s32[64,3]{0,1:T(4,128)} %param.10) | copy-start | bytes 2308
  13.5 1.2 %copy-start = (bf16[768,3,192]{0,2,1:T(8,128)(2,1)S(1)}, bf16[768,3,192]{0,2,1:T(8,128)(2,1)}, u32[]{:S(2)}) copy-start(bf16[768,3,192]{0,2,1:T(8,128)(2,1)} %param.13) | copy-start | bytes 2654212
  14.7 1.0 %copy-start.2 = (bf16[64,3,768]{2,0,1:T(8,128)(2,1)S(1)}, bf16[64,3,768]{2,0,1:T(8,128)(2,1)}, u32[]{:S(2)}) copy-start(bf16[64,3,768]{2,0,1:T(8,128)(2,1)} %param.9) | copy-start | bytes 884740
  15.6 0.7 copy-start.7
  16.3 2.6 %copy-start.1 = (bf16[768,3,192]{0,2,1:T(8,128)(2,1)S(1)}, bf16[768,3,192]{0,2,1:T(8,128)(2,1)}, u32[]{:S(2)}) copy-start(bf16[768,3,192]{0,2,1:T(8,128)(2,1)} %param.13) | copy-start | bytes 2654212
  17.3 17.4 %copy-start.3 = (bf16[64,3,768]{2,0,1:T(8,128)(2,1)S(1)}, bf16[64,3,768]{2,0,1:T(8,128)(2,1)}, u32[]{:S(2)}) copy-start(bf16[64,3,768]{2,0,1:T(8,128)(2,1)} %param.9) | copy-start | bytes 884740
  17.3 17.4 %copy-start.9 = (f32[768]{0:T(1024)S(1)}, f32[768]{0:T(1024)}, u32[]{:S(2)}) copy-start(f32[768]{0:T(1024)} %gain_ref.5) | copy-start | bytes 9220
  17.3 7.6 %collective-permute-start.5 = (bf16[1,192,768]{2,1,0:T(8,128)(2,1)S(1)}, bf16[1,192,768]{2,1,0:T(8,128)(2,1)S(1)}, u32[]{:S(2)}, u32[]{:S(2)}) collective-permute-start(bf16[1,192,768]{2,1,0:T(8,128)(2,1)S(1)} %bitcast.24), channel_id=1, source_target_pairs={{0,1},{1,0},{2,3},{3,2},{4,6},{5,7},{6,4},{7,5},{8,9},{9,8},{10,11... | collective-permute-start | bytes 884744 | tf_op jit(solution)/shard_map/ppermute | solution.py:275
  18.5 10.8 %copy-start.12 = (bf16[768,3,192]{0,2,1:T(8,128)(2,1)S(1)}, bf16[768,3,192]{0,2,1:T(8,128)(2,1)}, u32[]{:S(2)}) copy-start(bf16[768,3,192]{0,2,1:T(8,128)(2,1)} %param.16) | copy-start | bytes 2654212
  18.5 6.4 %collective-permute-start.6 = (bf16[1,96,768]{2,1,0:T(8,128)(2,1)S(1)}, bf16[1,96,768]{2,1,0:T(8,128)(2,1)S(1)}, u32[]{:S(2)}, u32[]{:S(2)}) collective-permute-start(bf16[1,96,768]{2,1,0:T(8,128)(2,1)S(1)} %half.2), channel_id=1, source_target_pairs={{0,3},{1,2},{2,1},{3,0},{4,7},{5,6},{6,5},{7,4},{8,11},{9,10},{10,... | collective-permute-start | bytes 442376 | tf_op jit(solution)/shard_map/ppermute | solution.py:275
  21.4 19.5 %copy-start.6 = (bf16[192,768]{1,0:T(8,128)(2,1)S(1)}, bf16[192,768]{1,0:T(8,128)(2,1)}, u32[]{:S(2)}) copy-start(bf16[192,768]{1,0:T(8,128)(2,1)} %u0.1) | copy-start | bytes 884740
  21.5 5.9 %collective-permute-start.10 = (bf16[3,64,192]{2,1,0:T(8,128)(2,1)S(1)}, bf16[3,64,192]{2,1,0:T(8,128)(2,1)S(1)}, u32[]{:S(2)}, u32[]{:S(2)}) collective-permute-start(bf16[3,64,192]{2,1,0:T(8,128)(2,1)S(1)} %get-tuple-element.42), channel_id=1, source_target_pairs={{0,3},{1,2},{2,1},{3,0},{4,7},{5,6},{6,5},{7,4},{8,11},{9,10},{10,... | collective-permute-start | bytes 221192 | tf_op jit(solution)/shard_map/ppermute | solution.py:275
  23.5 5.6 %collective-permute-start.8 = (bf16[3,64,192]{2,1,0:T(8,128)(2,1)S(1)}, bf16[3,64,192]{2,1,0:T(8,128)(2,1)S(1)}, u32[]{:S(2)}, u32[]{:S(2)}) collective-permute-start(bf16[3,64,192]{2,1,0:T(8,128)(2,1)S(1)} %get-tuple-element.40), channel_id=1, source_target_pairs={{0,1},{1,0},{2,3},{3,2},{4,6},{5,7},{6,4},{7,5},{8,9},{9,8},{10,11... | collective-permute-start | bytes 221192 | tf_op jit(solution)/shard_map/ppermute | solution.py:275
  23.9 5.4 %collective-permute-start.9 = (bf16[3,64,192]{2,1,0:T(8,128)(2,1)S(1)}, bf16[3,64,192]{2,1,0:T(8,128)(2,1)S(1)}, u32[]{:S(2)}, u32[]{:S(2)}) collective-permute-start(bf16[3,64,192]{2,1,0:T(8,128)(2,1)S(1)} %get-tuple-element.41), channel_id=1, source_target_pairs={{0,2},{1,3},{2,0},{3,1},{4,5},{5,4},{6,7},{7,6},{8,10},{9,11},{10,... | collective-permute-start | bytes 221192 | tf_op jit(solution)/shard_map/ppermute | solution.py:275
  29.3 19.8 %collective-permute-start.11 = (bf16[3,192,768]{2,1,0:T(8,128)(2,1)S(1)}, bf16[3,192,768]{2,1,0:T(8,128)(2,1)S(1)}, u32[]{:S(2)}, u32[]{:S(2)}) collective-permute-start(bf16[3,192,768]{2,1,0:T(8,128)(2,1)S(1)} %bitcast.30), channel_id=1, source_target_pairs={{0,1},{1,0},{2,3},{3,2},{4,6},{5,7},{6,4},{7,5},{8,9},{9,8},{10,11... | collective-permute-start | bytes 2654216 | tf_op jit(solution)/shard_map/ppermute | solution.py:275
  29.9 4.8 %collective-permute-start.13 = (bf16[1,192,768]{2,1,0:T(8,128)(2,1)S(1)}, bf16[1,192,768]{2,1,0:T(8,128)(2,1)S(1)}, u32[]{:S(2)}, u32[]{:S(2)}) collective-permute-start(bf16[1,192,768]{2,1,0:T(8,128)(2,1)S(1)} %collective-permute-done.5.w1), channel_id=1, source_target_pairs={{0,4},{4,0},{8,12},{12,8},{16,20},{20,16},{24,28},{28,24},{1,5},{5... | collective-permute-start | bytes 884744 | tf_op jit(solution)/shard_map/ppermute | solution.py:278
  33.3 1.4 %collective-permute-start.14 = (bf16[1,96,768]{2,1,0:T(8,128)(2,1)S(1)}, bf16[1,96,768]{2,1,0:T(8,128)(2,1)S(1)}, u32[]{:S(2)}, u32[]{:S(2)}) collective-permute-start(bf16[1,96,768]{2,1,0:T(8,128)(2,1)S(1)} %collective-permute-done.6.wa), channel_id=1, source_target_pairs={{0,4},{4,0},{8,12},{12,8},{16,20},{20,16},{24,28},{28,24},{1,5},{5... | collective-permute-start | bytes 442376 | tf_op jit(solution)/shard_map/ppermute | solution.py:278
  35.9 6.2 %collective-permute-start.17 = (bf16[2,64,768]{2,1,0:T(8,128)(2,1)S(1)}, bf16[2,64,768]{2,1,0:T(8,128)(2,1)S(1)}, u32[]{:S(2)}, u32[]{:S(2)}) collective-permute-start(bf16[2,64,768]{2,1,0:T(8,128)(2,1)S(1)} %get-tuple-element.52), channel_id=1, source_target_pairs={{0,8},{4,12},{8,0},{12,4},{16,24},{20,28},{24,16},{28,20},{1,9},{5... | collective-permute-start | bytes 589832 | tf_op jit(solution)/shard_map/ppermute | solution.py:362
  36.0 12.5 %collective-permute-start.15 = (bf16[3,64,768]{2,1,0:T(8,128)(2,1)S(1)}, bf16[3,64,768]{2,1,0:T(8,128)(2,1)S(1)}, u32[]{:S(2)}, u32[]{:S(2)}) collective-permute-start(bf16[3,64,768]{2,1,0:T(8,128)(2,1)S(1)} %get-tuple-element.51.x0), channel_id=1, source_target_pairs={{0,4},{4,0},{8,12},{12,8},{16,20},{20,16},{24,28},{28,24},{1,5},{5... | collective-permute-start | bytes 884744 | tf_op jit(solution)/shard_map/ppermute | solution.py:278
  36.6 11.9 %collective-permute-start.16 = (bf16[3,64,768]{2,1,0:T(8,128)(2,1)S(1)}, bf16[3,64,768]{2,1,0:T(8,128)(2,1)S(1)}, u32[]{:S(2)}, u32[]{:S(2)}) collective-permute-start(bf16[3,64,768]{2,1,0:T(8,128)(2,1)S(1)} %get-tuple-element.51.x0), channel_id=1, source_target_pairs={{4,8},{8,4},{12,16},{16,12},{20,24},{24,20},{5,9},{9,5},{13,17},{1... | collective-permute-start | bytes 884744 | tf_op jit(solution)/shard_map/ppermute | solution.py:360
  41.0 8.1 %collective-permute-start.12 = (bf16[1,192,768]{2,1,0:T(8,128)(2,1)S(1)}, bf16[1,192,768]{2,1,0:T(8,128)(2,1)S(1)}, u32[]{:S(2)}, u32[]{:S(2)}) collective-permute-start(bf16[1,192,768]{2,1,0:T(8,128)(2,1)S(1)} %bitcast.25), channel_id=1, source_target_pairs={{0,1},{1,0},{2,3},{3,2},{4,6},{5,7},{6,4},{7,5},{8,9},{9,8},{10,11... | collective-permute-start | bytes 884744 | tf_op jit(solution)/shard_map/ppermute | solution.py:275
  42.1 6.4 %collective-permute-start.18 = (bf16[2,64,768]{2,1,0:T(8,128)(2,1)S(1)}, bf16[2,64,768]{2,1,0:T(8,128)(2,1)S(1)}, u32[]{:S(2)}, u32[]{:S(2)}) collective-permute-start(bf16[2,64,768]{2,1,0:T(8,128)(2,1)S(1)} %get-tuple-element.53), channel_id=1, source_target_pairs={{8,16},{12,20},{16,8},{20,12},{9,17},{13,21},{17,9},{21,13},{10,18... | collective-permute-start | bytes 589832 | tf_op jit(solution)/shard_map/ppermute | solution.py:363
  49.1 5.3 %copy-start.11 = (s32[24]{0:T(128)S(1)}, s32[24]{0:T(128)}, u32[]{:S(2)}) copy-start(s32[24]{0:T(128)} %ids_ref.3) | copy-start | bytes 292
  49.1 5.3 %collective-permute-start.20 = (bf16[3,192,768]{2,1,0:T(8,128)(2,1)S(1)}, bf16[3,192,768]{2,1,0:T(8,128)(2,1)S(1)}, u32[]{:S(2)}, u32[]{:S(2)}) collective-permute-start(bf16[3,192,768]{2,1,0:T(8,128)(2,1)S(1)} %collective-permute-done.11.refs_0_.refs_1_), channel_id=1, source_target_pairs={{0,4},{4,0},{8,12},{12,8},{16,20},{20,16},{24,28},{28,24},{1,5},{5... | collective-permute-start | bytes 2654216 | tf_op jit(solution)/shard_map/ppermute | solution.py:278
  53.2 9.1 %collective-permute-start.19 = (bf16[4,96,768]{2,1,0:T(8,128)(2,1)S(1)}, bf16[4,96,768]{2,1,0:T(8,128)(2,1)S(1)}, u32[]{:S(2)}, u32[]{:S(2)}) collective-permute-start(bf16[4,96,768]{2,1,0:T(8,128)(2,1)S(1)} %half.3), channel_id=1, source_target_pairs={{0,2},{1,3},{2,0},{3,1},{4,5},{5,4},{6,7},{7,6},{8,10},{9,11},{10,... | collective-permute-start | bytes 1769480 | tf_op jit(solution)/shard_map/ppermute | solution.py:275
  62.3 2.5 %collective-permute-start.21 = (bf16[4,96,768]{2,1,0:T(8,128)(2,1)S(1)}, bf16[4,96,768]{2,1,0:T(8,128)(2,1)S(1)}, u32[]{:S(2)}, u32[]{:S(2)}) collective-permute-start(bf16[4,96,768]{2,1,0:T(8,128)(2,1)S(1)} %collective-permute-done.19.refs_0_.ua), channel_id=1, source_target_pairs={{0,4},{4,0},{8,12},{12,8},{16,20},{20,16},{24,28},{28,24},{1,5},{5... | collective-permute-start | bytes 1769480 | tf_op jit(solution)/shard_map/ppermute | solution.py:278
  63.2 4.7 %collective-permute-start.22 = (bf16[1,192,768]{2,1,0:T(8,128)(2,1)S(1)}, bf16[1,192,768]{2,1,0:T(8,128)(2,1)S(1)}, u32[]{:S(2)}, u32[]{:S(2)}) collective-permute-start(bf16[1,192,768]{2,1,0:T(8,128)(2,1)S(1)} %collective-permute-done.12.refs_1_.u1), channel_id=1, source_target_pairs={{0,4},{4,0},{8,12},{12,8},{16,20},{20,16},{24,28},{28,24},{1,5},{5... | collective-permute-start | bytes 884744 | tf_op jit(solution)/shard_map/ppermute | solution.py:278

commit v3 on v2

--- a/solution.py
+++ b/solution.py
@@ -43,12 +43,12 @@
 
 
 def time_kernel(
-    base_ref, early_ref, t3, m0, m1, m2, m3, gain_ref, w_ref, o0, o1, o2, o3
+    base_ref, early_ref, t3, m0, m1, m2, m3, gain_ref, w_ref, o0, o2, o13
 ):
-    outs, masks = (o0, o1, o2, o3), (m0, m1, m2, m3)
+    masks = (m0, m1, m2, m3)
     var_count, rows, depth = t3.shape
     width = w_ref.shape[0] // 3
-    blocks = len(outs)
+    blocks = len(masks)
     total = rows * blocks
     gain = gain_ref[...]
     x = jnp.concatenate([normed(t3[v].astype(jnp.float32), gain) for v in range(var_count)], axis=0)
@@ -87,32 +87,35 @@
             mixed = jnp.dot(weights, values, preferred_element_type=jnp.float32) * share
             attended = jnp.where(mine, mixed, attended)
         attended = attended.astype(jnp.bfloat16)
-        for block, out in enumerate(outs):
-            out[v] = attended[block * rows : (block + 1) * rows]
+        places = (o0.at[v], o13.at[v], o2.at[v], o13.at[var_count + v])
+        for block, out in enumerate(places):
+            out[...] = attended[block * rows : (block + 1) * rows]
+
+
+def part_kernel(a2, got, w0, w1, out_ref):
+    var_count, rows, width = a2.shape
+    own = a2[...].reshape(var_count * rows, width)
+    other = got[var_count:].reshape(var_count * rows, width)
+    summed = jnp.dot(own, w0[...], preferred_element_type=jnp.float32)
+    summed = summed + jnp.dot(other, w1[0], preferred_element_type=jnp.float32)
+    out_ref[...] = summed.astype(jnp.bfloat16).reshape(out_ref.shape)
 
 
 def mid_kernel(
-    place_ref, a0, a1, a2, a3, w0, w1, w2, wa, wb, tok_ref, gain_ref,
-    mid_ref, x_ref, f1_ref, f2_ref, last,
+    place_ref, a0, got, w0, w1, part_ref, tok_ref, gain_ref, mid_ref, x_ref
 ):
-    half = wa.shape[1]
-    core = place_ref[0]
-    last[pl.ds(pl.multiple_of(core * half, 32), half), :] = wa[0]
-    last[pl.ds(pl.multiple_of((1 - core) * half, 32), half), :] = wb[0]
     var_count, rows, depth = tok_ref.shape
     width = a0.shape[2]
     gain = gain_ref[...]
-    summed = 0.0
-    for a, w in ((a0, w0), (a1, w1.at[0]), (a2, w2.at[0]), (a3, last)):
-        attended = a[...].reshape(var_count * rows, width)
-        summed = summed + jnp.dot(attended, w[...], preferred_element_type=jnp.float32)
+    own = a0[...].reshape(var_count * rows, width)
+    other = got[:var_count].reshape(var_count * rows, width)
+    summed = part_ref[...].astype(jnp.float32).reshape(var_count * rows, depth)
+    summed = summed + jnp.dot(own, w0[...], preferred_element_type=jnp.float32)
+    summed = summed + jnp.dot(other, w1[0], preferred_element_type=jnp.float32)
     mid = tok_ref[...].astype(jnp.float32).reshape(var_count * rows, depth) + summed
     mid = mid.astype(jnp.bfloat16)
     x_ref[...] = normed(mid.astype(jnp.float32), gain).reshape(tok_ref.shape)
     mid_ref[...] = mid.reshape(tok_ref.shape)
-    far = f1_ref.shape[0]
-    f1_ref[...] = x_ref[pl.ds(place_ref[1], far)]
-    f2_ref[...] = x_ref[pl.ds(place_ref[2], far)]
 
 
 def half_kernel(parts, place_ref, *refs):
@@ -148,12 +151,17 @@
     target[pl.ds(pl.multiple_of(at + (1 - core) * half, 32), half), :] = second[...]
 
 
-def window_kernel(place_ref, x0, xs, xo, f1, f2, xall):
-    var_count, far_count = x0.shape[0], f1.shape[0]
-    for block, x in enumerate((x0, xs, xo)):
-        xall[block * var_count : (block + 1) * var_count] = x[...]
-    xall[pl.ds(3 * var_count + place_ref[3] * far_count, far_count)] = f1[...]
-    xall[pl.ds(3 * var_count + place_ref[4] * far_count, far_count)] = f2[...]
+def window_kernel(place_ref, x0, xs, got1, got2, swapped1, swapped2, xall):
+    var_count = x0.shape[0]
+    core, up_first = place_ref[0], place_ref[1] == 1
+    xall[:var_count] = x0[...]
+    xall[var_count : 2 * var_count] = xs[...]
+    other_first = up_first == (core == 1)
+    xall[2 * var_count : 3 * var_count] = jnp.where(other_first, swapped1[...], swapped2[...])
+    at = 3 * var_count
+    xall[at : at + var_count - 1] = jnp.where(up_first, got2[1:], got1[1:])
+    at += var_count - 1
+    xall[at : at + var_count - 1] = jnp.where(up_first, got1[:-1], got2[:-1])
 
 
 def out_kernel(place_ref, before, att, u0, u1, u2, ua, ub, mid_ref, out_ref, uall):
@@ -186,7 +194,7 @@
                 wall[kind, group * width : (group + 1) * width, :] = weight[kind]
     heads = inner // HD
 
-    variate = place_ref[5] * var_count
+    variate = place_ref[2] * var_count
     starts = (0, (1 - 2 * core) * var_count, (2 * core - 1) * var_count)
     offsets = [start + u for start in starts for u in range(var_count)]
     offsets += [u - var_count - far_count for u in range(far_count)]
@@ -266,7 +274,7 @@
 ):
     var_size, patch_size = lax.axis_size("var"), lax.axis_size("patch")
     var_index, patch_index = lax.axis_index("var"), lax.axis_index("patch")
-    core, level = var_index % 2, (var_index // 2) % 2
+    core = var_index % 2
     both = ("var", "patch")
     first, second, third = routes(var_size, patch_size)
     swap = pairs_of(var_size, lambda i: i ^ 1)
@@ -314,13 +322,10 @@
         )(place, *blocks)
 
     far_count = var_count - 1
-    place = jnp.stack([
-        core, jnp.where(level == 0, 1, 0), jnp.where(level == 0, 0, 1),
-        jnp.where(level == 0, 1, 0), jnp.where(level == 0, 0, 1), var_index,
-    ]).astype(jnp.int32)
-    t_half = half_of(((0, 1),), time_out[None])
-    t_own, t_half, early = lax.optimization_barrier((time_out[None], t_half, early))
-    t1, ta = send(t_own, first), send(t_half, third)
+    level = (var_index // 2) % 2
+    place = jnp.stack([core, 1 - level, var_index]).astype(jnp.int32)
+    t_own, early = lax.optimization_barrier((time_out[None], early))
+    t1 = send(t_own, first)
 
     near, far_step = jnp.where(core == 0, 1, 2), jnp.where(core == 0, 2, 1)
     bases = jnp.stack(
@@ -329,53 +334,59 @@
     block = jax.ShapeDtypeStruct((var_count, rows, width), bf)
     att = pl.pallas_call(
         time_kernel,
-        out_shape=[block] * 4,
+        out_shape=[block, block, jax.ShapeDtypeStruct((2 * var_count, rows, width), bf)],
         in_specs=[SM] + [VM] * 8,
-        out_specs=[VM] * 4,
+        out_specs=[VM] * 3,
+        compiler_params=params(),
+        cost_estimate=cost(10_000_000_000, 1000),
+        name="time",
+    )(bases, early, tok3, mask, mask1, mask2, mask3, time_gain, weight)
+    att0, att2, att13 = att
+    got = send(att13, first)
+    s_qkv, s_out, got = lax.optimization_barrier((qkv_s, space_out[None], got))
+    whole = jax.ShapeDtypeStruct((var_count, rows, depth), jnp.bfloat16)
+    part = jax.ShapeDtypeStruct((far_count, rows, depth), jnp.bfloat16)
+    partial = pl.pallas_call(
+        part_kernel,
+        out_shape=whole,
+        in_specs=[VM] * 4,
+        out_specs=VM,
         compiler_params=params(),
         cost_estimate=cost(1000, 1000),
-        name="time",
-    )(bases, early, tok3, mask, mask1, mask2, mask3, time_gain, weight)
-    att0 = att[0]
-    att1, att3, att2 = send(att[1], first), send(att[3], third), send(att[2], second)
-    s_qkv, s_out, t1, ta, att1, att2, att3 = lax.optimization_barrier(
-        (qkv_s, space_out[None], t1, ta, att1, att2, att3)
-    )
-    t2, tb = partner(t1), partner(ta)
+        name="part",
+    )(att2, got, time_out, t1)
+    partial = send(partial, second)
     qkv1, u1 = send(s_qkv, first), send(s_out, first)
-
-    whole = jax.ShapeDtypeStruct((var_count, rows, depth), jnp.bfloat16)
-    part = jax.ShapeDtypeStruct((far_count, rows, depth), jnp.bfloat16)
-    mid, x_own, far1, far2 = pl.pallas_call(
+    mid, x_own = pl.pallas_call(
         mid_kernel,
-        out_shape=[whole, whole, part, part],
-        in_specs=[SM] + [VM] * 11,
-        out_specs=[VM] * 4,
-        scratch_shapes=[pltpu.VMEM((width, depth), bf)],
+        out_shape=[whole, whole],
+        in_specs=[SM] + [VM] * 7,
+        out_specs=[VM] * 2,
         compiler_params=params(),
         cost_estimate=cost(1000, 1000),
         name="mid",
-    )(place, att0, att1, att2, att3, time_out, t1, t2, ta, tb, tok, space_gain)
-
-    x_other = lax.ppermute(x_own, "var", pairs_of(var_size, lambda i: i + 1 if i % 2 else i - 1))
+    )(place, att0, got, time_out, t1, partial, tok, space_gain)
+
+    got1 = lax.ppermute(x_own, "var", pairs_of(var_size, lambda i: i ^ 2))
+    got2 = lax.ppermute(
+        x_own, "var", pairs_of(var_size, lambda i: i + 2 if (i // 2) % 2 else i - 2)
+    )
     x_swap = partner(x_own)
-    far1 = lax.ppermute(far1, "var", pairs_of(var_size, lambda i: i ^ 2))
-    far2 = lax.ppermute(
-        far2, "var", pairs_of(var_size, lambda i: i + 2 if (i // 2) % 2 else i - 2)
-    )
+    qkv1, u1, x_swap = lax.optimization_barrier((qkv1, u1, x_swap))
+    rest_a = send(half_of(((0, 3), (0, 1)), qkv1, u1), second)
+    swapped1, swapped2 = partner(got1), partner(got2)
     count = 3 * var_count + 2 * far_count
     own_rows = var_count * rows
     window = pl.pallas_call(
         window_kernel,
         out_shape=jax.ShapeDtypeStruct((count, rows, depth), bf),
-        in_specs=[SM] + [VM] * 5,
+        in_specs=[SM] + [VM] * 6,
         out_specs=VM,
         compiler_params=params(8),
         cost_estimate=cost(1000, 1000),
         name="window",
-    )(place, x_own, x_swap, x_other, far1, far2)
-    qkv1, u1, window = lax.optimization_barrier((qkv1, u1, window))
-    rest_a = send(half_of(((0, 3), (0, 1)), qkv1, u1), second)
+    )(place, x_own, x_swap, got1, got2, swapped1, swapped2)
+    qkv1, window = lax.optimization_barrier((qkv1, window))
     qkv2 = partner(qkv1)
 
     def attend(groups, *weights):

time: 70 us -> 68.1 us (0.973); the launches traced: 69.7 us -> 66.8 us
  waiting for transfers between devices: 20.3 us -> 17.7 us
  local copies, waits for them, and re-layouts: 3.9 us -> 2.85 us
    ppermute x6, starting transfers between devices: 8.06 us -> 14.5 us  [partner(): return lax.ppermute(block, 'var', swap)]
    ppermute x3 -> x2, starting transfers between devices: 7.69 us -> 3.28 us  [the longest x1 3.21 us: on_device(): lax.ppermute(x_own, 'var', pairs_of(var_size, lambda i: i + 2 if i // 2 %...]
    ppermute x3 -> x2, waiting for transfers between devices: 3.58 us -> 0.01 us  [the longest x1 0.01 us: on_device(): lax.ppermute(x_own, 'var', pairs_of(var_size, lambda i: i + 2 if i // 2 %...]
    ppermute x14 -> x12, waiting for transfers between devices: 13.1 us -> 14.9 us  [send(): return lax.ppermute(block, both, route)]
    ppermute x14 -> x12, starting transfers between devices: 12.4 us -> 11 us  [send(): return lax.ppermute(block, both, route)]
    unnamed x26 -> x20, local copies, waits for them, and re-layouts: 3.82 us -> 2.85 us
    ppermute x6, waiting for transfers between devices: 3.62 us -> 2.82 us  [partner(): return lax.ppermute(block, 'var', swap)]
    pallas_call x2 -> x1, Pallas kernels: 1.59 us -> 0.84 us  [half_of(): pl.pallas_call(functools.partial(half_kernel, parts), out_shape=jax.Shape...]
  transfers between devices with their start and end apart: 23 -> 20, of which waited for: 12 -> 8; matrix products, arithmetic and copies ran while one was open for 0% -> 0% of each run, Pallas kernels for 22% -> 22%
where the time goes in v3:
time: 68.1 us; the launch traced here: 66.8 us
  starting transfers between devices  28.7 us (42%)
  waiting for transfers between devices  17.7 us (26%)
  Pallas kernels  17.2 us (25%)
  local copies, waits for them, and re-layouts  2.85 us (4%)
    ppermute x12, waiting for transfers between devices, send(): return lax.ppermute(block, both, route)  14.9 us
    ppermute x6, starting transfers between devices, partner(): return lax.ppermute(block, 'var', swap)  14.5 us
    ppermute x12, starting transfers between devices, send(): return lax.ppermute(block, both, route)  11 us
    pallas_call x2, Pallas kernels, attend(): pl.pallas_call(functools.partial(space_kernel, groups == 1, var_count), o...  9.04 us
    ppermute x1, starting transfers between devices, on_device(): lax.ppermute(x_own, 'var', pairs_of(var_size, lambda i: i + 2 if i // 2 %...  3.21 us
    unnamed x20, local copies, waits for them, and re-layouts  2.85 us
    ppermute x6, waiting for transfers between devices, partner(): return lax.ppermute(block, 'var', swap)  2.82 us
    pallas_call x1, Pallas kernels, on_device(): pl.pallas_call(time_kernel, out_shape=[block, block, jax.ShapeDtypeStruct...  2.55 us
  transfers between devices with their start and end apart: 20, of which 8 were waited for; matrix products, arithmetic and copies ran while one was open for 0% of the time, Pallas kernels for 22%

profile of v3, /device:TPU:9, one launch (start us, length us, event | category | flops | bytes accessed | tf_op | source)
XLA Modules:
  0.0 66.8 jit_solution(14218358074881711464)
XLA Ops:
  0.0 1.2 %collective-permute-start = (bf16[3,64,768]{2,1,0:T(8,128)(2,1)}, bf16[3,64,768]{2,1,0:T(8,128)(2,1)S(1)}, u32[]{:S(2)}, u32[]{:S(2)}) collective-permute-start(bf16[3,64,768]{2,1,0:T(8,128)(2,1)} %bitcast.16), channel_id=1, source_target_pairs={{0,1},{1,0},{2,3},{3,2},{4,6},{5,7},{6,4},{7,5},{8,9},{9,8},{10,11... | collective-permute-start | bytes 884744 | tf_op jit(solution)/shard_map/ppermute | solution.py:283
  1.2 1.2 %collective-permute-start.3 = (s32[3,64]{1,0:T(4,128)}, s32[3,64]{1,0:T(4,128)S(1)}, u32[]{:S(2)}, u32[]{:S(2)}) collective-permute-start(s32[3,64]{1,0:T(4,128)} %bitcast.24), channel_id=1, source_target_pairs={{0,3},{1,2},{2,1},{3,0},{4,7},{5,6},{6,5},{7,4},{8,11},{9,10},{10,... | collective-permute-start | bytes 2312 | tf_op jit(solution)/shard_map/ppermute | solution.py:283
  2.4 0.3 collective-permute-start.2
  2.7 1.2 %collective-permute-start.1 = (s32[3,64]{1,0:T(4,128)}, s32[3,64]{1,0:T(4,128)S(1)}, u32[]{:S(2)}, u32[]{:S(2)}) collective-permute-start(s32[3,64]{1,0:T(4,128)} %bitcast.26), channel_id=1, source_target_pairs={{0,1},{1,0},{2,3},{3,2},{4,6},{5,7},{6,4},{7,5},{8,9},{9,8},{10,11... | collective-permute-start | bytes 2312 | tf_op jit(solution)/shard_map/ppermute | solution.py:283
  3.9 1.2 %collective-permute-start.4 = (bf16[3,64,768]{2,1,0:T(8,128)(2,1)}, bf16[3,64,768]{2,1,0:T(8,128)(2,1)S(1)}, u32[]{:S(2)}, u32[]{:S(2)}) collective-permute-start(bf16[3,64,768]{2,1,0:T(8,128)(2,1)} %bitcast.17), channel_id=1, source_target_pairs={{0,2},{1,3},{2,0},{3,1},{4,5},{5,4},{6,7},{7,6},{8,10},{9,11},{10,... | collective-permute-start | bytes 884744 | tf_op jit(solution)/shard_map/ppermute | solution.py:283
  5.1 0.0 collective-permute-done.3.m3
  5.1 0.3 collective-permute-done.2.m2
  5.4 0.7 %collective-permute-done.1.m1 = s32[3,64]{1,0:T(4,128)S(1)} collective-permute-done((s32[3,64]{1,0:T(4,128)}, s32[3,64]{1,0:T(4,128)S(1)}, u32[]{:S(2)}, u32[]{:S(2)}) %collective-permute-start.1) | collective-permute-done | bytes 800 | tf_op jit(solution)/shard_map/ppermute | solution.py:283
  6.1 0.0 collective-permute-done.t1
  6.1 1.2 %collective-permute-start.5 = (bf16[3,64,768]{2,1,0:T(8,128)(2,1)S(1)}, bf16[3,64,768]{2,1,0:T(8,128)(2,1)S(1)}, u32[]{:S(2)}, u32[]{:S(2)}) collective-permute-start(bf16[3,64,768]{2,1,0:T(8,128)(2,1)S(1)} %collective-permute-done.t1), channel_id=1, source_target_pairs={{0,2},{1,3},{2,0},{3,1},{4,5},{5,4},{6,7},{7,6},{8,10},{9,11},{10,... | collective-permute-start | bytes 884744 | tf_op jit(solution)/shard_map/ppermute | solution.py:283
  7.3 0.1 add_multiply_fusion.base_ref
  7.4 3.0 %collective-permute-done.4.t2 = bf16[3,64,768]{2,1,0:T(8,128)(2,1)S(1)} collective-permute-done((bf16[3,64,768]{2,1,0:T(8,128)(2,1)}, bf16[3,64,768]{2,1,0:T(8,128)(2,1)S(1)}, u32[]{:S(2)}, u32[]{:S(2)}) %collective-permute-start.4) | collective-permute-done | bytes 294944 | tf_op jit(solution)/shard_map/ppermute | solution.py:283
  10.5 1.0 %copy-done = bf16[64,3,768]{2,0,1:T(8,128)(2,1)S(1)} copy-done((bf16[64,3,768]{2,0,1:T(8,128)(2,1)S(1)}, bf16[64,3,768]{2,0,1:T(8,128)(2,1)}, u32[]{:S(2)}) %copy-start) | copy-done | bytes 294936
  11.4 1.2 %copy-done.3 = bf16[768,3,192]{0,2,1:T(8,128)(2,1)S(1)} copy-done((bf16[768,3,192]{0,2,1:T(8,128)(2,1)S(1)}, bf16[768,3,192]{0,2,1:T(8,128)(2,1)}, u32[]{:S(2)}) %copy-start.3) | copy-done | bytes 884760
  12.6 0.7 %copy-done.6 = f32[768]{0:T(1024)S(1)} copy-done((f32[768]{0:T(1024)S(1)}, f32[768]{0:T(1024)}, u32[]{:S(2)}) %copy-start.6) | copy-done | bytes 3096
  13.3 1.0 %project.1.early_ref = bf16[576,576]{1,0:T(8,128)(2,1)S(1)} custom-call(bf16[3,64,768]{2,1,0:T(8,128)(2,1)S(1)} %bitcast.18, bf16[3,64,768]{2,1,0:T(8,128)(2,1)S(1)} %collective-permute-done.t1, bf16[3,64,768]{2,1,0:T(8,128)(2,1)S(1)} %collective-permute-done.4.t2, f32[768]{0:T(1024)S(1)} %copy-done.6, bf16[576,768]{1,0:T(8,128)(2,1)S(1)} %bitcast.21), custom_call_target="tpu_custom_call" | custom-call | flops 1000 | bytes 1000 | tf_op jit(solution)/shard_map/project/pallas_call | solution.py:302
  14.3 0.0 copy-done.2
  14.3 0.0 copy-start.7
  14.3 1.3 %collective-permute-start.9 = (bf16[1,192,768]{2,1,0:T(8,128)(2,1)S(1)}, bf16[1,192,768]{2,1,0:T(8,128)(2,1)S(1)}, u32[]{:S(2)}, u32[]{:S(2)}) collective-permute-start(bf16[1,192,768]{2,1,0:T(8,128)(2,1)S(1)} %bitcast.20), channel_id=1, source_target_pairs={{0,1},{1,0},{2,3},{3,2},{4,6},{5,7},{6,4},{7,5},{8,9},{9,8},{10,11... | collective-permute-start | bytes 884744 | tf_op jit(solution)/shard_map/ppermute | solution.py:283
  15.6 0.0 collective-permute-done.5.t3
  15.6 0.0 copy-done.9
  15.6 0.0 copy-done.4
  15.6 2.5 %time.1 = (bf16[3,64,192]{2,1,0:T(8,128)(2,1)S(1)}, bf16[3,64,192]{2,1,0:T(8,128)(2,1)S(1)}, bf16[6,64,192]{2,1,0:T(8,128)(2,1)S(1)}) custom-call(s32[4]{0:T(128)S(1)} %add_multiply_fusion.base_ref, bf16[576,576]{1,0:T(8,128)(2,1)S(1)} %project.1.early_ref, bf16[3,64,768]{2,1,0:T(8,128)(2,1)S(1)} %collective-permute-done.5.t3, s32[3,64]{1,0:T(4,128)S(1)} %bitcast.27, ...), custom_call_target="tpu_custom_call" | custom-call | flops 10000000000 | bytes 1000 | tf_op jit(solution)/shard_map/time/pallas_call | solution.py:335
  18.2 0.0 copy-start.1
  18.2 0.3 collective-permute-start.6
  18.5 4.6 %collective-permute-done.6.got = bf16[6,64,192]{2,1,0:T(8,128)(2,1)S(1)} collective-permute-done((bf16[6,64,192]{2,1,0:T(8,128)(2,1)S(1)}, bf16[6,64,192]{2,1,0:T(8,128)(2,1)S(1)}, u32[]{:S(2)}, u32[]{:S(2)}) %collective-permute-start.6) | collective-permute-done | bytes 147488 | tf_op jit(solution)/shard_map/ppermute | solution.py:283
  23.1 0.0 collective-permute-done.9.w1
  23.1 0.3 part.1
  23.4 1.3 %collective-permute-start.10 = (bf16[3,64,768]{2,1,0:T(8,128)(2,1)S(1)}, bf16[3,64,768]{2,1,0:T(8,128)(2,1)S(1)}, u32[]{:S(2)}, u32[]{:S(2)}) collective-permute-start(bf16[3,64,768]{2,1,0:T(8,128)(2,1)S(1)} %part.1), channel_id=1, source_target_pairs={{0,2},{1,3},{2,0},{3,1},{4,5},{5,4},{6,7},{7,6},{8,10},{9,11},{10,... | collective-permute-start | bytes 884744 | tf_op jit(solution)/shard_map/ppermute | solution.py:283
  24.7 0.2 collective-permute-start.7
  24.9 0.1 pad_add_fusion.place_ref
  25.0 4.4 %collective-permute-done.10.part_ref = bf16[3,64,768]{2,1,0:T(8,128)(2,1)S(1)} collective-permute-done((bf16[3,64,768]{2,1,0:T(8,128)(2,1)S(1)}, bf16[3,64,768]{2,1,0:T(8,128)(2,1)S(1)}, u32[]{:S(2)}, u32[]{:S(2)}) %collective-permute-start.10) | collective-permute-done | bytes 294944 | tf_op jit(solution)/shard_map/ppermute | solution.py:283
  29.3 0.0 copy-done.7
  29.3 0.0 copy-done.1
  29.3 1.0 %mid.1 = (bf16[3,64,768]{2,1,0:T(8,128)(2,1)S(1)}, bf16[3,64,768]{2,1,0:T(8,128)(2,1)S(1)}) custom-call(s32[3]{0:T(128)S(1)} %pad_add_fusion.place_ref, bf16[3,64,192]{2,1,0:T(8,128)(2,1)S(1)} %get-tuple-element.35.a0, bf16[6,64,192]{2,1,0:T(8,128)(2,1)S(1)} %collective-permute-done.6.got, bf16[192,768]{1,0:T(8,128)(2,1)S(1)} %copy-done.2, ...), custom_call_target="tpu_custom_call" | custom-call | flops 1000 | bytes 1000 | tf_op jit(solution)/shard_map/mid/pallas_call | solution.py:360
  30.4 3.2 %collective-permute-start.14 = (bf16[3,64,768]{2,1,0:T(8,128)(2,1)S(1)}, bf16[3,64,768]{2,1,0:T(8,128)(2,1)S(1)}, u32[]{:S(2)}, u32[]{:S(2)}) collective-permute-start(bf16[3,64,768]{2,1,0:T(8,128)(2,1)S(1)} %get-tuple-element.39.x0), channel_id=1, source_target_pairs={{8,16},{12,20},{16,8},{20,12},{9,17},{13,21},{17,9},{21,13},{10,18... | collective-permute-start | bytes 884744 | tf_op jit(solution)/shard_map/ppermute | solution.py:371
  33.6 0.1 collective-permute-start.13
  33.7 0.0 copy-done.5
  33.7 0.3 collective-permute-start.8
  34.0 7.9 %collective-permute-start.11 = (bf16[3,64,768]{2,1,0:T(8,128)(2,1)S(1)}, bf16[3,64,768]{2,1,0:T(8,128)(2,1)S(1)}, u32[]{:S(2)}, u32[]{:S(2)}) collective-permute-start(bf16[3,64,768]{2,1,0:T(8,128)(2,1)S(1)} %get-tuple-element.39.x0), channel_id=1, source_target_pairs={{0,4},{4,0},{8,12},{12,8},{16,20},{20,16},{24,28},{28,24},{1,5},{5... | collective-permute-start | bytes 884744 | tf_op jit(solution)/shard_map/ppermute | solution.py:286
  41.9 0.0 collective-permute-done.14.got2
  41.9 3.5 %collective-permute-start.16 = (bf16[3,64,768]{2,1,0:T(8,128)(2,1)S(1)}, bf16[3,64,768]{2,1,0:T(8,128)(2,1)S(1)}, u32[]{:S(2)}, u32[]{:S(2)}) collective-permute-start(bf16[3,64,768]{2,1,0:T(8,128)(2,1)S(1)} %collective-permute-done.14.got2), channel_id=1, source_target_pairs={{0,4},{4,0},{8,12},{12,8},{16,20},{20,16},{24,28},{28,24},{1,5},{5... | collective-permute-start | bytes 884744 | tf_op jit(solution)/shard_map/ppermute | solution.py:286
  45.3 0.0 collective-permute-done.13.got1
  45.3 1.7 %collective-permute-start.15 = (bf16[3,64,768]{2,1,0:T(8,128)(2,1)S(1)}, bf16[3,64,768]{2,1,0:T(8,128)(2,1)S(1)}, u32[]{:S(2)}, u32[]{:S(2)}) collective-permute-start(bf16[3,64,768]{2,1,0:T(8,128)(2,1)S(1)} %collective-permute-done.13.got1), channel_id=1, source_target_pairs={{0,4},{4,0},{8,12},{12,8},{16,20},{20,16},{24,28},{28,24},{1,5},{5... | collective-permute-start | bytes 884744 | tf_op jit(solution)/shard_map/ppermute | solution.py:286
  47.0 0.0 collective-permute-done.8.refs_1_.u1
  47.0 0.0 collective-permute-done.11.xs
  47.0 0.0 collective-permute-done.7.refs_0_.refs_1_
  47.0 0.0 collective-permute-done.16.swapped2
  47.0 1.2 %collective-permute-done.15.swapped1 = bf16[3,64,768]{2,1,0:T(8,128)(2,1)S(1)} collective-permute-done((bf16[3,64,768]{2,1,0:T(8,128)(2,1)S(1)}, bf16[3,64,768]{2,1,0:T(8,128)(2,1)S(1)}, u32[]{:S(2)}, u32[]{:S(2)}) %collective-permute-start.15) | collective-permute-done | bytes 294944 | tf_op jit(solution)/shard_map/ppermute | solution.py:286
  48.2 0.6 window.1.xall
  48.9 0.0 copy-start.8
  48.9 0.4 collective-permute-start.17
  49.3 0.8 %half.1 = bf16[4,96,768]{2,1,0:T(8,128)(2,1)S(1)} custom-call(s32[3]{0:T(128)S(1)} %pad_add_fusion.place_ref, bf16[3,192,768]{2,1,0:T(8,128)(2,1)S(1)} %collective-permute-done.7.refs_0_.refs_1_, bf16[1,192,768]{2,1,0:T(8,128)(2,1)S(1)} %collective-permute-done.8.refs_1_.u1), custom_call_target="tpu_custom_call" | custom-call | flops 1000 | bytes 1000 | tf_op jit(solution)/shard_map/half/pallas_call | solution.py:313
  50.2 1.3 %collective-permute-start.12 = (bf16[4,96,768]{2,1,0:T(8,128)(2,1)S(1)}, bf16[4,96,768]{2,1,0:T(8,128)(2,1)S(1)}, u32[]{:S(2)}, u32[]{:S(2)}) collective-permute-start(bf16[4,96,768]{2,1,0:T(8,128)(2,1)S(1)} %half.1), channel_id=1, source_target_pairs={{0,2},{1,3},{2,0},{3,1},{4,5},{5,4},{6,7},{7,6},{8,10},{9,11},{10,... | collective-permute-start | bytes 1769480 | tf_op jit(solution)/shard_map/ppermute | solution.py:283
  51.5 0.0 collective-permute-done.17.refs_2_
  51.5 0.0 copy-done.8
  51.5 5.9 %space.1.before = bf16[192,576]{1,0:T(8,128)(2,1)S(1)} custom-call(s32[3]{0:T(128)S(1)} %pad_add_fusion.place_ref, s32[24]{0:T(128)S(1)} %copy-done.8, bf16[13,64,768]{2,1,0:T(8,128)(2,1)S(1)} %window.1.xall, bf16[3,192,768]{2,1,0:T(8,128)(2,1)} %bitcast.3.refs_0_, bf16[3,192,768]{2,1,0:T(8,128)(2,1)S(1)} %collective-permute-done.7.refs_0_.refs_1_, ...), custom_call_target="tpu_custom_call" | custom-call | flops 10000000000 | bytes 1000 | tf_op jit(solution)/shard_map/space/pallas_call | solution.py:394
  57.4 1.9 %collective-permute-done.12.refs_0_.ua = bf16[4,96,768]{2,1,0:T(8,128)(2,1)S(1)} collective-permute-done((bf16[4,96,768]{2,1,0:T(8,128)(2,1)S(1)}, bf16[4,96,768]{2,1,0:T(8,128)(2,1)S(1)}, u32[]{:S(2)}, u32[]{:S(2)}) %collective-permute-start.12) | collective-permute-done | bytes 589856 | tf_op jit(solution)/shard_map/ppermute | solution.py:283
  59.2 1.0 %collective-permute-start.18 = (bf16[4,96,768]{2,1,0:T(8,128)(2,1)S(1)}, bf16[4,96,768]{2,1,0:T(8,128)(2,1)S(1)}, u32[]{:S(2)}, u32[]{:S(2)}) collective-permute-start(bf16[4,96,768]{2,1,0:T(8,128)(2,1)S(1)} %collective-permute-done.12.refs_0_.ua), channel_id=1, source_target_pairs={{0,4},{4,0},{8,12},{12,8},{16,20},{20,16},{24,28},{28,24},{1,5},{5... | collective-permute-start | bytes 1769480 | tf_op jit(solution)/shard_map/ppermute | solution.py:286
  60.2 0.0 collective-permute-start.19
  60.2 1.6 %collective-permute-done.18.refs_1_.ub = bf16[4,96,768]{2,1,0:T(8,128)(2,1)S(1)} collective-permute-done((bf16[4,96,768]{2,1,0:T(8,128)(2,1)S(1)}, bf16[4,96,768]{2,1,0:T(8,128)(2,1)S(1)}, u32[]{:S(2)}, u32[]{:S(2)}) %collective-permute-start.18) | collective-permute-done | bytes 589856 | tf_op jit(solution)/shard_map/ppermute | solution.py:286
  61.9 3.1 %space_last.1.att = bf16[192,192]{1,0:T(8,128)(2,1)S(1)} custom-call(s32[3]{0:T(128)S(1)} %pad_add_fusion.place_ref, s32[24]{0:T(128)S(1)} %copy-done.8, bf16[13,64,768]{2,1,0:T(8,128)(2,1)S(1)} %window.1.xall, bf16[4,96,768]{2,1,0:T(8,128)(2,1)S(1)} %collective-permute-done.12.refs_0_.ua, bf16[4,96,768]{2,1,0:T(8,128)(2,1)S(1)} %collective-permute-done.18.refs_1_.ub), custom_call_target="tpu_custom_call" | custom-call | flops 1000 | bytes 1000 | tf_op jit(solution)/shard_map/space_last/pallas_call | solution.py:394
  65.0 0.0 collective-permute-done.19.u2
  65.0 1.8 %out.1 = bf16[3,64,768]{2,1,0:T(8,128)(2,1)} custom-call(s32[3]{0:T(128)S(1)} %pad_add_fusion.place_ref, bf16[192,576]{1,0:T(8,128)(2,1)S(1)} %space.1.before, bf16[192,192]{1,0:T(8,128)(2,1)S(1)} %space_last.1.att, bf16[192,768]{1,0:T(8,128)(2,1)S(1)} %copy-done.5, bf16[1,192,768]{2,1,0:T(8,128)(2,1)S(1)} %collective-permute-done.8.refs_1_.u1, ...), custom_call_target="tpu_custom_call" | custom-call | flops 1000 | bytes 1000 | tf_op jit(solution)/shard_map/out/pallas_call | solution.py:414
  (7 shorter events, 0.0 us)
Async XLA Ops:
  0.0 6.1 %collective-permute-start = (bf16[3,64,768]{2,1,0:T(8,128)(2,1)}, bf16[3,64,768]{2,1,0:T(8,128)(2,1)S(1)}, u32[]{:S(2)}, u32[]{:S(2)}) collective-permute-start(bf16[3,64,768]{2,1,0:T(8,128)(2,1)} %bitcast.16), channel_id=1, source_target_pairs={{0,1},{1,0},{2,3},{3,2},{4,6},{5,7},{6,4},{7,5},{8,9},{9,8},{10,11... | collective-permute-start | bytes 884744 | tf_op jit(solution)/shard_map/ppermute | solution.py:283
  1.2 3.9 %collective-permute-start.3 = (s32[3,64]{1,0:T(4,128)}, s32[3,64]{1,0:T(4,128)S(1)}, u32[]{:S(2)}, u32[]{:S(2)}) collective-permute-start(s32[3,64]{1,0:T(4,128)} %bitcast.24), channel_id=1, source_target_pairs={{0,3},{1,2},{2,1},{3,0},{4,7},{5,6},{6,5},{7,4},{8,11},{9,10},{10,... | collective-permute-start | bytes 2312 | tf_op jit(solution)/shard_map/ppermute | solution.py:283
  2.4 3.0 %collective-permute-start.2 = (s32[3,64]{1,0:T(4,128)}, s32[3,64]{1,0:T(4,128)S(1)}, u32[]{:S(2)}, u32[]{:S(2)}) collective-permute-start(s32[3,64]{1,0:T(4,128)} %bitcast.25), channel_id=1, source_target_pairs={{0,2},{1,3},{2,0},{3,1},{4,5},{5,4},{6,7},{7,6},{8,10},{9,11},{10,... | collective-permute-start | bytes 2312 | tf_op jit(solution)/shard_map/ppermute | solution.py:283
  2.7 3.5 %collective-permute-start.1 = (s32[3,64]{1,0:T(4,128)}, s32[3,64]{1,0:T(4,128)S(1)}, u32[]{:S(2)}, u32[]{:S(2)}) collective-permute-start(s32[3,64]{1,0:T(4,128)} %bitcast.26), channel_id=1, source_target_pairs={{0,1},{1,0},{2,3},{3,2},{4,6},{5,7},{6,4},{7,5},{8,9},{9,8},{10,11... | collective-permute-start | bytes 2312 | tf_op jit(solution)/shard_map/ppermute | solution.py:283
  3.9 6.6 %collective-permute-start.4 = (bf16[3,64,768]{2,1,0:T(8,128)(2,1)}, bf16[3,64,768]{2,1,0:T(8,128)(2,1)S(1)}, u32[]{:S(2)}, u32[]{:S(2)}) collective-permute-start(bf16[3,64,768]{2,1,0:T(8,128)(2,1)} %bitcast.17), channel_id=1, source_target_pairs={{0,2},{1,3},{2,0},{3,1},{4,5},{5,4},{6,7},{7,6},{8,10},{9,11},{10,... | collective-permute-start | bytes 884744 | tf_op jit(solution)/shard_map/ppermute | solution.py:283
  6.1 9.5 %collective-permute-start.5 = (bf16[3,64,768]{2,1,0:T(8,128)(2,1)S(1)}, bf16[3,64,768]{2,1,0:T(8,128)(2,1)S(1)}, u32[]{:S(2)}, u32[]{:S(2)}) collective-permute-start(bf16[3,64,768]{2,1,0:T(8,128)(2,1)S(1)} %collective-permute-done.t1), channel_id=1, source_target_pairs={{0,2},{1,3},{2,0},{3,1},{4,5},{5,4},{6,7},{7,6},{8,10},{9,11},{10,... | collective-permute-start | bytes 884744 | tf_op jit(solution)/shard_map/ppermute | solution.py:283
  7.3 8.3 %copy-start.9 = (s32[64,3]{0,1:T(4,128)S(1)}, s32[64,3]{0,1:T(4,128)}, u32[]{:S(2)}) copy-start(s32[64,3]{0,1:T(4,128)} %param.10) | copy-start | bytes 2308
  10.5 1.0 %copy-start = (bf16[64,3,768]{2,0,1:T(8,128)(2,1)S(1)}, bf16[64,3,768]{2,0,1:T(8,128)(2,1)}, u32[]{:S(2)}) copy-start(bf16[64,3,768]{2,0,1:T(8,128)(2,1)} %param.9) | copy-start | bytes 884740
  11.4 1.2 %copy-start.3 = (bf16[768,3,192]{0,2,1:T(8,128)(2,1)S(1)}, bf16[768,3,192]{0,2,1:T(8,128)(2,1)}, u32[]{:S(2)}) copy-start(bf16[768,3,192]{0,2,1:T(8,128)(2,1)} %param.13) | copy-start | bytes 2654212
  12.6 0.7 %copy-start.6 = (f32[768]{0:T(1024)S(1)}, f32[768]{0:T(1024)}, u32[]{:S(2)}) copy-start(f32[768]{0:T(1024)} %gain_ref.4) | copy-start | bytes 9220
  13.3 1.0 %copy-start.2 = (bf16[192,768]{1,0:T(8,128)(2,1)S(1)}, bf16[192,768]{1,0:T(8,128)(2,1)}, u32[]{:S(2)}) copy-start(bf16[192,768]{1,0:T(8,128)(2,1)} %w0.3) | copy-start | bytes 884740
  13.3 2.3 %copy-start.4 = (bf16[768,3,192]{0,2,1:T(8,128)(2,1)S(1)}, bf16[768,3,192]{0,2,1:T(8,128)(2,1)}, u32[]{:S(2)}) copy-start(bf16[768,3,192]{0,2,1:T(8,128)(2,1)} %param.13) | copy-start | bytes 2654212
  14.3 15.0 %copy-start.7 = (f32[768]{0:T(1024)S(1)}, f32[768]{0:T(1024)}, u32[]{:S(2)}) copy-start(f32[768]{0:T(1024)} %gain_ref.5) | copy-start | bytes 9220
  14.3 8.8 %collective-permute-start.9 = (bf16[1,192,768]{2,1,0:T(8,128)(2,1)S(1)}, bf16[1,192,768]{2,1,0:T(8,128)(2,1)S(1)}, u32[]{:S(2)}, u32[]{:S(2)}) collective-permute-start(bf16[1,192,768]{2,1,0:T(8,128)(2,1)S(1)} %bitcast.20), channel_id=1, source_target_pairs={{0,1},{1,0},{2,3},{3,2},{4,6},{5,7},{6,4},{7,5},{8,9},{9,8},{10,11... | collective-permute-start | bytes 884744 | tf_op jit(solution)/shard_map/ppermute | solution.py:283
  18.2 11.2 %copy-start.1 = (bf16[64,3,768]{2,0,1:T(8,128)(2,1)S(1)}, bf16[64,3,768]{2,0,1:T(8,128)(2,1)}, u32[]{:S(2)}) copy-start(bf16[64,3,768]{2,0,1:T(8,128)(2,1)} %param.9) | copy-start | bytes 884740
  18.2 4.9 %collective-permute-start.6 = (bf16[6,64,192]{2,1,0:T(8,128)(2,1)S(1)}, bf16[6,64,192]{2,1,0:T(8,128)(2,1)S(1)}, u32[]{:S(2)}, u32[]{:S(2)}) collective-permute-start(bf16[6,64,192]{2,1,0:T(8,128)(2,1)S(1)} %get-tuple-element.32), channel_id=1, source_target_pairs={{0,1},{1,0},{2,3},{3,2},{4,6},{5,7},{6,4},{7,5},{8,9},{9,8},{10,11... | collective-permute-start | bytes 442376 | tf_op jit(solution)/shard_map/ppermute | solution.py:283
  23.1 10.6 %copy-start.5 = (bf16[192,768]{1,0:T(8,128)(2,1)S(1)}, bf16[192,768]{1,0:T(8,128)(2,1)}, u32[]{:S(2)}) copy-start(bf16[192,768]{1,0:T(8,128)(2,1)} %u0.1) | copy-start | bytes 884740
  23.4 5.9 %collective-permute-start.10 = (bf16[3,64,768]{2,1,0:T(8,128)(2,1)S(1)}, bf16[3,64,768]{2,1,0:T(8,128)(2,1)S(1)}, u32[]{:S(2)}, u32[]{:S(2)}) collective-permute-start(bf16[3,64,768]{2,1,0:T(8,128)(2,1)S(1)} %part.1), channel_id=1, source_target_pairs={{0,2},{1,3},{2,0},{3,1},{4,5},{5,4},{6,7},{7,6},{8,10},{9,11},{10,... | collective-permute-start | bytes 884744 | tf_op jit(solution)/shard_map/ppermute | solution.py:283
  24.7 22.3 %collective-permute-start.7 = (bf16[3,192,768]{2,1,0:T(8,128)(2,1)}, bf16[3,192,768]{2,1,0:T(8,128)(2,1)S(1)}, u32[]{:S(2)}, u32[]{:S(2)}) collective-permute-start(bf16[3,192,768]{2,1,0:T(8,128)(2,1)} %bitcast.3.refs_0_), channel_id=1, source_target_pairs={{0,1},{1,0},{2,3},{3,2},{4,6},{5,7},{6,4},{7,5},{8,9},{9,8},{10,11... | collective-permute-start | bytes 2654216 | tf_op jit(solution)/shard_map/ppermute | solution.py:283
  30.4 11.5 %collective-permute-start.14 = (bf16[3,64,768]{2,1,0:T(8,128)(2,1)S(1)}, bf16[3,64,768]{2,1,0:T(8,128)(2,1)S(1)}, u32[]{:S(2)}, u32[]{:S(2)}) collective-permute-start(bf16[3,64,768]{2,1,0:T(8,128)(2,1)S(1)} %get-tuple-element.39.x0), channel_id=1, source_target_pairs={{8,16},{12,20},{16,8},{20,12},{9,17},{13,21},{17,9},{21,13},{10,18... | collective-permute-start | bytes 884744 | tf_op jit(solution)/shard_map/ppermute | solution.py:371
  33.6 11.8 %collective-permute-start.13 = (bf16[3,64,768]{2,1,0:T(8,128)(2,1)S(1)}, bf16[3,64,768]{2,1,0:T(8,128)(2,1)S(1)}, u32[]{:S(2)}, u32[]{:S(2)}) collective-permute-start(bf16[3,64,768]{2,1,0:T(8,128)(2,1)S(1)} %get-tuple-element.39.x0), channel_id=1, source_target_pairs={{0,8},{4,12},{8,0},{12,4},{16,24},{20,28},{24,16},{28,20},{1,9},{5... | collective-permute-start | bytes 884744 | tf_op jit(solution)/shard_map/ppermute | solution.py:370
  33.7 13.3 %collective-permute-start.8 = (bf16[1,192,768]{2,1,0:T(8,128)(2,1)S(1)}, bf16[1,192,768]{2,1,0:T(8,128)(2,1)S(1)}, u32[]{:S(2)}, u32[]{:S(2)}) collective-permute-start(bf16[1,192,768]{2,1,0:T(8,128)(2,1)S(1)} %bitcast.23), channel_id=1, source_target_pairs={{0,1},{1,0},{2,3},{3,2},{4,6},{5,7},{6,4},{7,5},{8,9},{9,8},{10,11... | collective-permute-start | bytes 884744 | tf_op jit(solution)/shard_map/ppermute | solution.py:283
  34.0 13.0 %collective-permute-start.11 = (bf16[3,64,768]{2,1,0:T(8,128)(2,1)S(1)}, bf16[3,64,768]{2,1,0:T(8,128)(2,1)S(1)}, u32[]{:S(2)}, u32[]{:S(2)}) collective-permute-start(bf16[3,64,768]{2,1,0:T(8,128)(2,1)S(1)} %get-tuple-element.39.x0), channel_id=1, source_target_pairs={{0,4},{4,0},{8,12},{12,8},{16,20},{20,16},{24,28},{28,24},{1,5},{5... | collective-permute-start | bytes 884744 | tf_op jit(solution)/shard_map/ppermute | solution.py:286
  41.9 5.1 %collective-permute-start.16 = (bf16[3,64,768]{2,1,0:T(8,128)(2,1)S(1)}, bf16[3,64,768]{2,1,0:T(8,128)(2,1)S(1)}, u32[]{:S(2)}, u32[]{:S(2)}) collective-permute-start(bf16[3,64,768]{2,1,0:T(8,128)(2,1)S(1)} %collective-permute-done.14.got2), channel_id=1, source_target_pairs={{0,4},{4,0},{8,12},{12,8},{16,20},{20,16},{24,28},{28,24},{1,5},{5... | collective-permute-start | bytes 884744 | tf_op jit(solution)/shard_map/ppermute | solution.py:286
  45.3 2.9 %collective-permute-start.15 = (bf16[3,64,768]{2,1,0:T(8,128)(2,1)S(1)}, bf16[3,64,768]{2,1,0:T(8,128)(2,1)S(1)}, u32[]{:S(2)}, u32[]{:S(2)}) collective-permute-start(bf16[3,64,768]{2,1,0:T(8,128)(2,1)S(1)} %collective-permute-done.13.got1), channel_id=1, source_target_pairs={{0,4},{4,0},{8,12},{12,8},{16,20},{20,16},{24,28},{28,24},{1,5},{5... | collective-permute-start | bytes 884744 | tf_op jit(solution)/shard_map/ppermute | solution.py:286
  48.9 2.6 %copy-start.8 = (s32[24]{0:T(128)S(1)}, s32[24]{0:T(128)}, u32[]{:S(2)}) copy-start(s32[24]{0:T(128)} %ids_ref.3) | copy-start | bytes 292
  48.9 2.6 %collective-permute-start.17 = (bf16[3,192,768]{2,1,0:T(8,128)(2,1)S(1)}, bf16[3,192,768]{2,1,0:T(8,128)(2,1)S(1)}, u32[]{:S(2)}, u32[]{:S(2)}) collective-permute-start(bf16[3,192,768]{2,1,0:T(8,128)(2,1)S(1)} %collective-permute-done.7.refs_0_.refs_1_), channel_id=1, source_target_pairs={{0,4},{4,0},{8,12},{12,8},{16,20},{20,16},{24,28},{28,24},{1,5},{5... | collective-permute-start | bytes 2654216 | tf_op jit(solution)/shard_map/ppermute | solution.py:286
  50.2 9.1 %collective-permute-start.12 = (bf16[4,96,768]{2,1,0:T(8,128)(2,1)S(1)}, bf16[4,96,768]{2,1,0:T(8,128)(2,1)S(1)}, u32[]{:S(2)}, u32[]{:S(2)}) collective-permute-start(bf16[4,96,768]{2,1,0:T(8,128)(2,1)S(1)} %half.1), channel_id=1, source_target_pairs={{0,2},{1,3},{2,0},{3,1},{4,5},{5,4},{6,7},{7,6},{8,10},{9,11},{10,... | collective-permute-start | bytes 1769480 | tf_op jit(solution)/shard_map/ppermute | solution.py:283
  59.2 2.6 %collective-permute-start.18 = (bf16[4,96,768]{2,1,0:T(8,128)(2,1)S(1)}, bf16[4,96,768]{2,1,0:T(8,128)(2,1)S(1)}, u32[]{:S(2)}, u32[]{:S(2)}) collective-permute-start(bf16[4,96,768]{2,1,0:T(8,128)(2,1)S(1)} %collective-permute-done.12.refs_0_.ua), channel_id=1, source_target_pairs={{0,4},{4,0},{8,12},{12,8},{16,20},{20,16},{24,28},{28,24},{1,5},{5... | collective-permute-start | bytes 1769480 | tf_op jit(solution)/shard_map/ppermute | solution.py:286
  60.2 4.8 %collective-permute-start.19 = (bf16[1,192,768]{2,1,0:T(8,128)(2,1)S(1)}, bf16[1,192,768]{2,1,0:T(8,128)(2,1)S(1)}, u32[]{:S(2)}, u32[]{:S(2)}) collective-permute-start(bf16[1,192,768]{2,1,0:T(8,128)(2,1)S(1)} %collective-permute-done.8.refs_1_.u1), channel_id=1, source_target_pairs={{0,4},{4,0},{8,12},{12,8},{16,20},{20,16},{24,28},{28,24},{1,5},{5... | collective-permute-start | bytes 884744 | tf_op jit(solution)/shard_map/ppermute | solution.py:286

commit v4 on v3

--- a/solution.py
+++ b/solution.py
@@ -118,17 +118,17 @@
     mid_ref[...] = mid.reshape(tok_ref.shape)
 
 
-def half_kernel(parts, place_ref, *refs):
-    *sources, out, sems = refs
-    half = out.shape[1]
-    at = pl.multiple_of(place_ref[0] * half, 32)
-    copies, kind = [], 0
-    for source, (low, high) in zip(sources, parts):
-        size = high - low
-        cut = source.at[low:high, pl.ds(at, half)]
-        copies.append(pltpu.make_async_copy(cut, out.at[kind : kind + size], sems.at[len(copies)]))
-        copies[-1].start()
-        kind += size
+def split_kernel(place_ref, qkv_hbm, u_hbm, mine_hbm, other_hbm, sems):
+    kinds, half, core = qkv_hbm.shape[0], mine_hbm.shape[1], place_ref[0]
+    copies = []
+    for target, index in ((mine_hbm, core), (other_hbm, 1 - core)):
+        at = pl.multiple_of(index * half, 32)
+        for source, part in (
+            (qkv_hbm.at[:, pl.ds(at, half)], target.at[:kinds]),
+            (u_hbm.at[pl.ds(at, half)], target.at[kinds]),
+        ):
+            copies.append(pltpu.make_async_copy(source, part, sems.at[len(copies)]))
+            copies[-1].start()
     for copy in copies:
         copy.wait()
 
@@ -164,34 +164,21 @@
     xall[at : at + var_count - 1] = jnp.where(up_first, got1[:-1], got2[:-1])
 
 
-def out_kernel(place_ref, before, att, u0, u1, u2, ua, ub, mid_ref, out_ref, uall):
-    width = u0.shape[0]
-    for group, u in enumerate((u0, u1.at[0], u2.at[0])):
-        uall[group * width : (group + 1) * width, :] = u[...]
-    join_halves(place_ref, ua.at[3], ub.at[3], uall, 3 * width)
-    summed, at = mid_ref[...].astype(jnp.float32).reshape(att.shape[0], -1), 0
-    for attended in (before, att):
-        size = attended.shape[1]
-        summed = summed + jnp.dot(
-            attended[...], uall[at : at + size, :], preferred_element_type=jnp.float32
-        )
-        at += size
-    out_ref[...] = summed.astype(jnp.bfloat16).reshape(out_ref.shape)
-
-
-def space_kernel(halves, var_count, place_ref, ids_ref, xall, *refs):
-    *weights, out_ref, wall, qbuf, kbuf, vbuf = refs
+def space_kernel(
+    var_count, place_ref, ids_ref, xall, own, u_own, c1, o1, c2, o2, c3, o3, mid_ref,
+    out_ref, wall, uall, qbuf, kbuf, vbuf, att,
+):
     count, rows, depth = xall.shape
     far_count = var_count - 1
     inner = wall.shape[1]
     core = place_ref[0]
-    for kind in range(3):
-        if halves:
-            join_halves(place_ref, weights[0].at[kind], weights[1].at[kind], wall.at[kind], 0)
-        else:
-            width = inner // len(weights)
-            for group, weight in enumerate(weights):
-                wall[kind, group * width : (group + 1) * width, :] = weight[kind]
+    width = u_own.shape[0]
+    for kind in range(4):
+        target = wall.at[kind] if kind < 3 else uall
+        target[:width, :] = own[kind] if kind < 3 else u_own[...]
+        join_halves(place_ref, c1.at[kind], o1.at[kind], target, width)
+        join_halves(place_ref, o2.at[kind], c2.at[kind], target, 2 * width)
+        join_halves(place_ref, c3.at[kind], o3.at[kind], target, 3 * width)
     heads = inner // HD
 
     variate = place_ref[2] * var_count
@@ -247,7 +234,10 @@
                 at = slice(w * rows, (w + 1) * rows)
                 term = each[at] * vbuf[at, :].astype(jnp.float32)
                 mixed = term if mixed is None else mixed + term
-        out_ref[u * rows : (u + 1) * rows, :] = mixed.astype(jnp.bfloat16)
+        att[u * rows : (u + 1) * rows, :] = mixed.astype(jnp.bfloat16)
+    summed = jnp.dot(att[...], uall[...], preferred_element_type=jnp.float32)
+    summed = summed + mid_ref[...].astype(jnp.float32).reshape(summed.shape)
+    out_ref[...] = summed.astype(jnp.bfloat16).reshape(out_ref.shape)
 
 
 def routes(var_size, patch_size):
@@ -309,23 +299,22 @@
         name="project",
     )(tok, tok1f, tok2, time_gain, weight)
 
-    def half_of(parts, *blocks, weight=1000):
-        return pl.pallas_call(
-            functools.partial(half_kernel, parts),
-            out_shape=jax.ShapeDtypeStruct((sum(b - a for a, b in parts), half, depth), bf),
-            in_specs=[SM] + [HB] * len(blocks),
-            out_specs=HB,
-            scratch_shapes=[pltpu.SemaphoreType.DMA((len(blocks),))],
-            compiler_params=params(1),
-            cost_estimate=cost(weight, 1000),
-            name="half",
-        )(place, *blocks)
-
     far_count = var_count - 1
     level = (var_index // 2) % 2
     place = jnp.stack([core, 1 - level, var_index]).astype(jnp.int32)
-    t_own, early = lax.optimization_barrier((time_out[None], early))
-    t1 = send(t_own, first)
+    piece = jax.ShapeDtypeStruct((kind + 1, half, depth), bf)
+    mine, other = pl.pallas_call(
+        split_kernel,
+        out_shape=[piece] * 2,
+        in_specs=[SM] + [HB] * 2,
+        out_specs=[HB] * 2,
+        scratch_shapes=[pltpu.SemaphoreType.DMA((4,))],
+        compiler_params=params(1),
+        cost_estimate=cost(1000, 1000),
+        name="split",
+    )(place, qkv_s, space_out)
+    t_own, mine, other, early = lax.optimization_barrier((time_out[None], mine, other, early))
+    t1, c1 = send(t_own, first), send(mine, second)
 
     near, far_step = jnp.where(core == 0, 1, 2), jnp.where(core == 0, 2, 1)
     bases = jnp.stack(
@@ -343,7 +332,6 @@
     )(bases, early, tok3, mask, mask1, mask2, mask3, time_gain, weight)
     att0, att2, att13 = att
     got = send(att13, first)
-    s_qkv, s_out, got = lax.optimization_barrier((qkv_s, space_out[None], got))
     whole = jax.ShapeDtypeStruct((var_count, rows, depth), jnp.bfloat16)
     part = jax.ShapeDtypeStruct((far_count, rows, depth), jnp.bfloat16)
     partial = pl.pallas_call(
@@ -356,7 +344,8 @@
         name="part",
     )(att2, got, time_out, t1)
     partial = send(partial, second)
-    qkv1, u1 = send(s_qkv, first), send(s_out, first)
+    other, partial = lax.optimization_barrier((other, partial))
+    o1 = send(other, second)
     mid, x_own = pl.pallas_call(
         mid_kernel,
         out_shape=[whole, whole],
@@ -372,9 +361,12 @@
         x_own, "var", pairs_of(var_size, lambda i: i + 2 if (i // 2) % 2 else i - 2)
     )
     x_swap = partner(x_own)
-    qkv1, u1, x_swap = lax.optimization_barrier((qkv1, u1, x_swap))
-    rest_a = send(half_of(((0, 3), (0, 1)), qkv1, u1), second)
+    c1f, _ = lax.optimization_barrier((c1, x_own))
+    c3 = send(c1f, first)
     swapped1, swapped2 = partner(got1), partner(got2)
+    c1, o1, got1, got2 = lax.optimization_barrier((c1, o1, got1, got2))
+    c2, o2 = partner(c1), partner(o1)
+    o3 = partner(c3)
     count = 3 * var_count + 2 * far_count
     own_rows = var_count * rows
     window = pl.pallas_call(
@@ -386,41 +378,24 @@
         cost_estimate=cost(1000, 1000),
         name="window",
     )(place, x_own, x_swap, got1, got2, swapped1, swapped2)
-    qkv1, window = lax.optimization_barrier((qkv1, window))
-    qkv2 = partner(qkv1)
-
-    def attend(groups, *weights):
-        inner = width * groups
-        return pl.pallas_call(
-            functools.partial(space_kernel, groups == 1, var_count),
-            out_shape=jax.ShapeDtypeStruct((own_rows, inner), bf),
-            in_specs=[SM] * 2 + [VM] * (1 + len(weights)),
-            out_specs=VM,
-            scratch_shapes=[
-                pltpu.VMEM((kind, inner, depth), bf),
-                pltpu.VMEM((own_rows, inner), bf),
-                pltpu.VMEM((count * rows, inner), bf),
-                pltpu.VMEM((count * rows, inner), bf),
-            ],
-            compiler_params=params(),
-            cost_estimate=cost(1000 if groups == 1 else SPACE_COST, 1000),
-            name="space_last" if groups == 1 else "space",
-        )(place, group_ids, window, *weights)
-
-    first_parts = attend(3, qkv_s, qkv1, qkv2)
-    rest_a, u1, first_parts = lax.optimization_barrier((rest_a, u1, first_parts))
-    rest_b, u2 = partner(rest_a), partner(u1)
-    last_part = attend(1, rest_a, rest_b)
+    inner = 4 * width
     out = pl.pallas_call(
-        out_kernel,
+        functools.partial(space_kernel, var_count),
         out_shape=whole,
-        in_specs=[SM] + [VM] * 8,
+        in_specs=[SM] * 2 + [VM] * 10,
         out_specs=VM,
-        scratch_shapes=[pltpu.VMEM((4 * width, depth), bf)],
-        compiler_params=params(),
-        cost_estimate=cost(1000, 1000),
-        name="out",
-    )(place, first_parts, last_part, space_out, u1, u2, rest_a, rest_b, mid)
+        scratch_shapes=[
+            pltpu.VMEM((kind, inner, depth), bf),
+            pltpu.VMEM((inner, depth), bf),
+            pltpu.VMEM((own_rows, inner), bf),
+            pltpu.VMEM((count * rows, inner), bf),
+            pltpu.VMEM((count * rows, inner), bf),
+            pltpu.VMEM((own_rows, inner), bf),
+        ],
+        compiler_params=params(28),
+        cost_estimate=cost(1000, 1000),
+        name="space",
+    )(place, group_ids, window, qkv_s, space_out, c1, o1, c2, o2, c3, o3, mid)
     return jnp.transpose(out, (1, 0, 2))
 
 

time: 68.1 us -> 64.6 us (0.949)
  waiting for transfers between devices: 17.7 us -> 14.9 us
  Pallas kernels: 17.2 us -> 15 us
  starting transfers between devices: 28.7 us -> 29.8 us
  local copies, waits for them, and re-layouts: 2.85 us -> 3.54 us
    ppermute x12, waiting for transfers between devices: 14.9 us -> 11.7 us  [send(): return lax.ppermute(block, both, route)]
    pallas_call x4 -> x2, Pallas kernels: 11.7 us -> 9.56 us  [the longest x1 8.42 us: on_device(): pl.pallas_call(functools.partial(space_kernel, var_count), out_shape=whol...]
    ppermute x12, starting transfers between devices: 11 us -> 12.6 us  [send(): return lax.ppermute(block, both, route)]
    unnamed x20 -> x30, local copies, waits for them, and re-layouts: 2.85 us -> 3.54 us
  transfers between devices with their start and end apart: 20 -> 20, of which waited for: 8 -> 7; matrix products, arithmetic and copies ran while one was open for 0% -> 0% of each run, Pallas kernels for 22% -> 10%
where the time goes in v4:
time: 64.6 us; the launch traced here: 63.6 us
  starting transfers between devices  29.8 us (46%)
  Pallas kernels  15 us (23%)
  waiting for transfers between devices  14.9 us (23%)
  local copies, waits for them, and re-layouts  3.54 us (5%)
    ppermute x6, starting transfers between devices, partner(): return lax.ppermute(block, 'var', swap)  14 us
    ppermute x12, starting transfers between devices, send(): return lax.ppermute(block, both, route)  12.6 us
    ppermute x12, waiting for transfers between devices, send(): return lax.ppermute(block, both, route)  11.7 us
    pallas_call x1, Pallas kernels, on_device(): pl.pallas_call(functools.partial(space_kernel, var_count), out_shape=whol...  8.42 us
    unnamed x30, local copies, waits for them, and re-layouts  3.54 us
    ppermute x1, starting transfers between devices, on_device(): lax.ppermute(x_own, 'var', pairs_of(var_size, lambda i: i + 2 if i // 2 %...  3.19 us
    ppermute x6, waiting for transfers between devices, partner(): return lax.ppermute(block, 'var', swap)  3.14 us
    pallas_call x1, Pallas kernels, on_device(): pl.pallas_call(time_kernel, out_shape=[block, block, jax.ShapeDtypeStruct...  2.53 us
  transfers between devices with their start and end apart: 20, of which 7 were waited for; matrix products, arithmetic and copies ran while one was open for 0% of the time, Pallas kernels for 10%

profile of v4, /device:TPU:9, one launch (start us, length us, event | category | flops | bytes accessed | tf_op | source)
XLA Modules:
  0.0 63.6 jit_solution(7637762334182524987)
XLA Ops:
  0.0 1.2 %collective-permute-start = (bf16[3,64,768]{2,1,0:T(8,128)(2,1)}, bf16[3,64,768]{2,1,0:T(8,128)(2,1)S(1)}, u32[]{:S(2)}, u32[]{:S(2)}) collective-permute-start(bf16[3,64,768]{2,1,0:T(8,128)(2,1)} %bitcast.17), channel_id=1, source_target_pairs={{0,1},{1,0},{2,3},{3,2},{4,6},{5,7},{6,4},{7,5},{8,9},{9,8},{10,11... | collective-permute-start | bytes 884744 | tf_op jit(solution)/shard_map/ppermute | solution.py:273
  1.2 1.2 %collective-permute-start.3 = (s32[3,64]{1,0:T(4,128)}, s32[3,64]{1,0:T(4,128)S(1)}, u32[]{:S(2)}, u32[]{:S(2)}) collective-permute-start(s32[3,64]{1,0:T(4,128)} %bitcast.24), channel_id=1, source_target_pairs={{0,3},{1,2},{2,1},{3,0},{4,7},{5,6},{6,5},{7,4},{8,11},{9,10},{10,... | collective-permute-start | bytes 2312 | tf_op jit(solution)/shard_map/ppermute | solution.py:273
  2.4 0.3 collective-permute-start.2
  2.7 1.2 %collective-permute-start.1 = (s32[3,64]{1,0:T(4,128)}, s32[3,64]{1,0:T(4,128)S(1)}, u32[]{:S(2)}, u32[]{:S(2)}) collective-permute-start(s32[3,64]{1,0:T(4,128)} %bitcast.26), channel_id=1, source_target_pairs={{0,1},{1,0},{2,3},{3,2},{4,6},{5,7},{6,4},{7,5},{8,9},{9,8},{10,11... | collective-permute-start | bytes 2312 | tf_op jit(solution)/shard_map/ppermute | solution.py:273
  3.9 1.2 %collective-permute-start.4 = (bf16[3,64,768]{2,1,0:T(8,128)(2,1)}, bf16[3,64,768]{2,1,0:T(8,128)(2,1)S(1)}, u32[]{:S(2)}, u32[]{:S(2)}) collective-permute-start(bf16[3,64,768]{2,1,0:T(8,128)(2,1)} %bitcast.18), channel_id=1, source_target_pairs={{0,2},{1,3},{2,0},{3,1},{4,5},{5,4},{6,7},{7,6},{8,10},{9,11},{10,... | collective-permute-start | bytes 884744 | tf_op jit(solution)/shard_map/ppermute | solution.py:273
  5.1 0.0 collective-permute-done.3.m3
  5.1 0.3 collective-permute-done.2.m2
  5.4 0.7 %collective-permute-done.1.m1 = s32[3,64]{1,0:T(4,128)S(1)} collective-permute-done((s32[3,64]{1,0:T(4,128)}, s32[3,64]{1,0:T(4,128)S(1)}, u32[]{:S(2)}, u32[]{:S(2)}) %collective-permute-start.1) | collective-permute-done | bytes 800 | tf_op jit(solution)/shard_map/ppermute | solution.py:273
  6.1 0.0 collective-permute-done.t1
  6.1 1.2 %collective-permute-start.5 = (bf16[3,64,768]{2,1,0:T(8,128)(2,1)S(1)}, bf16[3,64,768]{2,1,0:T(8,128)(2,1)S(1)}, u32[]{:S(2)}, u32[]{:S(2)}) collective-permute-start(bf16[3,64,768]{2,1,0:T(8,128)(2,1)S(1)} %collective-permute-done.t1), channel_id=1, source_target_pairs={{0,2},{1,3},{2,0},{3,1},{4,5},{5,4},{6,7},{7,6},{8,10},{9,11},{10,... | collective-permute-start | bytes 884744 | tf_op jit(solution)/shard_map/ppermute | solution.py:273
  7.3 0.1 pad_add_fusion.place_ref
  7.4 0.0 copy-done.13
  7.4 1.2 %copy-done = bf16[768,3,192]{0,2,1:T(8,128)(2,1)S(1)} copy-done((bf16[768,3,192]{0,2,1:T(8,128)(2,1)S(1)}, bf16[768,3,192]{0,2,1:T(8,128)(2,1)}, u32[]{:S(2)}) %copy-start) | copy-done | bytes 884760
  8.6 1.0 %copy-done.3 = bf16[192,768]{1,0:T(8,128)(2,1)S(1)} copy-done((bf16[192,768]{1,0:T(8,128)(2,1)S(1)}, bf16[192,768]{1,0:T(8,128)(2,1)}, u32[]{:S(2)}) %copy-start.3) | copy-done | bytes 294936
  9.6 1.1 %split.1 = (bf16[4,96,768]{2,1,0:T(8,128)(2,1)S(1)}, bf16[4,96,768]{2,1,0:T(8,128)(2,1)S(1)}) custom-call(s32[3]{0:T(128)S(1)} %pad_add_fusion.place_ref, bf16[3,192,768]{2,1,0:T(8,128)(2,1)S(1)} %bitcast.15, bf16[192,768]{1,0:T(8,128)(2,1)S(1)} %copy-done.3), custom_call_target="tpu_custom_call" | custom-call | flops 1000 | bytes 1000 | tf_op jit(solution)/shard_map/split/pallas_call | solution.py:306
  10.7 0.0 copy-start.5
  10.7 0.0 copy-start.10
  10.7 0.1 add_multiply_fusion.base_ref
  10.8 0.0 collective-permute-done.4.t2
  10.8 0.0 copy-done.7
  10.8 1.0 %project.1.early_ref = bf16[576,576]{1,0:T(8,128)(2,1)S(1)} custom-call(bf16[3,64,768]{2,1,0:T(8,128)(2,1)S(1)} %bitcast.19, bf16[3,64,768]{2,1,0:T(8,128)(2,1)S(1)} %collective-permute-done.t1, bf16[3,64,768]{2,1,0:T(8,128)(2,1)S(1)} %collective-permute-done.4.t2, f32[768]{0:T(1024)S(1)} %copy-done.7, bf16[576,768]{1,0:T(8,128)(2,1)S(1)} %bitcast.22), custom_call_target="tpu_custom_call" | custom-call | flops 1000 | bytes 1000 | tf_op jit(solution)/shard_map/project/pallas_call | solution.py:292
  11.8 0.0 copy-start.8
  11.9 1.3 %collective-permute-start.7 = (bf16[1,192,768]{2,1,0:T(8,128)(2,1)S(1)}, bf16[1,192,768]{2,1,0:T(8,128)(2,1)S(1)}, u32[]{:S(2)}, u32[]{:S(2)}) collective-permute-start(bf16[1,192,768]{2,1,0:T(8,128)(2,1)S(1)} %bitcast.21), channel_id=1, source_target_pairs={{0,1},{1,0},{2,3},{3,2},{4,6},{5,7},{6,4},{7,5},{8,9},{9,8},{10,11... | collective-permute-start | bytes 884744 | tf_op jit(solution)/shard_map/ppermute | solution.py:273
  13.2 0.8 %collective-permute-start.10 = (bf16[4,96,768]{2,1,0:T(8,128)(2,1)S(1)}, bf16[4,96,768]{2,1,0:T(8,128)(2,1)S(1)}, u32[]{:S(2)}, u32[]{:S(2)}) collective-permute-start(bf16[4,96,768]{2,1,0:T(8,128)(2,1)S(1)} %get-tuple-element.41), channel_id=1, source_target_pairs={{0,2},{1,3},{2,0},{3,1},{4,5},{5,4},{6,7},{7,6},{8,10},{9,11},{10,... | collective-permute-start | bytes 1769480 | tf_op jit(solution)/shard_map/ppermute | solution.py:273
  14.0 0.0 collective-permute-done.5.t3
  14.0 0.0 copy-done.10
  14.0 0.7 %copy-done.12 = s32[3,64]{1,0:T(4,128)S(1)} copy-done((s32[3,64]{1,0:T(4,128)S(1)}, s32[3,64]{1,0:T(4,128)}, u32[]{:S(2)}) %copy-start.12) | copy-done | bytes 792
  14.7 0.7 %copy-done.14 = s32[3,64]{1,0:T(4,128)S(1)} copy-done((s32[3,64]{1,0:T(4,128)S(1)}, s32[3,64]{1,0:T(4,128)}, u32[]{:S(2)}) %copy-start.14) | copy-done | bytes 792
  15.4 2.5 %time.1 = (bf16[3,64,192]{2,1,0:T(8,128)(2,1)S(1)}, bf16[3,64,192]{2,1,0:T(8,128)(2,1)S(1)}, bf16[6,64,192]{2,1,0:T(8,128)(2,1)S(1)}) custom-call(s32[4]{0:T(128)S(1)} %add_multiply_fusion.base_ref, bf16[576,576]{1,0:T(8,128)(2,1)S(1)} %project.1.early_ref, bf16[3,64,768]{2,1,0:T(8,128)(2,1)S(1)} %collective-permute-done.5.t3, s32[3,64]{1,0:T(4,128)S(1)} %bitcast.27, ...), custom_call_target="tpu_custom_call" | custom-call | flops 10000000000 | bytes 1000 | tf_op jit(solution)/shard_map/time/pallas_call | solution.py:324
  17.9 0.9 %collective-permute-start.6 = (bf16[6,64,192]{2,1,0:T(8,128)(2,1)S(1)}, bf16[6,64,192]{2,1,0:T(8,128)(2,1)S(1)}, u32[]{:S(2)}, u32[]{:S(2)}) collective-permute-start(bf16[6,64,192]{2,1,0:T(8,128)(2,1)S(1)} %get-tuple-element.35), channel_id=1, source_target_pairs={{0,1},{1,0},{2,3},{3,2},{4,6},{5,7},{6,4},{7,5},{8,9},{9,8},{10,11... | collective-permute-start | bytes 442376 | tf_op jit(solution)/shard_map/ppermute | solution.py:273
  18.8 0.8 %collective-permute-done.7.w1 = bf16[1,192,768]{2,1,0:T(8,128)(2,1)S(1)} collective-permute-done((bf16[1,192,768]{2,1,0:T(8,128)(2,1)S(1)}, bf16[1,192,768]{2,1,0:T(8,128)(2,1)S(1)}, u32[]{:S(2)}, u32[]{:S(2)}) %collective-permute-start.7) | collective-permute-done | bytes 294944 | tf_op jit(solution)/shard_map/ppermute | solution.py:273
  19.6 5.2 %collective-permute-done.6.got = bf16[6,64,192]{2,1,0:T(8,128)(2,1)S(1)} collective-permute-done((bf16[6,64,192]{2,1,0:T(8,128)(2,1)S(1)}, bf16[6,64,192]{2,1,0:T(8,128)(2,1)S(1)}, u32[]{:S(2)}, u32[]{:S(2)}) %collective-permute-start.6) | collective-permute-done | bytes 147488 | tf_op jit(solution)/shard_map/ppermute | solution.py:273
  24.9 0.3 part.1
  25.2 1.0 %collective-permute-start.8 = (bf16[3,64,768]{2,1,0:T(8,128)(2,1)S(1)}, bf16[3,64,768]{2,1,0:T(8,128)(2,1)S(1)}, u32[]{:S(2)}, u32[]{:S(2)}) collective-permute-start(bf16[3,64,768]{2,1,0:T(8,128)(2,1)S(1)} %part.1), channel_id=1, source_target_pairs={{0,2},{1,3},{2,0},{3,1},{4,5},{5,4},{6,7},{7,6},{8,10},{9,11},{10,... | collective-permute-start | bytes 884744 | tf_op jit(solution)/shard_map/ppermute | solution.py:273
  26.1 4.7 %collective-permute-done.8.part_ref = bf16[3,64,768]{2,1,0:T(8,128)(2,1)S(1)} collective-permute-done((bf16[3,64,768]{2,1,0:T(8,128)(2,1)S(1)}, bf16[3,64,768]{2,1,0:T(8,128)(2,1)S(1)}, u32[]{:S(2)}, u32[]{:S(2)}) %collective-permute-start.8) | collective-permute-done | bytes 294944 | tf_op jit(solution)/shard_map/ppermute | solution.py:273
  30.8 1.6 %collective-permute-start.11 = (bf16[4,96,768]{2,1,0:T(8,128)(2,1)S(1)}, bf16[4,96,768]{2,1,0:T(8,128)(2,1)S(1)}, u32[]{:S(2)}, u32[]{:S(2)}) collective-permute-start(bf16[4,96,768]{2,1,0:T(8,128)(2,1)S(1)} %get-tuple-element.42), channel_id=1, source_target_pairs={{0,2},{1,3},{2,0},{3,1},{4,5},{5,4},{6,7},{7,6},{8,10},{9,11},{10,... | collective-permute-start | bytes 1769480 | tf_op jit(solution)/shard_map/ppermute | solution.py:273
  32.4 1.0 %mid.1 = (bf16[3,64,768]{2,1,0:T(8,128)(2,1)S(1)}, bf16[3,64,768]{2,1,0:T(8,128)(2,1)S(1)}) custom-call(s32[3]{0:T(128)S(1)} %pad_add_fusion.place_ref, bf16[3,64,192]{2,1,0:T(8,128)(2,1)S(1)} %get-tuple-element.34.a0, bf16[6,64,192]{2,1,0:T(8,128)(2,1)S(1)} %collective-permute-done.6.got, bf16[192,768]{1,0:T(8,128)(2,1)S(1)} %copy-done.5, ...), custom_call_target="tpu_custom_call" | custom-call | flops 1000 | bytes 1000 | tf_op jit(solution)/shard_map/mid/pallas_call | solution.py:349
  33.5 0.0 collective-permute-done.10.c1
  33.5 0.0 copy-start.1
  33.5 0.0 copy-start.4
  33.5 0.0 copy-start.9
  33.5 0.6 collective-permute-start.18
  34.1 3.2 %collective-permute-start.13 = (bf16[3,64,768]{2,1,0:T(8,128)(2,1)S(1)}, bf16[3,64,768]{2,1,0:T(8,128)(2,1)S(1)}, u32[]{:S(2)}, u32[]{:S(2)}) collective-permute-start(bf16[3,64,768]{2,1,0:T(8,128)(2,1)S(1)} %get-tuple-element.40.x0), channel_id=1, source_target_pairs={{8,16},{12,20},{16,8},{20,12},{9,17},{13,21},{17,9},{21,13},{10,18... | collective-permute-start | bytes 884744 | tf_op jit(solution)/shard_map/ppermute | solution.py:360
  37.3 0.1 collective-permute-start.12
  37.4 6.3 %collective-permute-start.9 = (bf16[3,64,768]{2,1,0:T(8,128)(2,1)S(1)}, bf16[3,64,768]{2,1,0:T(8,128)(2,1)S(1)}, u32[]{:S(2)}, u32[]{:S(2)}) collective-permute-start(bf16[3,64,768]{2,1,0:T(8,128)(2,1)S(1)} %get-tuple-element.40.x0), channel_id=1, source_target_pairs={{0,4},{4,0},{8,12},{12,8},{16,20},{20,16},{24,28},{28,24},{1,5},{5... | collective-permute-start | bytes 884744 | tf_op jit(solution)/shard_map/ppermute | solution.py:276
  43.7 0.0 collective-permute-done.13.got2
  43.7 0.0 collective-permute-done.12.got1
  43.7 0.0 collective-permute-done.11.o1
  43.7 6.6 %collective-permute-start.16 = (bf16[4,96,768]{2,1,0:T(8,128)(2,1)S(1)}, bf16[4,96,768]{2,1,0:T(8,128)(2,1)S(1)}, u32[]{:S(2)}, u32[]{:S(2)}) collective-permute-start(bf16[4,96,768]{2,1,0:T(8,128)(2,1)S(1)} %collective-permute-done.10.c1), channel_id=1, source_target_pairs={{0,4},{4,0},{8,12},{12,8},{16,20},{20,16},{24,28},{28,24},{1,5},{5... | collective-permute-start | bytes 1769480 | tf_op jit(solution)/shard_map/ppermute | solution.py:276
  50.3 0.0 collective-permute-start.17
  50.3 0.0 collective-permute-done.18.c3
  50.3 0.5 collective-permute-start.19
  50.9 0.0 collective-permute-start.15
  50.9 0.0 collective-permute-done.9.xs
  50.9 0.5 collective-permute-start.14
  51.4 2.7 %collective-permute-done.15.swapped2 = bf16[3,64,768]{2,1,0:T(8,128)(2,1)S(1)} collective-permute-done((bf16[3,64,768]{2,1,0:T(8,128)(2,1)S(1)}, bf16[3,64,768]{2,1,0:T(8,128)(2,1)S(1)}, u32[]{:S(2)}, u32[]{:S(2)}) %collective-permute-start.15) | collective-permute-done | bytes 294944 | tf_op jit(solution)/shard_map/ppermute | solution.py:276
  54.1 0.4 collective-permute-done.14.swapped1
  54.5 0.6 %window.1.xall = bf16[13,64,768]{2,1,0:T(8,128)(2,1)S(1)} custom-call(s32[3]{0:T(128)S(1)} %pad_add_fusion.place_ref, bf16[3,64,768]{2,1,0:T(8,128)(2,1)S(1)} %get-tuple-element.40.x0, bf16[3,64,768]{2,1,0:T(8,128)(2,1)S(1)} %collective-permute-done.9.xs, bf16[3,64,768]{2,1,0:T(8,128)(2,1)S(1)} %collective-permute-done.12.got1, ...), custom_call_target="tpu_custom_call" | custom-call | flops 1000 | bytes 1000 | tf_op jit(solution)/shard_map/window/pallas_call | solution.py:372
  55.1 0.0 collective-permute-done.16.c2
  55.2 0.0 collective-permute-done.17.o2
  55.2 0.0 collective-permute-done.19.o3
  55.2 0.0 copy-done.1
  55.2 0.0 copy-done.4
  55.2 8.4 %space.1 = bf16[3,64,768]{2,1,0:T(8,128)(2,1)} custom-call(s32[3]{0:T(128)S(1)} %pad_add_fusion.place_ref, s32[24]{0:T(128)S(1)} %copy-done.9, bf16[13,64,768]{2,1,0:T(8,128)(2,1)S(1)} %window.1.xall, bf16[3,192,768]{2,1,0:T(8,128)(2,1)S(1)} %bitcast.16, bf16[192,768]{1,0:T(8,128)(2,1)S(1)} %copy-done.4, bf16[4,96,768]{2,1,0:T(8,128)(2,1)S(1)} %collective-permute-done.10.c1, ...), custom_call_target="tpu_custom_call" | custom-call | flops 1000 | bytes 1000 | tf_op jit(solution)/shard_map/space/pallas_call | solution.py:382
  (15 shorter events, 0.0 us)
Async XLA Ops:
  0.0 10.8 %copy-start.7 = (f32[768]{0:T(1024)S(1)}, f32[768]{0:T(1024)}, u32[]{:S(2)}) copy-start(f32[768]{0:T(1024)} %gain_ref.4) | copy-start | bytes 9220
  0.0 6.1 %collective-permute-start = (bf16[3,64,768]{2,1,0:T(8,128)(2,1)}, bf16[3,64,768]{2,1,0:T(8,128)(2,1)S(1)}, u32[]{:S(2)}, u32[]{:S(2)}) collective-permute-start(bf16[3,64,768]{2,1,0:T(8,128)(2,1)} %bitcast.17), channel_id=1, source_target_pairs={{0,1},{1,0},{2,3},{3,2},{4,6},{5,7},{6,4},{7,5},{8,9},{9,8},{10,11... | collective-permute-start | bytes 884744 | tf_op jit(solution)/shard_map/ppermute | solution.py:273
  1.2 3.9 %collective-permute-start.3 = (s32[3,64]{1,0:T(4,128)}, s32[3,64]{1,0:T(4,128)S(1)}, u32[]{:S(2)}, u32[]{:S(2)}) collective-permute-start(s32[3,64]{1,0:T(4,128)} %bitcast.24), channel_id=1, source_target_pairs={{0,3},{1,2},{2,1},{3,0},{4,7},{5,6},{6,5},{7,4},{8,11},{9,10},{10,... | collective-permute-start | bytes 2312 | tf_op jit(solution)/shard_map/ppermute | solution.py:273
  2.4 3.0 %collective-permute-start.2 = (s32[3,64]{1,0:T(4,128)}, s32[3,64]{1,0:T(4,128)S(1)}, u32[]{:S(2)}, u32[]{:S(2)}) collective-permute-start(s32[3,64]{1,0:T(4,128)} %bitcast.25), channel_id=1, source_target_pairs={{0,2},{1,3},{2,0},{3,1},{4,5},{5,4},{6,7},{7,6},{8,10},{9,11},{10,... | collective-permute-start | bytes 2312 | tf_op jit(solution)/shard_map/ppermute | solution.py:273
  2.7 3.5 %collective-permute-start.1 = (s32[3,64]{1,0:T(4,128)}, s32[3,64]{1,0:T(4,128)S(1)}, u32[]{:S(2)}, u32[]{:S(2)}) collective-permute-start(s32[3,64]{1,0:T(4,128)} %bitcast.26), channel_id=1, source_target_pairs={{0,1},{1,0},{2,3},{3,2},{4,6},{5,7},{6,4},{7,5},{8,9},{9,8},{10,11... | collective-permute-start | bytes 2312 | tf_op jit(solution)/shard_map/ppermute | solution.py:273
  3.9 6.9 %collective-permute-start.4 = (bf16[3,64,768]{2,1,0:T(8,128)(2,1)}, bf16[3,64,768]{2,1,0:T(8,128)(2,1)S(1)}, u32[]{:S(2)}, u32[]{:S(2)}) collective-permute-start(bf16[3,64,768]{2,1,0:T(8,128)(2,1)} %bitcast.18), channel_id=1, source_target_pairs={{0,2},{1,3},{2,0},{3,1},{4,5},{5,4},{6,7},{7,6},{8,10},{9,11},{10,... | collective-permute-start | bytes 884744 | tf_op jit(solution)/shard_map/ppermute | solution.py:273
  5.4 2.0 %copy-start.11 = (s32[3,64]{1,0:T(4,128)}, s32[3,64]{1,0:T(4,128)S(1)}, u32[]{:S(2)}) copy-start(s32[3,64]{1,0:T(4,128)S(1)} %collective-permute-done.2.m2) | copy-start | bytes 2308
  6.1 1.3 %copy-start.13 = (s32[3,64]{1,0:T(4,128)}, s32[3,64]{1,0:T(4,128)S(1)}, u32[]{:S(2)}) copy-start(s32[3,64]{1,0:T(4,128)S(1)} %collective-permute-done.1.m1) | copy-start | bytes 2308
  6.1 7.9 %collective-permute-start.5 = (bf16[3,64,768]{2,1,0:T(8,128)(2,1)S(1)}, bf16[3,64,768]{2,1,0:T(8,128)(2,1)S(1)}, u32[]{:S(2)}, u32[]{:S(2)}) collective-permute-start(bf16[3,64,768]{2,1,0:T(8,128)(2,1)S(1)} %collective-permute-done.t1), channel_id=1, source_target_pairs={{0,2},{1,3},{2,0},{3,1},{4,5},{5,4},{6,7},{7,6},{8,10},{9,11},{10,... | collective-permute-start | bytes 884744 | tf_op jit(solution)/shard_map/ppermute | solution.py:273
  7.4 1.2 %copy-start = (bf16[768,3,192]{0,2,1:T(8,128)(2,1)S(1)}, bf16[768,3,192]{0,2,1:T(8,128)(2,1)}, u32[]{:S(2)}) copy-start(bf16[768,3,192]{0,2,1:T(8,128)(2,1)} %param.16) | copy-start | bytes 2654212
  8.6 1.0 %copy-start.3 = (bf16[192,768]{1,0:T(8,128)(2,1)S(1)}, bf16[192,768]{1,0:T(8,128)(2,1)}, u32[]{:S(2)}) copy-start(bf16[192,768]{1,0:T(8,128)(2,1)} %u_own.1) | copy-start | bytes 884740
  9.6 1.3 %copy-start.2 = (bf16[64,3,768]{2,0,1:T(8,128)(2,1)S(1)}, bf16[64,3,768]{2,0,1:T(8,128)(2,1)}, u32[]{:S(2)}) copy-start(bf16[64,3,768]{2,0,1:T(8,128)(2,1)} %param.9) | copy-start | bytes 884740
  9.6 1.3 %copy-start.6 = (bf16[768,3,192]{0,2,1:T(8,128)(2,1)S(1)}, bf16[768,3,192]{0,2,1:T(8,128)(2,1)}, u32[]{:S(2)}) copy-start(bf16[768,3,192]{0,2,1:T(8,128)(2,1)} %param.13) | copy-start | bytes 2654212
  10.7 1.1 %copy-start.5 = (bf16[192,768]{1,0:T(8,128)(2,1)S(1)}, bf16[192,768]{1,0:T(8,128)(2,1)}, u32[]{:S(2)}) copy-start(bf16[192,768]{1,0:T(8,128)(2,1)} %w0.3) | copy-start | bytes 884740
  10.7 3.3 %copy-start.10 = (s32[64,3]{0,1:T(4,128)S(1)}, s32[64,3]{0,1:T(4,128)}, u32[]{:S(2)}) copy-start(s32[64,3]{0,1:T(4,128)} %param.10) | copy-start | bytes 2308
  11.8 20.6 %copy-start.8 = (f32[768]{0:T(1024)S(1)}, f32[768]{0:T(1024)}, u32[]{:S(2)}) copy-start(f32[768]{0:T(1024)} %gain_ref.5) | copy-start | bytes 9220
  11.9 7.8 %collective-permute-start.7 = (bf16[1,192,768]{2,1,0:T(8,128)(2,1)S(1)}, bf16[1,192,768]{2,1,0:T(8,128)(2,1)S(1)}, u32[]{:S(2)}, u32[]{:S(2)}) collective-permute-start(bf16[1,192,768]{2,1,0:T(8,128)(2,1)S(1)} %bitcast.21), channel_id=1, source_target_pairs={{0,1},{1,0},{2,3},{3,2},{4,6},{5,7},{6,4},{7,5},{8,9},{9,8},{10,11... | collective-permute-start | bytes 884744 | tf_op jit(solution)/shard_map/ppermute | solution.py:273
  13.2 20.3 %collective-permute-start.10 = (bf16[4,96,768]{2,1,0:T(8,128)(2,1)S(1)}, bf16[4,96,768]{2,1,0:T(8,128)(2,1)S(1)}, u32[]{:S(2)}, u32[]{:S(2)}) collective-permute-start(bf16[4,96,768]{2,1,0:T(8,128)(2,1)S(1)} %get-tuple-element.41), channel_id=1, source_target_pairs={{0,2},{1,3},{2,0},{3,1},{4,5},{5,4},{6,7},{7,6},{8,10},{9,11},{10,... | collective-permute-start | bytes 1769480 | tf_op jit(solution)/shard_map/ppermute | solution.py:273
  14.0 0.7 %copy-start.12 = (s32[3,64]{1,0:T(4,128)S(1)}, s32[3,64]{1,0:T(4,128)}, u32[]{:S(2)}) copy-start(s32[3,64]{1,0:T(4,128)} %copy-done.11) | copy-start | bytes 2308
  14.7 0.7 %copy-start.14 = (s32[3,64]{1,0:T(4,128)S(1)}, s32[3,64]{1,0:T(4,128)}, u32[]{:S(2)}) copy-start(s32[3,64]{1,0:T(4,128)} %copy-done.13) | copy-start | bytes 2308
  17.9 7.0 %collective-permute-start.6 = (bf16[6,64,192]{2,1,0:T(8,128)(2,1)S(1)}, bf16[6,64,192]{2,1,0:T(8,128)(2,1)S(1)}, u32[]{:S(2)}, u32[]{:S(2)}) collective-permute-start(bf16[6,64,192]{2,1,0:T(8,128)(2,1)S(1)} %get-tuple-element.35), channel_id=1, source_target_pairs={{0,1},{1,0},{2,3},{3,2},{4,6},{5,7},{6,4},{7,5},{8,9},{9,8},{10,11... | collective-permute-start | bytes 442376 | tf_op jit(solution)/shard_map/ppermute | solution.py:273
  25.2 5.6 %collective-permute-start.8 = (bf16[3,64,768]{2,1,0:T(8,128)(2,1)S(1)}, bf16[3,64,768]{2,1,0:T(8,128)(2,1)S(1)}, u32[]{:S(2)}, u32[]{:S(2)}) collective-permute-start(bf16[3,64,768]{2,1,0:T(8,128)(2,1)S(1)} %part.1), channel_id=1, source_target_pairs={{0,2},{1,3},{2,0},{3,1},{4,5},{5,4},{6,7},{7,6},{8,10},{9,11},{10,... | collective-permute-start | bytes 884744 | tf_op jit(solution)/shard_map/ppermute | solution.py:273
  30.8 12.9 %collective-permute-start.11 = (bf16[4,96,768]{2,1,0:T(8,128)(2,1)S(1)}, bf16[4,96,768]{2,1,0:T(8,128)(2,1)S(1)}, u32[]{:S(2)}, u32[]{:S(2)}) collective-permute-start(bf16[4,96,768]{2,1,0:T(8,128)(2,1)S(1)} %get-tuple-element.42), channel_id=1, source_target_pairs={{0,2},{1,3},{2,0},{3,1},{4,5},{5,4},{6,7},{7,6},{8,10},{9,11},{10,... | collective-permute-start | bytes 1769480 | tf_op jit(solution)/shard_map/ppermute | solution.py:273
  33.5 21.7 %copy-start.1 = (bf16[768,3,192]{0,2,1:T(8,128)(2,1)S(1)}, bf16[768,3,192]{0,2,1:T(8,128)(2,1)}, u32[]{:S(2)}) copy-start(bf16[768,3,192]{0,2,1:T(8,128)(2,1)} %param.16) | copy-start | bytes 2654212
  33.5 21.7 %copy-start.4 = (bf16[192,768]{1,0:T(8,128)(2,1)S(1)}, bf16[192,768]{1,0:T(8,128)(2,1)}, u32[]{:S(2)}) copy-start(bf16[192,768]{1,0:T(8,128)(2,1)} %u_own.1) | copy-start | bytes 884740
  33.5 21.7 %copy-start.9 = (s32[24]{0:T(128)S(1)}, s32[24]{0:T(128)}, u32[]{:S(2)}) copy-start(s32[24]{0:T(128)} %ids_ref.1) | copy-start | bytes 292
  33.5 16.8 %collective-permute-start.18 = (bf16[4,96,768]{2,1,0:T(8,128)(2,1)S(1)}, bf16[4,96,768]{2,1,0:T(8,128)(2,1)S(1)}, u32[]{:S(2)}, u32[]{:S(2)}) collective-permute-start(bf16[4,96,768]{2,1,0:T(8,128)(2,1)S(1)} %collective-permute-done.10.c1), channel_id=1, source_target_pairs={{0,1},{1,0},{2,3},{3,2},{4,6},{5,7},{6,4},{7,5},{8,9},{9,8},{10,11... | collective-permute-start | bytes 1769480 | tf_op jit(solution)/shard_map/ppermute | solution.py:273
  34.1 9.6 %collective-permute-start.13 = (bf16[3,64,768]{2,1,0:T(8,128)(2,1)S(1)}, bf16[3,64,768]{2,1,0:T(8,128)(2,1)S(1)}, u32[]{:S(2)}, u32[]{:S(2)}) collective-permute-start(bf16[3,64,768]{2,1,0:T(8,128)(2,1)S(1)} %get-tuple-element.40.x0), channel_id=1, source_target_pairs={{8,16},{12,20},{16,8},{20,12},{9,17},{13,21},{17,9},{21,13},{10,18... | collective-permute-start | bytes 884744 | tf_op jit(solution)/shard_map/ppermute | solution.py:360
  37.3 6.4 %collective-permute-start.12 = (bf16[3,64,768]{2,1,0:T(8,128)(2,1)S(1)}, bf16[3,64,768]{2,1,0:T(8,128)(2,1)S(1)}, u32[]{:S(2)}, u32[]{:S(2)}) collective-permute-start(bf16[3,64,768]{2,1,0:T(8,128)(2,1)S(1)} %get-tuple-element.40.x0), channel_id=1, source_target_pairs={{0,8},{4,12},{8,0},{12,4},{16,24},{20,28},{24,16},{28,20},{1,9},{5... | collective-permute-start | bytes 884744 | tf_op jit(solution)/shard_map/ppermute | solution.py:359
  37.4 13.5 %collective-permute-start.9 = (bf16[3,64,768]{2,1,0:T(8,128)(2,1)S(1)}, bf16[3,64,768]{2,1,0:T(8,128)(2,1)S(1)}, u32[]{:S(2)}, u32[]{:S(2)}) collective-permute-start(bf16[3,64,768]{2,1,0:T(8,128)(2,1)S(1)} %get-tuple-element.40.x0), channel_id=1, source_target_pairs={{0,4},{4,0},{8,12},{12,8},{16,20},{20,16},{24,28},{28,24},{1,5},{5... | collective-permute-start | bytes 884744 | tf_op jit(solution)/shard_map/ppermute | solution.py:276
  43.7 11.5 %collective-permute-start.16 = (bf16[4,96,768]{2,1,0:T(8,128)(2,1)S(1)}, bf16[4,96,768]{2,1,0:T(8,128)(2,1)S(1)}, u32[]{:S(2)}, u32[]{:S(2)}) collective-permute-start(bf16[4,96,768]{2,1,0:T(8,128)(2,1)S(1)} %collective-permute-done.10.c1), channel_id=1, source_target_pairs={{0,4},{4,0},{8,12},{12,8},{16,20},{20,16},{24,28},{28,24},{1,5},{5... | collective-permute-start | bytes 1769480 | tf_op jit(solution)/shard_map/ppermute | solution.py:276
  50.3 4.8 %collective-permute-start.17 = (bf16[4,96,768]{2,1,0:T(8,128)(2,1)S(1)}, bf16[4,96,768]{2,1,0:T(8,128)(2,1)S(1)}, u32[]{:S(2)}, u32[]{:S(2)}) collective-permute-start(bf16[4,96,768]{2,1,0:T(8,128)(2,1)S(1)} %collective-permute-done.11.o1), channel_id=1, source_target_pairs={{0,4},{4,0},{8,12},{12,8},{16,20},{20,16},{24,28},{28,24},{1,5},{5... | collective-permute-start | bytes 1769480 | tf_op jit(solution)/shard_map/ppermute | solution.py:276
  50.3 4.8 %collective-permute-start.19 = (bf16[4,96,768]{2,1,0:T(8,128)(2,1)S(1)}, bf16[4,96,768]{2,1,0:T(8,128)(2,1)S(1)}, u32[]{:S(2)}, u32[]{:S(2)}) collective-permute-start(bf16[4,96,768]{2,1,0:T(8,128)(2,1)S(1)} %collective-permute-done.18.c3), channel_id=1, source_target_pairs={{0,4},{4,0},{8,12},{12,8},{16,20},{20,16},{24,28},{28,24},{1,5},{5... | collective-permute-start | bytes 1769480 | tf_op jit(solution)/shard_map/ppermute | solution.py:276
  50.9 3.2 %collective-permute-start.15 = (bf16[3,64,768]{2,1,0:T(8,128)(2,1)S(1)}, bf16[3,64,768]{2,1,0:T(8,128)(2,1)S(1)}, u32[]{:S(2)}, u32[]{:S(2)}) collective-permute-start(bf16[3,64,768]{2,1,0:T(8,128)(2,1)S(1)} %collective-permute-done.13.got2), channel_id=1, source_target_pairs={{0,4},{4,0},{8,12},{12,8},{16,20},{20,16},{24,28},{28,24},{1,5},{5... | collective-permute-start | bytes 884744 | tf_op jit(solution)/shard_map/ppermute | solution.py:276
  50.9 3.6 %collective-permute-start.14 = (bf16[3,64,768]{2,1,0:T(8,128)(2,1)S(1)}, bf16[3,64,768]{2,1,0:T(8,128)(2,1)S(1)}, u32[]{:S(2)}, u32[]{:S(2)}) collective-permute-start(bf16[3,64,768]{2,1,0:T(8,128)(2,1)S(1)} %collective-permute-done.12.got1), channel_id=1, source_target_pairs={{0,4},{4,0},{8,12},{12,8},{16,20},{20,16},{24,28},{28,24},{1,5},{5... | collective-permute-start | bytes 884744 | tf_op jit(solution)/shard_map/ppermute | solution.py:276

commit v5 on v4

--- a/solution.py
+++ b/solution.py
@@ -210,30 +210,35 @@
     own_id = jnp.full((1, lanes), -2, jnp.int32)
     for u in range(var_count):
         own_id = jnp.where(lane_u == u, ids[u], own_id)
-    keys = kbuf[...].reshape(count, rows, inner)
-    score = 0.0
+    reach = [
+        [w for w in range(count) if needed(u, w, var_count, far_count)] for u in range(var_count)
+    ]
+    score = [0.0] * count
     for u in range(var_count):
-        product = keys * qbuf[u * rows : (u + 1) * rows, :][None]
-        score = score + jnp.dot(
-            product.reshape(count * rows, inner), collect[u], preferred_element_type=jnp.float32
+        query = qbuf[u * rows : (u + 1) * rows, :]
+        product = [kbuf[w * rows : (w + 1) * rows, :] * query for w in reach[u]]
+        part = jnp.dot(
+            jnp.concatenate(product, axis=0), collect[u], preferred_element_type=jnp.float32
         )
+        for place, w in enumerate(reach[u]):
+            score[w] = score[w] + part[place * rows : (place + 1) * rows]
     scores = [
-        jnp.where(own_id == ids[w], score[w * rows : (w + 1) * rows], -jnp.inf) for w in range(count)
+        jnp.where(own_id == ids[w], score[w], -jnp.inf) for w in range(count)
     ]
     highest = functools.reduce(jnp.maximum, scores)
     highest = jnp.where(lane_u < var_count, highest, 0.0)
     raised = [jnp.exp(one - highest) for one in scores]
     total = functools.reduce(lambda a, b: a + b, raised)
     share = 1.0 / jnp.where(lane_u < var_count, total, 1.0)
-    prob = jnp.concatenate([(one * share).astype(jnp.bfloat16) for one in raised], axis=0)
+    prob = [(one * share).astype(jnp.bfloat16) for one in raised]
     for u in range(var_count):
-        each = jnp.dot(prob, spread[u], preferred_element_type=jnp.float32)
+        shares = jnp.concatenate([prob[w] for w in reach[u]], axis=0)
+        each = jnp.dot(shares, spread[u], preferred_element_type=jnp.float32)
         mixed = None
-        for w in range(count):
-            if needed(u, w, var_count, far_count):
-                at = slice(w * rows, (w + 1) * rows)
-                term = each[at] * vbuf[at, :].astype(jnp.float32)
-                mixed = term if mixed is None else mixed + term
+        for place, w in enumerate(reach[u]):
+            values = vbuf[w * rows : (w + 1) * rows, :].astype(jnp.float32)
+            term = each[place * rows : (place + 1) * rows] * values
+            mixed = term if mixed is None else mixed + term
         att[u * rows : (u + 1) * rows, :] = mixed.astype(jnp.bfloat16)
     summed = jnp.dot(att[...], uall[...], preferred_element_type=jnp.float32)
     summed = summed + mid_ref[...].astype(jnp.float32).reshape(summed.shape)
@@ -364,8 +369,9 @@
     c1f, _ = lax.optimization_barrier((c1, x_own))
     c3 = send(c1f, first)
     swapped1, swapped2 = partner(got1), partner(got2)
-    c1, o1, got1, got2 = lax.optimization_barrier((c1, o1, got1, got2))
-    c2, o2 = partner(c1), partner(o1)
+    c2 = partner(c1f)
+    o1, got1, got2 = lax.optimization_barrier((o1, got1, got2))
+    o2 = partner(o1)
     o3 = partner(c3)
     count = 3 * var_count + 2 * far_count
     own_rows = var_count * rows

time: 64.6 us -> 63.1 us (0.977)
  Pallas kernels: 15 us -> 14.3 us
    pallas_call x1, Pallas kernels: 8.42 us -> 7.72 us  [on_device(): pl.pallas_call(functools.partial(space_kernel, var_count), out_shape=whol...]
  transfers between devices with their start and end apart: 20 -> 20, of which waited for: 7 -> 7; matrix products, arithmetic and copies ran while one was open for 0% -> 0% of each run, Pallas kernels for 10% -> 11%
where the time goes in v5:
time: 63.1 us; the launch traced here: 62.1 us
  starting transfers between devices  29.4 us (47%)
  waiting for transfers between devices  14.5 us (23%)
  Pallas kernels  14.3 us (23%)
  local copies, waits for them, and re-layouts  3.54 us (6%)
    ppermute x6, starting transfers between devices, partner(): return lax.ppermute(block, 'var', swap)  13.5 us
    ppermute x12, starting transfers between devices, send(): return lax.ppermute(block, both, route)  12.6 us
    ppermute x12, waiting for transfers between devices, send(): return lax.ppermute(block, both, route)  11.7 us
    pallas_call x1, Pallas kernels, on_device(): pl.pallas_call(functools.partial(space_kernel, var_count), out_shape=whol...  7.72 us
    unnamed x30, local copies, waits for them, and re-layouts  3.54 us
    ppermute x1, starting transfers between devices, on_device(): lax.ppermute(x_own, 'var', pairs_of(var_size, lambda i: i + 2 if i // 2 %...  3.19 us
    ppermute x6, waiting for transfers between devices, partner(): return lax.ppermute(block, 'var', swap)  2.74 us
    pallas_call x1, Pallas kernels, on_device(): pl.pallas_call(time_kernel, out_shape=[block, block, jax.ShapeDtypeStruct...  2.53 us
  transfers between devices with their start and end apart: 20, of which 7 were waited for; matrix products, arithmetic and copies ran while one was open for 0% of the time, Pallas kernels for 11%

profile of v5, /device:TPU:9, one launch (start us, length us, event | category | flops | bytes accessed | tf_op | source)
XLA Modules:
  0.0 62.1 jit_solution(12560270237526459684)
XLA Ops:
  0.0 1.2 %collective-permute-start = (bf16[3,64,768]{2,1,0:T(8,128)(2,1)}, bf16[3,64,768]{2,1,0:T(8,128)(2,1)S(1)}, u32[]{:S(2)}, u32[]{:S(2)}) collective-permute-start(bf16[3,64,768]{2,1,0:T(8,128)(2,1)} %bitcast.17), channel_id=1, source_target_pairs={{0,1},{1,0},{2,3},{3,2},{4,6},{5,7},{6,4},{7,5},{8,9},{9,8},{10,11... | collective-permute-start | bytes 884744 | tf_op jit(solution)/shard_map/ppermute | solution.py:278
  1.2 1.2 %collective-permute-start.3 = (s32[3,64]{1,0:T(4,128)}, s32[3,64]{1,0:T(4,128)S(1)}, u32[]{:S(2)}, u32[]{:S(2)}) collective-permute-start(s32[3,64]{1,0:T(4,128)} %bitcast.24), channel_id=1, source_target_pairs={{0,3},{1,2},{2,1},{3,0},{4,7},{5,6},{6,5},{7,4},{8,11},{9,10},{10,... | collective-permute-start | bytes 2312 | tf_op jit(solution)/shard_map/ppermute | solution.py:278
  2.4 0.3 collective-permute-start.2
  2.7 1.2 %collective-permute-start.1 = (s32[3,64]{1,0:T(4,128)}, s32[3,64]{1,0:T(4,128)S(1)}, u32[]{:S(2)}, u32[]{:S(2)}) collective-permute-start(s32[3,64]{1,0:T(4,128)} %bitcast.26), channel_id=1, source_target_pairs={{0,1},{1,0},{2,3},{3,2},{4,6},{5,7},{6,4},{7,5},{8,9},{9,8},{10,11... | collective-permute-start | bytes 2312 | tf_op jit(solution)/shard_map/ppermute | solution.py:278
  3.9 1.2 %collective-permute-start.4 = (bf16[3,64,768]{2,1,0:T(8,128)(2,1)}, bf16[3,64,768]{2,1,0:T(8,128)(2,1)S(1)}, u32[]{:S(2)}, u32[]{:S(2)}) collective-permute-start(bf16[3,64,768]{2,1,0:T(8,128)(2,1)} %bitcast.18), channel_id=1, source_target_pairs={{0,2},{1,3},{2,0},{3,1},{4,5},{5,4},{6,7},{7,6},{8,10},{9,11},{10,... | collective-permute-start | bytes 884744 | tf_op jit(solution)/shard_map/ppermute | solution.py:278
  5.1 0.0 collective-permute-done.3.m3
  5.1 0.3 collective-permute-done.2.m2
  5.4 0.7 %collective-permute-done.1.m1 = s32[3,64]{1,0:T(4,128)S(1)} collective-permute-done((s32[3,64]{1,0:T(4,128)}, s32[3,64]{1,0:T(4,128)S(1)}, u32[]{:S(2)}, u32[]{:S(2)}) %collective-permute-start.1) | collective-permute-done | bytes 800 | tf_op jit(solution)/shard_map/ppermute | solution.py:278
  6.1 0.0 collective-permute-done.t1
  6.1 1.2 %collective-permute-start.5 = (bf16[3,64,768]{2,1,0:T(8,128)(2,1)S(1)}, bf16[3,64,768]{2,1,0:T(8,128)(2,1)S(1)}, u32[]{:S(2)}, u32[]{:S(2)}) collective-permute-start(bf16[3,64,768]{2,1,0:T(8,128)(2,1)S(1)} %collective-permute-done.t1), channel_id=1, source_target_pairs={{0,2},{1,3},{2,0},{3,1},{4,5},{5,4},{6,7},{7,6},{8,10},{9,11},{10,... | collective-permute-start | bytes 884744 | tf_op jit(solution)/shard_map/ppermute | solution.py:278
  7.3 0.0 copy-done.11
  7.3 0.1 pad_add_fusion.place_ref
  7.4 1.2 %copy-done = bf16[768,3,192]{0,2,1:T(8,128)(2,1)S(1)} copy-done((bf16[768,3,192]{0,2,1:T(8,128)(2,1)S(1)}, bf16[768,3,192]{0,2,1:T(8,128)(2,1)}, u32[]{:S(2)}) %copy-start) | copy-done | bytes 884760
  8.6 1.0 %copy-done.3 = bf16[192,768]{1,0:T(8,128)(2,1)S(1)} copy-done((bf16[192,768]{1,0:T(8,128)(2,1)S(1)}, bf16[192,768]{1,0:T(8,128)(2,1)}, u32[]{:S(2)}) %copy-start.3) | copy-done | bytes 294936
  9.6 1.1 %split.1 = (bf16[4,96,768]{2,1,0:T(8,128)(2,1)S(1)}, bf16[4,96,768]{2,1,0:T(8,128)(2,1)S(1)}) custom-call(s32[3]{0:T(128)S(1)} %pad_add_fusion.place_ref, bf16[3,192,768]{2,1,0:T(8,128)(2,1)S(1)} %bitcast.15, bf16[192,768]{1,0:T(8,128)(2,1)S(1)} %copy-done.3), custom_call_target="tpu_custom_call" | custom-call | flops 1000 | bytes 1000 | tf_op jit(solution)/shard_map/split/pallas_call | solution.py:311
  10.7 0.0 copy-start.5
  10.7 0.0 copy-start.10
  10.7 0.1 add_multiply_fusion.base_ref
  10.8 0.0 collective-permute-done.4.t2
  10.8 0.0 copy-done.2
  10.8 1.0 %project.1.early_ref = bf16[576,576]{1,0:T(8,128)(2,1)S(1)} custom-call(bf16[3,64,768]{2,1,0:T(8,128)(2,1)S(1)} %bitcast.19, bf16[3,64,768]{2,1,0:T(8,128)(2,1)S(1)} %collective-permute-done.t1, bf16[3,64,768]{2,1,0:T(8,128)(2,1)S(1)} %collective-permute-done.4.t2, f32[768]{0:T(1024)S(1)} %copy-done.7, bf16[576,768]{1,0:T(8,128)(2,1)S(1)} %bitcast.22), custom_call_target="tpu_custom_call" | custom-call | flops 1000 | bytes 1000 | tf_op jit(solution)/shard_map/project/pallas_call | solution.py:297
  11.8 0.0 copy-done.5
  11.8 0.0 copy-start.8
  11.9 1.3 %collective-permute-start.7 = (bf16[1,192,768]{2,1,0:T(8,128)(2,1)S(1)}, bf16[1,192,768]{2,1,0:T(8,128)(2,1)S(1)}, u32[]{:S(2)}, u32[]{:S(2)}) collective-permute-start(bf16[1,192,768]{2,1,0:T(8,128)(2,1)S(1)} %bitcast.21), channel_id=1, source_target_pairs={{0,1},{1,0},{2,3},{3,2},{4,6},{5,7},{6,4},{7,5},{8,9},{9,8},{10,11... | collective-permute-start | bytes 884744 | tf_op jit(solution)/shard_map/ppermute | solution.py:278
  13.2 0.8 %collective-permute-start.15 = (bf16[4,96,768]{2,1,0:T(8,128)(2,1)S(1)}, bf16[4,96,768]{2,1,0:T(8,128)(2,1)S(1)}, u32[]{:S(2)}, u32[]{:S(2)}) collective-permute-start(bf16[4,96,768]{2,1,0:T(8,128)(2,1)S(1)} %get-tuple-element.43), channel_id=1, source_target_pairs={{0,2},{1,3},{2,0},{3,1},{4,5},{5,4},{6,7},{7,6},{8,10},{9,11},{10,... | collective-permute-start | bytes 1769480 | tf_op jit(solution)/shard_map/ppermute | solution.py:278
  14.0 0.0 collective-permute-done.5.t3
  14.0 0.7 %copy-done.12 = s32[3,64]{1,0:T(4,128)S(1)} copy-done((s32[3,64]{1,0:T(4,128)S(1)}, s32[3,64]{1,0:T(4,128)}, u32[]{:S(2)}) %copy-start.12) | copy-done | bytes 792
  14.7 0.7 %copy-done.14 = s32[3,64]{1,0:T(4,128)S(1)} copy-done((s32[3,64]{1,0:T(4,128)S(1)}, s32[3,64]{1,0:T(4,128)}, u32[]{:S(2)}) %copy-start.14) | copy-done | bytes 792
  15.4 2.5 %time.1 = (bf16[3,64,192]{2,1,0:T(8,128)(2,1)S(1)}, bf16[3,64,192]{2,1,0:T(8,128)(2,1)S(1)}, bf16[6,64,192]{2,1,0:T(8,128)(2,1)S(1)}) custom-call(s32[4]{0:T(128)S(1)} %add_multiply_fusion.base_ref, bf16[576,576]{1,0:T(8,128)(2,1)S(1)} %project.1.early_ref, bf16[3,64,768]{2,1,0:T(8,128)(2,1)S(1)} %collective-permute-done.5.t3, s32[3,64]{1,0:T(4,128)S(1)} %bitcast.27, ...), custom_call_target="tpu_custom_call" | custom-call | flops 10000000000 | bytes 1000 | tf_op jit(solution)/shard_map/time/pallas_call | solution.py:329
  17.9 0.9 %collective-permute-start.6 = (bf16[6,64,192]{2,1,0:T(8,128)(2,1)S(1)}, bf16[6,64,192]{2,1,0:T(8,128)(2,1)S(1)}, u32[]{:S(2)}, u32[]{:S(2)}) collective-permute-start(bf16[6,64,192]{2,1,0:T(8,128)(2,1)S(1)} %get-tuple-element.34), channel_id=1, source_target_pairs={{0,1},{1,0},{2,3},{3,2},{4,6},{5,7},{6,4},{7,5},{8,9},{9,8},{10,11... | collective-permute-start | bytes 442376 | tf_op jit(solution)/shard_map/ppermute | solution.py:278
  18.8 0.8 %collective-permute-done.7.w1 = bf16[1,192,768]{2,1,0:T(8,128)(2,1)S(1)} collective-permute-done((bf16[1,192,768]{2,1,0:T(8,128)(2,1)S(1)}, bf16[1,192,768]{2,1,0:T(8,128)(2,1)S(1)}, u32[]{:S(2)}, u32[]{:S(2)}) %collective-permute-start.7) | collective-permute-done | bytes 294944 | tf_op jit(solution)/shard_map/ppermute | solution.py:278
  19.6 5.2 %collective-permute-done.6.got = bf16[6,64,192]{2,1,0:T(8,128)(2,1)S(1)} collective-permute-done((bf16[6,64,192]{2,1,0:T(8,128)(2,1)S(1)}, bf16[6,64,192]{2,1,0:T(8,128)(2,1)S(1)}, u32[]{:S(2)}, u32[]{:S(2)}) %collective-permute-start.6) | collective-permute-done | bytes 147488 | tf_op jit(solution)/shard_map/ppermute | solution.py:278
  24.9 0.3 part.1
  25.2 1.0 %collective-permute-start.8 = (bf16[3,64,768]{2,1,0:T(8,128)(2,1)S(1)}, bf16[3,64,768]{2,1,0:T(8,128)(2,1)S(1)}, u32[]{:S(2)}, u32[]{:S(2)}) collective-permute-start(bf16[3,64,768]{2,1,0:T(8,128)(2,1)S(1)} %part.1), channel_id=1, source_target_pairs={{0,2},{1,3},{2,0},{3,1},{4,5},{5,4},{6,7},{7,6},{8,10},{9,11},{10,... | collective-permute-start | bytes 884744 | tf_op jit(solution)/shard_map/ppermute | solution.py:278
  26.1 4.7 %collective-permute-done.8.part_ref = bf16[3,64,768]{2,1,0:T(8,128)(2,1)S(1)} collective-permute-done((bf16[3,64,768]{2,1,0:T(8,128)(2,1)S(1)}, bf16[3,64,768]{2,1,0:T(8,128)(2,1)S(1)}, u32[]{:S(2)}, u32[]{:S(2)}) %collective-permute-start.8) | collective-permute-done | bytes 294944 | tf_op jit(solution)/shard_map/ppermute | solution.py:278
  30.8 1.6 %collective-permute-start.10 = (bf16[4,96,768]{2,1,0:T(8,128)(2,1)S(1)}, bf16[4,96,768]{2,1,0:T(8,128)(2,1)S(1)}, u32[]{:S(2)}, u32[]{:S(2)}) collective-permute-start(bf16[4,96,768]{2,1,0:T(8,128)(2,1)S(1)} %get-tuple-element.40), channel_id=1, source_target_pairs={{0,2},{1,3},{2,0},{3,1},{4,5},{5,4},{6,7},{7,6},{8,10},{9,11},{10,... | collective-permute-start | bytes 1769480 | tf_op jit(solution)/shard_map/ppermute | solution.py:278
  32.4 1.0 %mid.1 = (bf16[3,64,768]{2,1,0:T(8,128)(2,1)S(1)}, bf16[3,64,768]{2,1,0:T(8,128)(2,1)S(1)}) custom-call(s32[3]{0:T(128)S(1)} %pad_add_fusion.place_ref, bf16[3,64,192]{2,1,0:T(8,128)(2,1)S(1)} %get-tuple-element.33.a0, bf16[6,64,192]{2,1,0:T(8,128)(2,1)S(1)} %collective-permute-done.6.got, bf16[192,768]{1,0:T(8,128)(2,1)S(1)} %copy-done.5, ...), custom_call_target="tpu_custom_call" | custom-call | flops 1000 | bytes 1000 | tf_op jit(solution)/shard_map/mid/pallas_call | solution.py:354
  33.5 0.0 collective-permute-done.15.c1
  33.5 0.0 copy-start.1
  33.5 0.0 copy-start.4
  33.5 0.0 copy-start.9
  33.5 0.6 collective-permute-start.18
  34.1 3.2 %collective-permute-start.12 = (bf16[3,64,768]{2,1,0:T(8,128)(2,1)S(1)}, bf16[3,64,768]{2,1,0:T(8,128)(2,1)S(1)}, u32[]{:S(2)}, u32[]{:S(2)}) collective-permute-start(bf16[3,64,768]{2,1,0:T(8,128)(2,1)S(1)} %get-tuple-element.39.x0), channel_id=1, source_target_pairs={{8,16},{12,20},{16,8},{20,12},{9,17},{13,21},{17,9},{21,13},{10,18... | collective-permute-start | bytes 884744 | tf_op jit(solution)/shard_map/ppermute | solution.py:365
  37.3 0.1 collective-permute-start.11
  37.4 6.3 %collective-permute-start.9 = (bf16[3,64,768]{2,1,0:T(8,128)(2,1)S(1)}, bf16[3,64,768]{2,1,0:T(8,128)(2,1)S(1)}, u32[]{:S(2)}, u32[]{:S(2)}) collective-permute-start(bf16[3,64,768]{2,1,0:T(8,128)(2,1)S(1)} %get-tuple-element.39.x0), channel_id=1, source_target_pairs={{0,4},{4,0},{8,12},{12,8},{16,20},{20,16},{24,28},{28,24},{1,5},{5... | collective-permute-start | bytes 884744 | tf_op jit(solution)/shard_map/ppermute | solution.py:281
  43.7 0.0 collective-permute-done.12.got2
  43.7 5.0 %collective-permute-start.16 = (bf16[4,96,768]{2,1,0:T(8,128)(2,1)S(1)}, bf16[4,96,768]{2,1,0:T(8,128)(2,1)S(1)}, u32[]{:S(2)}, u32[]{:S(2)}) collective-permute-start(bf16[4,96,768]{2,1,0:T(8,128)(2,1)S(1)} %collective-permute-done.15.c1), channel_id=1, source_target_pairs={{0,4},{4,0},{8,12},{12,8},{16,20},{20,16},{24,28},{28,24},{1,5},{5... | collective-permute-start | bytes 1769480 | tf_op jit(solution)/shard_map/ppermute | solution.py:281
  48.7 0.0 collective-permute-done.11.got1
  48.7 0.0 collective-permute-done.10.o1
  48.7 1.7 %collective-permute-start.17 = (bf16[4,96,768]{2,1,0:T(8,128)(2,1)S(1)}, bf16[4,96,768]{2,1,0:T(8,128)(2,1)S(1)}, u32[]{:S(2)}, u32[]{:S(2)}) collective-permute-start(bf16[4,96,768]{2,1,0:T(8,128)(2,1)S(1)} %collective-permute-done.10.o1), channel_id=1, source_target_pairs={{0,4},{4,0},{8,12},{12,8},{16,20},{20,16},{24,28},{28,24},{1,5},{5... | collective-permute-start | bytes 1769480 | tf_op jit(solution)/shard_map/ppermute | solution.py:281
  50.3 0.0 collective-permute-done.18.c3
  50.3 0.1 collective-permute-start.19
  50.4 0.4 collective-permute-start.14
  50.9 0.0 collective-permute-done.9.xs
  50.9 0.1 collective-permute-start.13
  50.9 2.3 %collective-permute-done.14.swapped2 = bf16[3,64,768]{2,1,0:T(8,128)(2,1)S(1)} collective-permute-done((bf16[3,64,768]{2,1,0:T(8,128)(2,1)S(1)}, bf16[3,64,768]{2,1,0:T(8,128)(2,1)S(1)}, u32[]{:S(2)}, u32[]{:S(2)}) %collective-permute-start.14) | collective-permute-done | bytes 294944 | tf_op jit(solution)/shard_map/ppermute | solution.py:281
  53.2 0.4 collective-permute-done.13.swapped1
  53.7 0.6 %window.1.xall = bf16[13,64,768]{2,1,0:T(8,128)(2,1)S(1)} custom-call(s32[3]{0:T(128)S(1)} %pad_add_fusion.place_ref, bf16[3,64,768]{2,1,0:T(8,128)(2,1)S(1)} %get-tuple-element.39.x0, bf16[3,64,768]{2,1,0:T(8,128)(2,1)S(1)} %collective-permute-done.9.xs, bf16[3,64,768]{2,1,0:T(8,128)(2,1)S(1)} %collective-permute-done.11.got1, ...), custom_call_target="tpu_custom_call" | custom-call | flops 1000 | bytes 1000 | tf_op jit(solution)/shard_map/window/pallas_call | solution.py:378
  54.3 0.0 collective-permute-done.16.c2
  54.3 0.0 collective-permute-done.17.o2
  54.3 0.0 collective-permute-done.19.o3
  54.3 0.0 copy-done.1
  54.3 0.0 copy-done.4
  54.4 7.7 %space.1 = bf16[3,64,768]{2,1,0:T(8,128)(2,1)} custom-call(s32[3]{0:T(128)S(1)} %pad_add_fusion.place_ref, s32[24]{0:T(128)S(1)} %copy-done.9, bf16[13,64,768]{2,1,0:T(8,128)(2,1)S(1)} %window.1.xall, bf16[3,192,768]{2,1,0:T(8,128)(2,1)S(1)} %bitcast.16, bf16[192,768]{1,0:T(8,128)(2,1)S(1)} %copy-done.4, bf16[4,96,768]{2,1,0:T(8,128)(2,1)S(1)} %collective-permute-done.15.c1, ...), custom_call_target="tpu_custom_call" | custom-call | flops 1000 | bytes 1000 | tf_op jit(solution)/shard_map/space/pallas_call | solution.py:388
  (15 shorter events, 0.0 us)
Async XLA Ops:
  0.0 10.8 %copy-start.7 = (f32[768]{0:T(1024)S(1)}, f32[768]{0:T(1024)}, u32[]{:S(2)}) copy-start(f32[768]{0:T(1024)} %gain_ref.4) | copy-start | bytes 9220
  0.0 6.1 %collective-permute-start = (bf16[3,64,768]{2,1,0:T(8,128)(2,1)}, bf16[3,64,768]{2,1,0:T(8,128)(2,1)S(1)}, u32[]{:S(2)}, u32[]{:S(2)}) collective-permute-start(bf16[3,64,768]{2,1,0:T(8,128)(2,1)} %bitcast.17), channel_id=1, source_target_pairs={{0,1},{1,0},{2,3},{3,2},{4,6},{5,7},{6,4},{7,5},{8,9},{9,8},{10,11... | collective-permute-start | bytes 884744 | tf_op jit(solution)/shard_map/ppermute | solution.py:278
  1.2 3.9 %collective-permute-start.3 = (s32[3,64]{1,0:T(4,128)}, s32[3,64]{1,0:T(4,128)S(1)}, u32[]{:S(2)}, u32[]{:S(2)}) collective-permute-start(s32[3,64]{1,0:T(4,128)} %bitcast.24), channel_id=1, source_target_pairs={{0,3},{1,2},{2,1},{3,0},{4,7},{5,6},{6,5},{7,4},{8,11},{9,10},{10,... | collective-permute-start | bytes 2312 | tf_op jit(solution)/shard_map/ppermute | solution.py:278
  2.4 3.0 %collective-permute-start.2 = (s32[3,64]{1,0:T(4,128)}, s32[3,64]{1,0:T(4,128)S(1)}, u32[]{:S(2)}, u32[]{:S(2)}) collective-permute-start(s32[3,64]{1,0:T(4,128)} %bitcast.25), channel_id=1, source_target_pairs={{0,2},{1,3},{2,0},{3,1},{4,5},{5,4},{6,7},{7,6},{8,10},{9,11},{10,... | collective-permute-start | bytes 2312 | tf_op jit(solution)/shard_map/ppermute | solution.py:278
  2.7 3.5 %collective-permute-start.1 = (s32[3,64]{1,0:T(4,128)}, s32[3,64]{1,0:T(4,128)S(1)}, u32[]{:S(2)}, u32[]{:S(2)}) collective-permute-start(s32[3,64]{1,0:T(4,128)} %bitcast.26), channel_id=1, source_target_pairs={{0,1},{1,0},{2,3},{3,2},{4,6},{5,7},{6,4},{7,5},{8,9},{9,8},{10,11... | collective-permute-start | bytes 2312 | tf_op jit(solution)/shard_map/ppermute | solution.py:278
  3.9 6.9 %collective-permute-start.4 = (bf16[3,64,768]{2,1,0:T(8,128)(2,1)}, bf16[3,64,768]{2,1,0:T(8,128)(2,1)S(1)}, u32[]{:S(2)}, u32[]{:S(2)}) collective-permute-start(bf16[3,64,768]{2,1,0:T(8,128)(2,1)} %bitcast.18), channel_id=1, source_target_pairs={{0,2},{1,3},{2,0},{3,1},{4,5},{5,4},{6,7},{7,6},{8,10},{9,11},{10,... | collective-permute-start | bytes 884744 | tf_op jit(solution)/shard_map/ppermute | solution.py:278
  5.4 2.0 %copy-start.11 = (s32[3,64]{1,0:T(4,128)}, s32[3,64]{1,0:T(4,128)S(1)}, u32[]{:S(2)}) copy-start(s32[3,64]{1,0:T(4,128)S(1)} %collective-permute-done.2.m2) | copy-start | bytes 2308
  6.1 1.3 %copy-start.13 = (s32[3,64]{1,0:T(4,128)}, s32[3,64]{1,0:T(4,128)S(1)}, u32[]{:S(2)}) copy-start(s32[3,64]{1,0:T(4,128)S(1)} %collective-permute-done.1.m1) | copy-start | bytes 2308
  6.1 7.9 %collective-permute-start.5 = (bf16[3,64,768]{2,1,0:T(8,128)(2,1)S(1)}, bf16[3,64,768]{2,1,0:T(8,128)(2,1)S(1)}, u32[]{:S(2)}, u32[]{:S(2)}) collective-permute-start(bf16[3,64,768]{2,1,0:T(8,128)(2,1)S(1)} %collective-permute-done.t1), channel_id=1, source_target_pairs={{0,2},{1,3},{2,0},{3,1},{4,5},{5,4},{6,7},{7,6},{8,10},{9,11},{10,... | collective-permute-start | bytes 884744 | tf_op jit(solution)/shard_map/ppermute | solution.py:278
  7.4 1.2 %copy-start = (bf16[768,3,192]{0,2,1:T(8,128)(2,1)S(1)}, bf16[768,3,192]{0,2,1:T(8,128)(2,1)}, u32[]{:S(2)}) copy-start(bf16[768,3,192]{0,2,1:T(8,128)(2,1)} %param.16) | copy-start | bytes 2654212
  8.6 1.0 %copy-start.3 = (bf16[192,768]{1,0:T(8,128)(2,1)S(1)}, bf16[192,768]{1,0:T(8,128)(2,1)}, u32[]{:S(2)}) copy-start(bf16[192,768]{1,0:T(8,128)(2,1)} %u_own.1) | copy-start | bytes 884740
  9.6 1.3 %copy-start.2 = (bf16[64,3,768]{2,0,1:T(8,128)(2,1)S(1)}, bf16[64,3,768]{2,0,1:T(8,128)(2,1)}, u32[]{:S(2)}) copy-start(bf16[64,3,768]{2,0,1:T(8,128)(2,1)} %param.9) | copy-start | bytes 884740
  9.6 1.3 %copy-start.6 = (bf16[768,3,192]{0,2,1:T(8,128)(2,1)S(1)}, bf16[768,3,192]{0,2,1:T(8,128)(2,1)}, u32[]{:S(2)}) copy-start(bf16[768,3,192]{0,2,1:T(8,128)(2,1)} %param.13) | copy-start | bytes 2654212
  10.7 1.1 %copy-start.5 = (bf16[192,768]{1,0:T(8,128)(2,1)S(1)}, bf16[192,768]{1,0:T(8,128)(2,1)}, u32[]{:S(2)}) copy-start(bf16[192,768]{1,0:T(8,128)(2,1)} %w0.3) | copy-start | bytes 884740
  10.7 3.3 %copy-start.10 = (s32[64,3]{0,1:T(4,128)S(1)}, s32[64,3]{0,1:T(4,128)}, u32[]{:S(2)}) copy-start(s32[64,3]{0,1:T(4,128)} %param.10) | copy-start | bytes 2308
  11.8 20.6 %copy-start.8 = (f32[768]{0:T(1024)S(1)}, f32[768]{0:T(1024)}, u32[]{:S(2)}) copy-start(f32[768]{0:T(1024)} %gain_ref.5) | copy-start | bytes 9220
  11.9 7.8 %collective-permute-start.7 = (bf16[1,192,768]{2,1,0:T(8,128)(2,1)S(1)}, bf16[1,192,768]{2,1,0:T(8,128)(2,1)S(1)}, u32[]{:S(2)}, u32[]{:S(2)}) collective-permute-start(bf16[1,192,768]{2,1,0:T(8,128)(2,1)S(1)} %bitcast.21), channel_id=1, source_target_pairs={{0,1},{1,0},{2,3},{3,2},{4,6},{5,7},{6,4},{7,5},{8,9},{9,8},{10,11... | collective-permute-start | bytes 884744 | tf_op jit(solution)/shard_map/ppermute | solution.py:278
  13.2 20.3 %collective-permute-start.15 = (bf16[4,96,768]{2,1,0:T(8,128)(2,1)S(1)}, bf16[4,96,768]{2,1,0:T(8,128)(2,1)S(1)}, u32[]{:S(2)}, u32[]{:S(2)}) collective-permute-start(bf16[4,96,768]{2,1,0:T(8,128)(2,1)S(1)} %get-tuple-element.43), channel_id=1, source_target_pairs={{0,2},{1,3},{2,0},{3,1},{4,5},{5,4},{6,7},{7,6},{8,10},{9,11},{10,... | collective-permute-start | bytes 1769480 | tf_op jit(solution)/shard_map/ppermute | solution.py:278
  14.0 0.7 %copy-start.12 = (s32[3,64]{1,0:T(4,128)S(1)}, s32[3,64]{1,0:T(4,128)}, u32[]{:S(2)}) copy-start(s32[3,64]{1,0:T(4,128)} %copy-done.11) | copy-start | bytes 2308
  14.7 0.7 %copy-start.14 = (s32[3,64]{1,0:T(4,128)S(1)}, s32[3,64]{1,0:T(4,128)}, u32[]{:S(2)}) copy-start(s32[3,64]{1,0:T(4,128)} %copy-done.13) | copy-start | bytes 2308
  17.9 7.0 %collective-permute-start.6 = (bf16[6,64,192]{2,1,0:T(8,128)(2,1)S(1)}, bf16[6,64,192]{2,1,0:T(8,128)(2,1)S(1)}, u32[]{:S(2)}, u32[]{:S(2)}) collective-permute-start(bf16[6,64,192]{2,1,0:T(8,128)(2,1)S(1)} %get-tuple-element.34), channel_id=1, source_target_pairs={{0,1},{1,0},{2,3},{3,2},{4,6},{5,7},{6,4},{7,5},{8,9},{9,8},{10,11... | collective-permute-start | bytes 442376 | tf_op jit(solution)/shard_map/ppermute | solution.py:278
  25.2 5.6 %collective-permute-start.8 = (bf16[3,64,768]{2,1,0:T(8,128)(2,1)S(1)}, bf16[3,64,768]{2,1,0:T(8,128)(2,1)S(1)}, u32[]{:S(2)}, u32[]{:S(2)}) collective-permute-start(bf16[3,64,768]{2,1,0:T(8,128)(2,1)S(1)} %part.1), channel_id=1, source_target_pairs={{0,2},{1,3},{2,0},{3,1},{4,5},{5,4},{6,7},{7,6},{8,10},{9,11},{10,... | collective-permute-start | bytes 884744 | tf_op jit(solution)/shard_map/ppermute | solution.py:278
  30.8 17.9 %collective-permute-start.10 = (bf16[4,96,768]{2,1,0:T(8,128)(2,1)S(1)}, bf16[4,96,768]{2,1,0:T(8,128)(2,1)S(1)}, u32[]{:S(2)}, u32[]{:S(2)}) collective-permute-start(bf16[4,96,768]{2,1,0:T(8,128)(2,1)S(1)} %get-tuple-element.40), channel_id=1, source_target_pairs={{0,2},{1,3},{2,0},{3,1},{4,5},{5,4},{6,7},{7,6},{8,10},{9,11},{10,... | collective-permute-start | bytes 1769480 | tf_op jit(solution)/shard_map/ppermute | solution.py:278
  33.5 20.9 %copy-start.1 = (bf16[768,3,192]{0,2,1:T(8,128)(2,1)S(1)}, bf16[768,3,192]{0,2,1:T(8,128)(2,1)}, u32[]{:S(2)}) copy-start(bf16[768,3,192]{0,2,1:T(8,128)(2,1)} %param.16) | copy-start | bytes 2654212
  33.5 20.9 %copy-start.4 = (bf16[192,768]{1,0:T(8,128)(2,1)S(1)}, bf16[192,768]{1,0:T(8,128)(2,1)}, u32[]{:S(2)}) copy-start(bf16[192,768]{1,0:T(8,128)(2,1)} %u_own.1) | copy-start | bytes 884740
  33.5 20.9 %copy-start.9 = (s32[24]{0:T(128)S(1)}, s32[24]{0:T(128)}, u32[]{:S(2)}) copy-start(s32[24]{0:T(128)} %ids_ref.1) | copy-start | bytes 292
  33.5 16.8 %collective-permute-start.18 = (bf16[4,96,768]{2,1,0:T(8,128)(2,1)S(1)}, bf16[4,96,768]{2,1,0:T(8,128)(2,1)S(1)}, u32[]{:S(2)}, u32[]{:S(2)}) collective-permute-start(bf16[4,96,768]{2,1,0:T(8,128)(2,1)S(1)} %collective-permute-done.15.c1), channel_id=1, source_target_pairs={{0,1},{1,0},{2,3},{3,2},{4,6},{5,7},{6,4},{7,5},{8,9},{9,8},{10,11... | collective-permute-start | bytes 1769480 | tf_op jit(solution)/shard_map/ppermute | solution.py:278
  34.1 9.6 %collective-permute-start.12 = (bf16[3,64,768]{2,1,0:T(8,128)(2,1)S(1)}, bf16[3,64,768]{2,1,0:T(8,128)(2,1)S(1)}, u32[]{:S(2)}, u32[]{:S(2)}) collective-permute-start(bf16[3,64,768]{2,1,0:T(8,128)(2,1)S(1)} %get-tuple-element.39.x0), channel_id=1, source_target_pairs={{8,16},{12,20},{16,8},{20,12},{9,17},{13,21},{17,9},{21,13},{10,18... | collective-permute-start | bytes 884744 | tf_op jit(solution)/shard_map/ppermute | solution.py:365
  37.3 11.4 %collective-permute-start.11 = (bf16[3,64,768]{2,1,0:T(8,128)(2,1)S(1)}, bf16[3,64,768]{2,1,0:T(8,128)(2,1)S(1)}, u32[]{:S(2)}, u32[]{:S(2)}) collective-permute-start(bf16[3,64,768]{2,1,0:T(8,128)(2,1)S(1)} %get-tuple-element.39.x0), channel_id=1, source_target_pairs={{0,8},{4,12},{8,0},{12,4},{16,24},{20,28},{24,16},{28,20},{1,9},{5... | collective-permute-start | bytes 884744 | tf_op jit(solution)/shard_map/ppermute | solution.py:364
  37.4 13.5 %collective-permute-start.9 = (bf16[3,64,768]{2,1,0:T(8,128)(2,1)S(1)}, bf16[3,64,768]{2,1,0:T(8,128)(2,1)S(1)}, u32[]{:S(2)}, u32[]{:S(2)}) collective-permute-start(bf16[3,64,768]{2,1,0:T(8,128)(2,1)S(1)} %get-tuple-element.39.x0), channel_id=1, source_target_pairs={{0,4},{4,0},{8,12},{12,8},{16,20},{20,16},{24,28},{28,24},{1,5},{5... | collective-permute-start | bytes 884744 | tf_op jit(solution)/shard_map/ppermute | solution.py:281
  43.7 10.6 %collective-permute-start.16 = (bf16[4,96,768]{2,1,0:T(8,128)(2,1)S(1)}, bf16[4,96,768]{2,1,0:T(8,128)(2,1)S(1)}, u32[]{:S(2)}, u32[]{:S(2)}) collective-permute-start(bf16[4,96,768]{2,1,0:T(8,128)(2,1)S(1)} %collective-permute-done.15.c1), channel_id=1, source_target_pairs={{0,4},{4,0},{8,12},{12,8},{16,20},{20,16},{24,28},{28,24},{1,5},{5... | collective-permute-start | bytes 1769480 | tf_op jit(solution)/shard_map/ppermute | solution.py:281
  48.7 5.6 %collective-permute-start.17 = (bf16[4,96,768]{2,1,0:T(8,128)(2,1)S(1)}, bf16[4,96,768]{2,1,0:T(8,128)(2,1)S(1)}, u32[]{:S(2)}, u32[]{:S(2)}) collective-permute-start(bf16[4,96,768]{2,1,0:T(8,128)(2,1)S(1)} %collective-permute-done.10.o1), channel_id=1, source_target_pairs={{0,4},{4,0},{8,12},{12,8},{16,20},{20,16},{24,28},{28,24},{1,5},{5... | collective-permute-start | bytes 1769480 | tf_op jit(solution)/shard_map/ppermute | solution.py:281
  50.3 4.0 %collective-permute-start.19 = (bf16[4,96,768]{2,1,0:T(8,128)(2,1)S(1)}, bf16[4,96,768]{2,1,0:T(8,128)(2,1)S(1)}, u32[]{:S(2)}, u32[]{:S(2)}) collective-permute-start(bf16[4,96,768]{2,1,0:T(8,128)(2,1)S(1)} %collective-permute-done.18.c3), channel_id=1, source_target_pairs={{0,4},{4,0},{8,12},{12,8},{16,20},{20,16},{24,28},{28,24},{1,5},{5... | collective-permute-start | bytes 1769480 | tf_op jit(solution)/shard_map/ppermute | solution.py:281
  50.4 2.8 %collective-permute-start.14 = (bf16[3,64,768]{2,1,0:T(8,128)(2,1)S(1)}, bf16[3,64,768]{2,1,0:T(8,128)(2,1)S(1)}, u32[]{:S(2)}, u32[]{:S(2)}) collective-permute-start(bf16[3,64,768]{2,1,0:T(8,128)(2,1)S(1)} %collective-permute-done.12.got2), channel_id=1, source_target_pairs={{0,4},{4,0},{8,12},{12,8},{16,20},{20,16},{24,28},{28,24},{1,5},{5... | collective-permute-start | bytes 884744 | tf_op jit(solution)/shard_map/ppermute | solution.py:281
  50.9 2.8 %collective-permute-start.13 = (bf16[3,64,768]{2,1,0:T(8,128)(2,1)S(1)}, bf16[3,64,768]{2,1,0:T(8,128)(2,1)S(1)}, u32[]{:S(2)}, u32[]{:S(2)}) collective-permute-start(bf16[3,64,768]{2,1,0:T(8,128)(2,1)S(1)} %collective-permute-done.11.got1), channel_id=1, source_target_pairs={{0,4},{4,0},{8,12},{12,8},{16,20},{20,16},{24,28},{28,24},{1,5},{5... | collective-permute-start | bytes 884744 | tf_op jit(solution)/shard_map/ppermute | solution.py:281

commit v6 on v5

--- a/solution.py
+++ b/solution.py
@@ -151,7 +151,7 @@
     target[pl.ds(pl.multiple_of(at + (1 - core) * half, 32), half), :] = second[...]
 
 
-def window_kernel(place_ref, x0, xs, got1, got2, swapped1, swapped2, xall):
+def gather_window(place_ref, x0, xs, got1, got2, swapped1, swapped2, xall):
     var_count = x0.shape[0]
     core, up_first = place_ref[0], place_ref[1] == 1
     xall[:var_count] = x0[...]
@@ -165,14 +165,16 @@
 
 
 def space_kernel(
-    var_count, place_ref, ids_ref, xall, own, u_own, c1, o1, c2, o2, c3, o3, mid_ref,
-    out_ref, wall, uall, qbuf, kbuf, vbuf, att,
+    var_count, place_ref, ids_ref, x0, xs, got1, got2, swapped1, swapped2,
+    own, u_own, c1, o1, c2, o2, c3, o3, mid_ref,
+    out_ref, xall, wall, uall, qbuf, kbuf, vbuf, att,
 ):
     count, rows, depth = xall.shape
     far_count = var_count - 1
     inner = wall.shape[1]
     core = place_ref[0]
     width = u_own.shape[0]
+    gather_window(place_ref, x0, xs, got1, got2, swapped1, swapped2, xall)
     for kind in range(4):
         target = wall.at[kind] if kind < 3 else uall
         target[:width, :] = own[kind] if kind < 3 else u_own[...]
@@ -375,22 +377,14 @@
     o3 = partner(c3)
     count = 3 * var_count + 2 * far_count
     own_rows = var_count * rows
-    window = pl.pallas_call(
-        window_kernel,
-        out_shape=jax.ShapeDtypeStruct((count, rows, depth), bf),
-        in_specs=[SM] + [VM] * 6,
-        out_specs=VM,
-        compiler_params=params(8),
-        cost_estimate=cost(1000, 1000),
-        name="window",
-    )(place, x_own, x_swap, got1, got2, swapped1, swapped2)
     inner = 4 * width
     out = pl.pallas_call(
         functools.partial(space_kernel, var_count),
         out_shape=whole,
-        in_specs=[SM] * 2 + [VM] * 10,
+        in_specs=[SM] * 2 + [VM] * 15,
         out_specs=VM,
         scratch_shapes=[
+            pltpu.VMEM((count, rows, depth), bf),
             pltpu.VMEM((kind, inner, depth), bf),
             pltpu.VMEM((inner, depth), bf),
             pltpu.VMEM((own_rows, inner), bf),
@@ -401,7 +395,7 @@
         compiler_params=params(28),
         cost_estimate=cost(1000, 1000),
         name="space",
-    )(place, group_ids, window, qkv_s, space_out, c1, o1, c2, o2, c3, o3, mid)
+    )(place, group_ids, x_own, x_swap, got1, got2, swapped1, swapped2, qkv_s, space_out, c1, o1, c2, o2, c3, o3, mid)
     return jnp.transpose(out, (1, 0, 2))
 
 

time: 63.1 us -> 61.7 us (0.978)
  local copies, waits for them, and re-layouts: 3.54 us -> 2.78 us
    ppermute x12, starting transfers between devices: 12.6 us -> 11.3 us  [send(): return lax.ppermute(block, both, route)]
    unnamed x30 -> x22, local copies, waits for them, and re-layouts: 3.54 us -> 2.78 us
    ppermute x6, starting transfers between devices: 13.5 us -> 14.2 us  [partner(): return lax.ppermute(block, 'var', swap)]
    pallas_call x1 -> x0, Pallas kernels: 0.64 us -> none  [on_device(): pl.pallas_call(window_kernel, out_shape=jax.ShapeDtypeStruct((count, rows...]
  transfers between devices with their start and end apart: 20 -> 20, of which waited for: 7 -> 7; matrix products, arithmetic and copies ran while one was open for 0% -> 0% of each run, Pallas kernels for 11% -> 10%
where the time goes in v6:
time: 61.7 us; the launch traced here: 60.7 us
  starting transfers between devices  28.8 us (47%)
  waiting for transfers between devices  15 us (24%)
  Pallas kernels  13.7 us (22%)
  local copies, waits for them, and re-layouts  2.78 us (5%)
    ppermute x6, starting transfers between devices, partner(): return lax.ppermute(block, 'var', swap)  14.2 us
    ppermute x12, waiting for transfers between devices, send(): return lax.ppermute(block, both, route)  12.3 us
    ppermute x12, starting transfers between devices, send(): return lax.ppermute(block, both, route)  11.3 us
    pallas_call x1, Pallas kernels, on_device(): pl.pallas_call(functools.partial(space_kernel, var_count), out_shape=whol...  7.75 us
    ppermute x1, starting transfers between devices, on_device(): lax.ppermute(x_own, 'var', pairs_of(var_size, lambda i: i + 2 if i // 2 %...  3.2 us
    unnamed x22, local copies, waits for them, and re-layouts  2.78 us
    ppermute x6, waiting for transfers between devices, partner(): return lax.ppermute(block, 'var', swap)  2.74 us
    pallas_call x1, Pallas kernels, on_device(): pl.pallas_call(time_kernel, out_shape=[block, block, jax.ShapeDtypeStruct...  2.53 us
  transfers between devices with their start and end apart: 20, of which 7 were waited for; matrix products, arithmetic and copies ran while one was open for 0% of the time, Pallas kernels for 10%

profile of v6, /device:TPU:9, one launch (start us, length us, event | category | flops | bytes accessed | tf_op | source)
XLA Modules:
  0.0 60.7 jit_solution(8151947559951157545)
XLA Ops:
  0.0 0.0 copy-start.10
  0.0 1.2 %collective-permute-start = (bf16[3,64,768]{2,1,0:T(8,128)(2,1)}, bf16[3,64,768]{2,1,0:T(8,128)(2,1)S(1)}, u32[]{:S(2)}, u32[]{:S(2)}) collective-permute-start(bf16[3,64,768]{2,1,0:T(8,128)(2,1)} %bitcast.17), channel_id=1, source_target_pairs={{0,1},{1,0},{2,3},{3,2},{4,6},{5,7},{6,4},{7,5},{8,9},{9,8},{10,11... | collective-permute-start | bytes 884744 | tf_op jit(solution)/shard_map/ppermute | solution.py:280
  1.2 0.0 copy-done.10
  1.2 1.6 %collective-permute-start.3 = (s32[3,64]{1,0:T(4,128)S(1)}, s32[3,64]{1,0:T(4,128)S(1)}, u32[]{:S(2)}, u32[]{:S(2)}) collective-permute-start(s32[3,64]{1,0:T(4,128)S(1)} %bitcast.24), channel_id=1, source_target_pairs={{0,3},{1,2},{2,1},{3,0},{4,7},{5,6},{6,5},{7,4},{8,11},{9,10},{10,... | collective-permute-start | bytes 2312 | tf_op jit(solution)/shard_map/ppermute | solution.py:280
  2.9 0.3 collective-permute-start.2
  3.1 0.8 %collective-permute-start.1 = (s32[3,64]{1,0:T(4,128)S(1)}, s32[3,64]{1,0:T(4,128)S(1)}, u32[]{:S(2)}, u32[]{:S(2)}) collective-permute-start(s32[3,64]{1,0:T(4,128)S(1)} %bitcast.26), channel_id=1, source_target_pairs={{0,1},{1,0},{2,3},{3,2},{4,6},{5,7},{6,4},{7,5},{8,9},{9,8},{10,11... | collective-permute-start | bytes 2312 | tf_op jit(solution)/shard_map/ppermute | solution.py:280
  3.9 1.2 %collective-permute-start.4 = (bf16[3,64,768]{2,1,0:T(8,128)(2,1)}, bf16[3,64,768]{2,1,0:T(8,128)(2,1)S(1)}, u32[]{:S(2)}, u32[]{:S(2)}) collective-permute-start(bf16[3,64,768]{2,1,0:T(8,128)(2,1)} %bitcast.18), channel_id=1, source_target_pairs={{0,2},{1,3},{2,0},{3,1},{4,5},{5,4},{6,7},{7,6},{8,10},{9,11},{10,... | collective-permute-start | bytes 884744 | tf_op jit(solution)/shard_map/ppermute | solution.py:280
  5.1 0.0 collective-permute-done.3.m3
  5.1 0.5 collective-permute-done.2.m2
  5.7 0.5 collective-permute-done.1.m1
  6.1 0.0 collective-permute-done.t1
  6.1 1.2 %collective-permute-start.5 = (bf16[3,64,768]{2,1,0:T(8,128)(2,1)S(1)}, bf16[3,64,768]{2,1,0:T(8,128)(2,1)S(1)}, u32[]{:S(2)}, u32[]{:S(2)}) collective-permute-start(bf16[3,64,768]{2,1,0:T(8,128)(2,1)S(1)} %collective-permute-done.t1), channel_id=1, source_target_pairs={{0,2},{1,3},{2,0},{3,1},{4,5},{5,4},{6,7},{7,6},{8,10},{9,11},{10,... | collective-permute-start | bytes 884744 | tf_op jit(solution)/shard_map/ppermute | solution.py:280
  7.3 0.1 pad_add_fusion.place_ref
  7.4 0.0 copy-start
  7.4 1.2 %copy-done = bf16[768,3,192]{0,2,1:T(8,128)(2,1)S(1)} copy-done((bf16[768,3,192]{0,2,1:T(8,128)(2,1)S(1)}, bf16[768,3,192]{0,2,1:T(8,128)(2,1)}, u32[]{:S(2)}) %copy-start) | copy-done | bytes 884760
  8.6 1.0 %copy-done.4 = bf16[192,768]{1,0:T(8,128)(2,1)S(1)} copy-done((bf16[192,768]{1,0:T(8,128)(2,1)S(1)}, bf16[192,768]{1,0:T(8,128)(2,1)}, u32[]{:S(2)}) %copy-start.4) | copy-done | bytes 294936
  9.6 1.1 %split.1 = (bf16[4,96,768]{2,1,0:T(8,128)(2,1)S(1)}, bf16[4,96,768]{2,1,0:T(8,128)(2,1)S(1)}) custom-call(s32[3]{0:T(128)S(1)} %pad_add_fusion.place_ref, bf16[3,192,768]{2,1,0:T(8,128)(2,1)S(1)} %bitcast.15, bf16[192,768]{1,0:T(8,128)(2,1)S(1)} %copy-done.4), custom_call_target="tpu_custom_call" | custom-call | flops 1000 | bytes 1000 | tf_op jit(solution)/shard_map/split/pallas_call | solution.py:313
  10.7 0.0 copy-start.7
  10.7 0.1 add_multiply_fusion.base_ref
  10.8 0.0 collective-permute-done.4.t2
  10.8 0.0 copy-done.2
  10.8 0.0 copy-done.6
  10.8 0.6 %copy-done.7 = f32[768]{0:T(1024)S(1)} copy-done((f32[768]{0:T(1024)S(1)}, f32[768]{0:T(1024)}, u32[]{:S(2)}) %copy-start.7) | copy-done | bytes 3096
  11.4 1.0 %project.1.early_ref = bf16[576,576]{1,0:T(8,128)(2,1)S(1)} custom-call(bf16[3,64,768]{2,1,0:T(8,128)(2,1)S(1)} %bitcast.19, bf16[3,64,768]{2,1,0:T(8,128)(2,1)S(1)} %collective-permute-done.t1, bf16[3,64,768]{2,1,0:T(8,128)(2,1)S(1)} %collective-permute-done.4.t2, f32[768]{0:T(1024)S(1)} %copy-done.7, bf16[576,768]{1,0:T(8,128)(2,1)S(1)} %bitcast.22), custom_call_target="tpu_custom_call" | custom-call | flops 1000 | bytes 1000 | tf_op jit(solution)/shard_map/project/pallas_call | solution.py:299
  12.4 0.0 copy-done.3
  12.4 1.3 %collective-permute-start.7 = (bf16[1,192,768]{2,1,0:T(8,128)(2,1)S(1)}, bf16[1,192,768]{2,1,0:T(8,128)(2,1)S(1)}, u32[]{:S(2)}, u32[]{:S(2)}) collective-permute-start(bf16[1,192,768]{2,1,0:T(8,128)(2,1)S(1)} %bitcast.21), channel_id=1, source_target_pairs={{0,1},{1,0},{2,3},{3,2},{4,6},{5,7},{6,4},{7,5},{8,9},{9,8},{10,11... | collective-permute-start | bytes 884744 | tf_op jit(solution)/shard_map/ppermute | solution.py:280
  13.8 0.3 collective-permute-start.15
  14.0 0.0 collective-permute-done.5.t3
  14.0 2.5 %time.1 = (bf16[3,64,192]{2,1,0:T(8,128)(2,1)S(1)}, bf16[3,64,192]{2,1,0:T(8,128)(2,1)S(1)}, bf16[6,64,192]{2,1,0:T(8,128)(2,1)S(1)}) custom-call(s32[4]{0:T(128)S(1)} %add_multiply_fusion.base_ref, bf16[576,576]{1,0:T(8,128)(2,1)S(1)} %project.1.early_ref, bf16[3,64,768]{2,1,0:T(8,128)(2,1)S(1)} %collective-permute-done.5.t3, s32[3,64]{1,0:T(4,128)S(1)} %bitcast.27, ...), custom_call_target="tpu_custom_call" | custom-call | flops 10000000000 | bytes 1000 | tf_op jit(solution)/shard_map/time/pallas_call | solution.py:331
  16.6 0.9 %collective-permute-start.6 = (bf16[6,64,192]{2,1,0:T(8,128)(2,1)S(1)}, bf16[6,64,192]{2,1,0:T(8,128)(2,1)S(1)}, u32[]{:S(2)}, u32[]{:S(2)}) collective-permute-start(bf16[6,64,192]{2,1,0:T(8,128)(2,1)S(1)} %get-tuple-element.34), channel_id=1, source_target_pairs={{0,1},{1,0},{2,3},{3,2},{4,6},{5,7},{6,4},{7,5},{8,9},{9,8},{10,11... | collective-permute-start | bytes 442376 | tf_op jit(solution)/shard_map/ppermute | solution.py:280
  17.4 1.7 %collective-permute-done.7.w1 = bf16[1,192,768]{2,1,0:T(8,128)(2,1)S(1)} collective-permute-done((bf16[1,192,768]{2,1,0:T(8,128)(2,1)S(1)}, bf16[1,192,768]{2,1,0:T(8,128)(2,1)S(1)}, u32[]{:S(2)}, u32[]{:S(2)}) %collective-permute-start.7) | collective-permute-done | bytes 294944 | tf_op jit(solution)/shard_map/ppermute | solution.py:280
  19.1 3.8 %collective-permute-done.6.got = bf16[6,64,192]{2,1,0:T(8,128)(2,1)S(1)} collective-permute-done((bf16[6,64,192]{2,1,0:T(8,128)(2,1)S(1)}, bf16[6,64,192]{2,1,0:T(8,128)(2,1)S(1)}, u32[]{:S(2)}, u32[]{:S(2)}) %collective-permute-start.6) | collective-permute-done | bytes 147488 | tf_op jit(solution)/shard_map/ppermute | solution.py:280
  22.9 0.3 part.1
  23.3 0.0 copy-start.1
  23.3 1.9 %collective-permute-start.8 = (bf16[3,64,768]{2,1,0:T(8,128)(2,1)S(1)}, bf16[3,64,768]{2,1,0:T(8,128)(2,1)S(1)}, u32[]{:S(2)}, u32[]{:S(2)}) collective-permute-start(bf16[3,64,768]{2,1,0:T(8,128)(2,1)S(1)} %part.1), channel_id=1, source_target_pairs={{0,2},{1,3},{2,0},{3,1},{4,5},{5,4},{6,7},{7,6},{8,10},{9,11},{10,... | collective-permute-start | bytes 884744 | tf_op jit(solution)/shard_map/ppermute | solution.py:280
  25.1 5.8 %collective-permute-done.8.part_ref = bf16[3,64,768]{2,1,0:T(8,128)(2,1)S(1)} collective-permute-done((bf16[3,64,768]{2,1,0:T(8,128)(2,1)S(1)}, bf16[3,64,768]{2,1,0:T(8,128)(2,1)S(1)}, u32[]{:S(2)}, u32[]{:S(2)}) %collective-permute-start.8) | collective-permute-done | bytes 294944 | tf_op jit(solution)/shard_map/ppermute | solution.py:280
  30.9 0.3 collective-permute-start.10
  31.2 0.0 copy-done.8
  31.2 1.0 %mid.1 = (bf16[3,64,768]{2,1,0:T(8,128)(2,1)S(1)}, bf16[3,64,768]{2,1,0:T(8,128)(2,1)S(1)}) custom-call(s32[3]{0:T(128)S(1)} %pad_add_fusion.place_ref, bf16[3,64,192]{2,1,0:T(8,128)(2,1)S(1)} %get-tuple-element.33.a0, bf16[6,64,192]{2,1,0:T(8,128)(2,1)S(1)} %collective-permute-done.6.got, bf16[192,768]{1,0:T(8,128)(2,1)S(1)} %copy-done.3, ...), custom_call_target="tpu_custom_call" | custom-call | flops 1000 | bytes 1000 | tf_op jit(solution)/shard_map/mid/pallas_call | solution.py:356
  32.2 0.0 collective-permute-done.15.c1
  32.2 0.0 copy-start.9
  32.2 0.4 collective-permute-start.18
  32.6 3.2 %collective-permute-start.12 = (bf16[3,64,768]{2,1,0:T(8,128)(2,1)S(1)}, bf16[3,64,768]{2,1,0:T(8,128)(2,1)S(1)}, u32[]{:S(2)}, u32[]{:S(2)}) collective-permute-start(bf16[3,64,768]{2,1,0:T(8,128)(2,1)S(1)} %get-tuple-element.39.x0), channel_id=1, source_target_pairs={{8,16},{12,20},{16,8},{20,12},{9,17},{13,21},{17,9},{21,13},{10,18... | collective-permute-start | bytes 884744 | tf_op jit(solution)/shard_map/ppermute | solution.py:367
  35.8 0.1 collective-permute-start.11
  35.9 7.0 %collective-permute-start.9 = (bf16[3,64,768]{2,1,0:T(8,128)(2,1)S(1)}, bf16[3,64,768]{2,1,0:T(8,128)(2,1)S(1)}, u32[]{:S(2)}, u32[]{:S(2)}) collective-permute-start(bf16[3,64,768]{2,1,0:T(8,128)(2,1)S(1)} %get-tuple-element.39.x0), channel_id=1, source_target_pairs={{0,4},{4,0},{8,12},{12,8},{16,20},{20,16},{24,28},{28,24},{1,5},{5... | collective-permute-start | bytes 884744 | tf_op jit(solution)/shard_map/ppermute | solution.py:283
  42.9 0.0 collective-permute-done.12.got2
  42.9 5.0 %collective-permute-start.16 = (bf16[4,96,768]{2,1,0:T(8,128)(2,1)S(1)}, bf16[4,96,768]{2,1,0:T(8,128)(2,1)S(1)}, u32[]{:S(2)}, u32[]{:S(2)}) collective-permute-start(bf16[4,96,768]{2,1,0:T(8,128)(2,1)S(1)} %collective-permute-done.15.c1), channel_id=1, source_target_pairs={{0,4},{4,0},{8,12},{12,8},{16,20},{20,16},{24,28},{28,24},{1,5},{5... | collective-permute-start | bytes 1769480 | tf_op jit(solution)/shard_map/ppermute | solution.py:283
  47.9 0.0 collective-permute-done.11.got1
  47.9 0.0 collective-permute-done.10.o1
  47.9 1.7 %collective-permute-start.17 = (bf16[4,96,768]{2,1,0:T(8,128)(2,1)S(1)}, bf16[4,96,768]{2,1,0:T(8,128)(2,1)S(1)}, u32[]{:S(2)}, u32[]{:S(2)}) collective-permute-start(bf16[4,96,768]{2,1,0:T(8,128)(2,1)S(1)} %collective-permute-done.10.o1), channel_id=1, source_target_pairs={{0,4},{4,0},{8,12},{12,8},{16,20},{20,16},{24,28},{28,24},{1,5},{5... | collective-permute-start | bytes 1769480 | tf_op jit(solution)/shard_map/ppermute | solution.py:283
  49.5 0.0 collective-permute-done.18.c3
  49.5 0.1 collective-permute-start.19
  49.6 0.4 collective-permute-start.14
  50.1 0.0 collective-permute-done.9.xs
  50.1 0.1 collective-permute-start.13
  50.1 2.3 %collective-permute-done.14.swapped2 = bf16[3,64,768]{2,1,0:T(8,128)(2,1)S(1)} collective-permute-done((bf16[3,64,768]{2,1,0:T(8,128)(2,1)S(1)}, bf16[3,64,768]{2,1,0:T(8,128)(2,1)S(1)}, u32[]{:S(2)}, u32[]{:S(2)}) %collective-permute-start.14) | collective-permute-done | bytes 294944 | tf_op jit(solution)/shard_map/ppermute | solution.py:283
  52.4 0.4 collective-permute-done.13.swapped1
  52.9 0.0 collective-permute-done.16.c2
  52.9 0.0 collective-permute-done.17.o2
  52.9 0.0 collective-permute-done.19.o3
  52.9 0.0 copy-done.1
  52.9 0.0 copy-done.5
  52.9 0.0 copy-done.9
  52.9 7.8 %space.1 = bf16[3,64,768]{2,1,0:T(8,128)(2,1)} custom-call(s32[3]{0:T(128)S(1)} %pad_add_fusion.place_ref, s32[24]{0:T(128)S(1)} %copy-done.9, bf16[3,64,768]{2,1,0:T(8,128)(2,1)S(1)} %get-tuple-element.39.x0, bf16[3,64,768]{2,1,0:T(8,128)(2,1)S(1)} %collective-permute-done.9.xs, bf16[3,64,768]{2,1,0:T(8,128)(2,1)S(1)} %collective-permute-done.11.got1, ...), custom_call_target="tpu_custom_call" | custom-call | flops 1000 | bytes 1000 | tf_op jit(solution)/shard_map/space/pallas_call | solution.py:381
  (6 shorter events, 0.0 us)
Async XLA Ops:
  0.0 1.2 %copy-start.10 = (s32[64,3]{0,1:T(4,128)S(1)}, s32[64,3]{0,1:T(4,128)}, u32[]{:S(2)}) copy-start(s32[64,3]{0,1:T(4,128)} %param.10) | copy-start | bytes 2308
  0.0 6.1 %collective-permute-start = (bf16[3,64,768]{2,1,0:T(8,128)(2,1)}, bf16[3,64,768]{2,1,0:T(8,128)(2,1)S(1)}, u32[]{:S(2)}, u32[]{:S(2)}) collective-permute-start(bf16[3,64,768]{2,1,0:T(8,128)(2,1)} %bitcast.17), channel_id=1, source_target_pairs={{0,1},{1,0},{2,3},{3,2},{4,6},{5,7},{6,4},{7,5},{8,9},{9,8},{10,11... | collective-permute-start | bytes 884744 | tf_op jit(solution)/shard_map/ppermute | solution.py:280
  1.2 3.9 %collective-permute-start.3 = (s32[3,64]{1,0:T(4,128)S(1)}, s32[3,64]{1,0:T(4,128)S(1)}, u32[]{:S(2)}, u32[]{:S(2)}) collective-permute-start(s32[3,64]{1,0:T(4,128)S(1)} %bitcast.24), channel_id=1, source_target_pairs={{0,3},{1,2},{2,1},{3,0},{4,7},{5,6},{6,5},{7,4},{8,11},{9,10},{10,... | collective-permute-start | bytes 2312 | tf_op jit(solution)/shard_map/ppermute | solution.py:280
  2.9 2.8 %collective-permute-start.2 = (s32[3,64]{1,0:T(4,128)S(1)}, s32[3,64]{1,0:T(4,128)S(1)}, u32[]{:S(2)}, u32[]{:S(2)}) collective-permute-start(s32[3,64]{1,0:T(4,128)S(1)} %bitcast.25), channel_id=1, source_target_pairs={{0,2},{1,3},{2,0},{3,1},{4,5},{5,4},{6,7},{7,6},{8,10},{9,11},{10,... | collective-permute-start | bytes 2312 | tf_op jit(solution)/shard_map/ppermute | solution.py:280
  3.1 3.0 %collective-permute-start.1 = (s32[3,64]{1,0:T(4,128)S(1)}, s32[3,64]{1,0:T(4,128)S(1)}, u32[]{:S(2)}, u32[]{:S(2)}) collective-permute-start(s32[3,64]{1,0:T(4,128)S(1)} %bitcast.26), channel_id=1, source_target_pairs={{0,1},{1,0},{2,3},{3,2},{4,6},{5,7},{6,4},{7,5},{8,9},{9,8},{10,11... | collective-permute-start | bytes 2312 | tf_op jit(solution)/shard_map/ppermute | solution.py:280
  3.9 6.9 %collective-permute-start.4 = (bf16[3,64,768]{2,1,0:T(8,128)(2,1)}, bf16[3,64,768]{2,1,0:T(8,128)(2,1)S(1)}, u32[]{:S(2)}, u32[]{:S(2)}) collective-permute-start(bf16[3,64,768]{2,1,0:T(8,128)(2,1)} %bitcast.18), channel_id=1, source_target_pairs={{0,2},{1,3},{2,0},{3,1},{4,5},{5,4},{6,7},{7,6},{8,10},{9,11},{10,... | collective-permute-start | bytes 884744 | tf_op jit(solution)/shard_map/ppermute | solution.py:280
  6.1 7.9 %collective-permute-start.5 = (bf16[3,64,768]{2,1,0:T(8,128)(2,1)S(1)}, bf16[3,64,768]{2,1,0:T(8,128)(2,1)S(1)}, u32[]{:S(2)}, u32[]{:S(2)}) collective-permute-start(bf16[3,64,768]{2,1,0:T(8,128)(2,1)S(1)} %collective-permute-done.t1), channel_id=1, source_target_pairs={{0,2},{1,3},{2,0},{3,1},{4,5},{5,4},{6,7},{7,6},{8,10},{9,11},{10,... | collective-permute-start | bytes 884744 | tf_op jit(solution)/shard_map/ppermute | solution.py:280
  7.4 1.2 %copy-start = (bf16[768,3,192]{0,2,1:T(8,128)(2,1)S(1)}, bf16[768,3,192]{0,2,1:T(8,128)(2,1)}, u32[]{:S(2)}) copy-start(bf16[768,3,192]{0,2,1:T(8,128)(2,1)} %param.16) | copy-start | bytes 2654212
  8.6 1.0 %copy-start.4 = (bf16[192,768]{1,0:T(8,128)(2,1)S(1)}, bf16[192,768]{1,0:T(8,128)(2,1)}, u32[]{:S(2)}) copy-start(bf16[192,768]{1,0:T(8,128)(2,1)} %u_own.1) | copy-start | bytes 884740
  9.5 1.3 %copy-start.2 = (bf16[64,3,768]{2,0,1:T(8,128)(2,1)S(1)}, bf16[64,3,768]{2,0,1:T(8,128)(2,1)}, u32[]{:S(2)}) copy-start(bf16[64,3,768]{2,0,1:T(8,128)(2,1)} %param.9) | copy-start | bytes 884740
  9.6 1.3 %copy-start.6 = (bf16[768,3,192]{0,2,1:T(8,128)(2,1)S(1)}, bf16[768,3,192]{0,2,1:T(8,128)(2,1)}, u32[]{:S(2)}) copy-start(bf16[768,3,192]{0,2,1:T(8,128)(2,1)} %param.13) | copy-start | bytes 2654212
  10.7 0.7 %copy-start.7 = (f32[768]{0:T(1024)S(1)}, f32[768]{0:T(1024)}, u32[]{:S(2)}) copy-start(f32[768]{0:T(1024)} %gain_ref.4) | copy-start | bytes 9220
  11.4 1.0 %copy-start.3 = (bf16[192,768]{1,0:T(8,128)(2,1)S(1)}, bf16[192,768]{1,0:T(8,128)(2,1)}, u32[]{:S(2)}) copy-start(bf16[192,768]{1,0:T(8,128)(2,1)} %w0.3) | copy-start | bytes 884740
  12.4 6.7 %collective-permute-start.7 = (bf16[1,192,768]{2,1,0:T(8,128)(2,1)S(1)}, bf16[1,192,768]{2,1,0:T(8,128)(2,1)S(1)}, u32[]{:S(2)}, u32[]{:S(2)}) collective-permute-start(bf16[1,192,768]{2,1,0:T(8,128)(2,1)S(1)} %bitcast.21), channel_id=1, source_target_pairs={{0,1},{1,0},{2,3},{3,2},{4,6},{5,7},{6,4},{7,5},{8,9},{9,8},{10,11... | collective-permute-start | bytes 884744 | tf_op jit(solution)/shard_map/ppermute | solution.py:280
  13.8 18.5 %collective-permute-start.15 = (bf16[4,96,768]{2,1,0:T(8,128)(2,1)S(1)}, bf16[4,96,768]{2,1,0:T(8,128)(2,1)S(1)}, u32[]{:S(2)}, u32[]{:S(2)}) collective-permute-start(bf16[4,96,768]{2,1,0:T(8,128)(2,1)S(1)} %get-tuple-element.43), channel_id=1, source_target_pairs={{0,2},{1,3},{2,0},{3,1},{4,5},{5,4},{6,7},{7,6},{8,10},{9,11},{10,... | collective-permute-start | bytes 1769480 | tf_op jit(solution)/shard_map/ppermute | solution.py:280
  16.6 6.4 %collective-permute-start.6 = (bf16[6,64,192]{2,1,0:T(8,128)(2,1)S(1)}, bf16[6,64,192]{2,1,0:T(8,128)(2,1)S(1)}, u32[]{:S(2)}, u32[]{:S(2)}) collective-permute-start(bf16[6,64,192]{2,1,0:T(8,128)(2,1)S(1)} %get-tuple-element.34), channel_id=1, source_target_pairs={{0,1},{1,0},{2,3},{3,2},{4,6},{5,7},{6,4},{7,5},{8,9},{9,8},{10,11... | collective-permute-start | bytes 442376 | tf_op jit(solution)/shard_map/ppermute | solution.py:280
  22.9 8.2 %copy-start.8 = (f32[768]{0:T(1024)S(1)}, f32[768]{0:T(1024)}, u32[]{:S(2)}) copy-start(f32[768]{0:T(1024)} %gain_ref.5) | copy-start | bytes 9220
  23.3 29.6 %copy-start.1 = (bf16[768,3,192]{0,2,1:T(8,128)(2,1)S(1)}, bf16[768,3,192]{0,2,1:T(8,128)(2,1)}, u32[]{:S(2)}) copy-start(bf16[768,3,192]{0,2,1:T(8,128)(2,1)} %param.16) | copy-start | bytes 2654212
  23.3 7.6 %collective-permute-start.8 = (bf16[3,64,768]{2,1,0:T(8,128)(2,1)S(1)}, bf16[3,64,768]{2,1,0:T(8,128)(2,1)S(1)}, u32[]{:S(2)}, u32[]{:S(2)}) collective-permute-start(bf16[3,64,768]{2,1,0:T(8,128)(2,1)S(1)} %part.1), channel_id=1, source_target_pairs={{0,2},{1,3},{2,0},{3,1},{4,5},{5,4},{6,7},{7,6},{8,10},{9,11},{10,... | collective-permute-start | bytes 884744 | tf_op jit(solution)/shard_map/ppermute | solution.py:280
  30.9 17.0 %collective-permute-start.10 = (bf16[4,96,768]{2,1,0:T(8,128)(2,1)S(1)}, bf16[4,96,768]{2,1,0:T(8,128)(2,1)S(1)}, u32[]{:S(2)}, u32[]{:S(2)}) collective-permute-start(bf16[4,96,768]{2,1,0:T(8,128)(2,1)S(1)} %get-tuple-element.40), channel_id=1, source_target_pairs={{0,2},{1,3},{2,0},{3,1},{4,5},{5,4},{6,7},{7,6},{8,10},{9,11},{10,... | collective-permute-start | bytes 1769480 | tf_op jit(solution)/shard_map/ppermute | solution.py:280
  31.2 21.7 %copy-start.5 = (bf16[192,768]{1,0:T(8,128)(2,1)S(1)}, bf16[192,768]{1,0:T(8,128)(2,1)}, u32[]{:S(2)}) copy-start(bf16[192,768]{1,0:T(8,128)(2,1)} %u_own.1) | copy-start | bytes 884740
  32.2 20.7 %copy-start.9 = (s32[24]{0:T(128)S(1)}, s32[24]{0:T(128)}, u32[]{:S(2)}) copy-start(s32[24]{0:T(128)} %ids_ref.1) | copy-start | bytes 292
  32.2 17.3 %collective-permute-start.18 = (bf16[4,96,768]{2,1,0:T(8,128)(2,1)S(1)}, bf16[4,96,768]{2,1,0:T(8,128)(2,1)S(1)}, u32[]{:S(2)}, u32[]{:S(2)}) collective-permute-start(bf16[4,96,768]{2,1,0:T(8,128)(2,1)S(1)} %collective-permute-done.15.c1), channel_id=1, source_target_pairs={{0,1},{1,0},{2,3},{3,2},{4,6},{5,7},{6,4},{7,5},{8,9},{9,8},{10,11... | collective-permute-start | bytes 1769480 | tf_op jit(solution)/shard_map/ppermute | solution.py:280
  32.6 10.3 %collective-permute-start.12 = (bf16[3,64,768]{2,1,0:T(8,128)(2,1)S(1)}, bf16[3,64,768]{2,1,0:T(8,128)(2,1)S(1)}, u32[]{:S(2)}, u32[]{:S(2)}) collective-permute-start(bf16[3,64,768]{2,1,0:T(8,128)(2,1)S(1)} %get-tuple-element.39.x0), channel_id=1, source_target_pairs={{8,16},{12,20},{16,8},{20,12},{9,17},{13,21},{17,9},{21,13},{10,18... | collective-permute-start | bytes 884744 | tf_op jit(solution)/shard_map/ppermute | solution.py:367
  35.8 12.1 %collective-permute-start.11 = (bf16[3,64,768]{2,1,0:T(8,128)(2,1)S(1)}, bf16[3,64,768]{2,1,0:T(8,128)(2,1)S(1)}, u32[]{:S(2)}, u32[]{:S(2)}) collective-permute-start(bf16[3,64,768]{2,1,0:T(8,128)(2,1)S(1)} %get-tuple-element.39.x0), channel_id=1, source_target_pairs={{0,8},{4,12},{8,0},{12,4},{16,24},{20,28},{24,16},{28,20},{1,9},{5... | collective-permute-start | bytes 884744 | tf_op jit(solution)/shard_map/ppermute | solution.py:366
  35.9 14.2 %collective-permute-start.9 = (bf16[3,64,768]{2,1,0:T(8,128)(2,1)S(1)}, bf16[3,64,768]{2,1,0:T(8,128)(2,1)S(1)}, u32[]{:S(2)}, u32[]{:S(2)}) collective-permute-start(bf16[3,64,768]{2,1,0:T(8,128)(2,1)S(1)} %get-tuple-element.39.x0), channel_id=1, source_target_pairs={{0,4},{4,0},{8,12},{12,8},{16,20},{20,16},{24,28},{28,24},{1,5},{5... | collective-permute-start | bytes 884744 | tf_op jit(solution)/shard_map/ppermute | solution.py:283
  42.9 10.0 %collective-permute-start.16 = (bf16[4,96,768]{2,1,0:T(8,128)(2,1)S(1)}, bf16[4,96,768]{2,1,0:T(8,128)(2,1)S(1)}, u32[]{:S(2)}, u32[]{:S(2)}) collective-permute-start(bf16[4,96,768]{2,1,0:T(8,128)(2,1)S(1)} %collective-permute-done.15.c1), channel_id=1, source_target_pairs={{0,4},{4,0},{8,12},{12,8},{16,20},{20,16},{24,28},{28,24},{1,5},{5... | collective-permute-start | bytes 1769480 | tf_op jit(solution)/shard_map/ppermute | solution.py:283
  47.9 5.0 %collective-permute-start.17 = (bf16[4,96,768]{2,1,0:T(8,128)(2,1)S(1)}, bf16[4,96,768]{2,1,0:T(8,128)(2,1)S(1)}, u32[]{:S(2)}, u32[]{:S(2)}) collective-permute-start(bf16[4,96,768]{2,1,0:T(8,128)(2,1)S(1)} %collective-permute-done.10.o1), channel_id=1, source_target_pairs={{0,4},{4,0},{8,12},{12,8},{16,20},{20,16},{24,28},{28,24},{1,5},{5... | collective-permute-start | bytes 1769480 | tf_op jit(solution)/shard_map/ppermute | solution.py:283
  49.5 3.3 %collective-permute-start.19 = (bf16[4,96,768]{2,1,0:T(8,128)(2,1)S(1)}, bf16[4,96,768]{2,1,0:T(8,128)(2,1)S(1)}, u32[]{:S(2)}, u32[]{:S(2)}) collective-permute-start(bf16[4,96,768]{2,1,0:T(8,128)(2,1)S(1)} %collective-permute-done.18.c3), channel_id=1, source_target_pairs={{0,4},{4,0},{8,12},{12,8},{16,20},{20,16},{24,28},{28,24},{1,5},{5... | collective-permute-start | bytes 1769480 | tf_op jit(solution)/shard_map/ppermute | solution.py:283
  49.6 2.8 %collective-permute-start.14 = (bf16[3,64,768]{2,1,0:T(8,128)(2,1)S(1)}, bf16[3,64,768]{2,1,0:T(8,128)(2,1)S(1)}, u32[]{:S(2)}, u32[]{:S(2)}) collective-permute-start(bf16[3,64,768]{2,1,0:T(8,128)(2,1)S(1)} %collective-permute-done.12.got2), channel_id=1, source_target_pairs={{0,4},{4,0},{8,12},{12,8},{16,20},{20,16},{24,28},{28,24},{1,5},{5... | collective-permute-start | bytes 884744 | tf_op jit(solution)/shard_map/ppermute | solution.py:283
  50.1 2.8 %collective-permute-start.13 = (bf16[3,64,768]{2,1,0:T(8,128)(2,1)S(1)}, bf16[3,64,768]{2,1,0:T(8,128)(2,1)S(1)}, u32[]{:S(2)}, u32[]{:S(2)}) collective-permute-start(bf16[3,64,768]{2,1,0:T(8,128)(2,1)S(1)} %collective-permute-done.11.got1), channel_id=1, source_target_pairs={{0,4},{4,0},{8,12},{12,8},{16,20},{20,16},{24,28},{28,24},{1,5},{5... | collective-permute-start | bytes 884744 | tf_op jit(solution)/shard_map/ppermute | solution.py:283

commit v7 on v6

--- a/solution.py
+++ b/solution.py
@@ -34,7 +34,8 @@
     return lax.dot_general(a, b, NT, preferred_element_type=jnp.float32)
 
 
-def project_kernel(t0, t1, t2, gain_ref, w_ref, out_ref):
+def project_kernel(t0, t1, t2, gain_ref, w_ref, m0, m1, m2, m3, out_ref, marks_ref):
+    marks_ref[...] = jnp.concatenate([m[...] for m in (m0, m1, m2, m3)], axis=1)
     var_count, rows, depth = t0.shape
     gain = gain_ref[...]
     x = [normed(t[v].astype(jnp.float32), gain) for v in range(var_count) for t in (t0, t1, t2)]
@@ -43,12 +44,11 @@
 
 
 def time_kernel(
-    base_ref, early_ref, t3, m0, m1, m2, m3, gain_ref, w_ref, o0, o2, o13
+    base_ref, early_ref, t3, marks_ref, gain_ref, w_ref, o0, o2, o13
 ):
-    masks = (m0, m1, m2, m3)
     var_count, rows, depth = t3.shape
     width = w_ref.shape[0] // 3
-    blocks = len(masks)
+    blocks = marks_ref.shape[1] // rows
     total = rows * blocks
     gain = gain_ref[...]
     x = jnp.concatenate([normed(t3[v].astype(jnp.float32), gain) for v in range(var_count)], axis=0)
@@ -66,7 +66,7 @@
     query_pos, key_pos = positions(row), positions(col)
     causal, same = key_pos <= query_pos, key_pos == query_pos
     head_of = lax.broadcasted_iota(jnp.int32, (1, width), 1) // HD
-    marks = jnp.concatenate([m[...] for m in masks], axis=1)
+    marks = marks_ref[...]
     early = rows * (blocks - 1)
     for v in range(var_count):
         projected = jnp.concatenate(
@@ -296,15 +296,18 @@
     tok3 = send(tok1f, second)
     weight = qkv_t.reshape(kind * width, depth)
     bf = jnp.bfloat16
-    early = pl.pallas_call(
+    early, marks = pl.pallas_call(
         project_kernel,
-        out_shape=jax.ShapeDtypeStruct((3 * var_count * rows, kind * width), bf),
-        in_specs=[VM] * 5,
-        out_specs=VM,
+        out_shape=[
+            jax.ShapeDtypeStruct((3 * var_count * rows, kind * width), bf),
+            jax.ShapeDtypeStruct((var_count, patch_size * rows), jnp.int32),
+        ],
+        in_specs=[VM] * 9,
+        out_specs=[VM] * 2,
         compiler_params=params(),
         cost_estimate=cost(1000, 1000),
         name="project",
-    )(tok, tok1f, tok2, time_gain, weight)
+    )(tok, tok1f, tok2, time_gain, weight, mask, mask1, mask2, mask3)
 
     far_count = var_count - 1
     level = (var_index // 2) % 2
@@ -331,12 +334,12 @@
     att = pl.pallas_call(
         time_kernel,
         out_shape=[block, block, jax.ShapeDtypeStruct((2 * var_count, rows, width), bf)],
-        in_specs=[SM] + [VM] * 8,
+        in_specs=[SM] + [VM] * 5,
         out_specs=[VM] * 3,
         compiler_params=params(),
         cost_estimate=cost(10_000_000_000, 1000),
         name="time",
-    )(bases, early, tok3, mask, mask1, mask2, mask3, time_gain, weight)
+    )(bases, early, tok3, marks, time_gain, weight)
     att0, att2, att13 = att
     got = send(att13, first)
     whole = jax.ShapeDtypeStruct((var_count, rows, depth), jnp.bfloat16)
@@ -351,8 +354,6 @@
         name="part",
     )(att2, got, time_out, t1)
     partial = send(partial, second)
-    other, partial = lax.optimization_barrier((other, partial))
-    o1 = send(other, second)
     mid, x_own = pl.pallas_call(
         mid_kernel,
         out_shape=[whole, whole],
@@ -369,6 +370,8 @@
     )
     x_swap = partner(x_own)
     c1f, _ = lax.optimization_barrier((c1, x_own))
+    other, _ = lax.optimization_barrier((other, x_own))
+    o1 = send(other, second)
     c3 = send(c1f, first)
     swapped1, swapped2 = partner(got1), partner(got2)
     c2 = partner(c1f)

time: 61.7 us -> 61.7 us (level)
  no operation moved by 1% of the time
where the time goes in v7:
time: 61.7 us; the launch traced here: 60.7 us
  starting transfers between devices  28.9 us (47%)
  waiting for transfers between devices  15 us (24%)
  Pallas kernels  13.7 us (22%)
  local copies, waits for them, and re-layouts  2.78 us (5%)
    ppermute x6, starting transfers between devices, partner(): return lax.ppermute(block, 'var', swap)  14.4 us
    ppermute x12, waiting for transfers between devices, send(): return lax.ppermute(block, both, route)  12.3 us
    ppermute x12, starting transfers between devices, send(): return lax.ppermute(block, both, route)  11.3 us
    pallas_call x1, Pallas kernels, on_device(): pl.pallas_call(functools.partial(space_kernel, var_count), out_shape=whol...  7.74 us
    ppermute x1, starting transfers between devices, on_device(): lax.ppermute(x_own, 'var', pairs_of(var_size, lambda i: i + 2 if i // 2 %...  3.19 us
    unnamed x22, local copies, waits for them, and re-layouts  2.78 us
    ppermute x6, waiting for transfers between devices, partner(): return lax.ppermute(block, 'var', swap)  2.74 us
    pallas_call x1, Pallas kernels, on_device(): pl.pallas_call(time_kernel, out_shape=[block, block, jax.ShapeDtypeStruct...  2.52 us
  transfers between devices with their start and end apart: 20, of which 7 were waited for; matrix products, arithmetic and copies ran while one was open for 0% of the time, Pallas kernels for 10%

profile of v7, /device:TPU:9, one launch (start us, length us, event | category | flops | bytes accessed | tf_op | source)
XLA Modules:
  0.0 60.7 jit_solution(11012058431097882015)
XLA Ops:
  0.0 1.2 %collective-permute-start = (bf16[3,64,768]{2,1,0:T(8,128)(2,1)}, bf16[3,64,768]{2,1,0:T(8,128)(2,1)S(1)}, u32[]{:S(2)}, u32[]{:S(2)}) collective-permute-start(bf16[3,64,768]{2,1,0:T(8,128)(2,1)} %bitcast.17), channel_id=1, source_target_pairs={{0,1},{1,0},{2,3},{3,2},{4,6},{5,7},{6,4},{7,5},{8,9},{9,8},{10,11... | collective-permute-start | bytes 884744 | tf_op jit(solution)/shard_map/ppermute | solution.py:280
  1.2 0.0 copy-done.9
  1.2 1.6 %collective-permute-start.3 = (s32[3,64]{1,0:T(4,128)S(1)}, s32[3,64]{1,0:T(4,128)S(1)}, u32[]{:S(2)}, u32[]{:S(2)}) collective-permute-start(s32[3,64]{1,0:T(4,128)S(1)} %bitcast.24), channel_id=1, source_target_pairs={{0,3},{1,2},{2,1},{3,0},{4,7},{5,6},{6,5},{7,4},{8,11},{9,10},{10,... | collective-permute-start | bytes 2312 | tf_op jit(solution)/shard_map/ppermute | solution.py:280
  2.9 0.3 collective-permute-start.2
  3.1 0.8 %collective-permute-start.1 = (s32[3,64]{1,0:T(4,128)S(1)}, s32[3,64]{1,0:T(4,128)S(1)}, u32[]{:S(2)}, u32[]{:S(2)}) collective-permute-start(s32[3,64]{1,0:T(4,128)S(1)} %bitcast.26), channel_id=1, source_target_pairs={{0,1},{1,0},{2,3},{3,2},{4,6},{5,7},{6,4},{7,5},{8,9},{9,8},{10,11... | collective-permute-start | bytes 2312 | tf_op jit(solution)/shard_map/ppermute | solution.py:280
  3.9 1.2 %collective-permute-start.4 = (bf16[3,64,768]{2,1,0:T(8,128)(2,1)}, bf16[3,64,768]{2,1,0:T(8,128)(2,1)S(1)}, u32[]{:S(2)}, u32[]{:S(2)}) collective-permute-start(bf16[3,64,768]{2,1,0:T(8,128)(2,1)} %bitcast.18), channel_id=1, source_target_pairs={{0,2},{1,3},{2,0},{3,1},{4,5},{5,4},{6,7},{7,6},{8,10},{9,11},{10,... | collective-permute-start | bytes 884744 | tf_op jit(solution)/shard_map/ppermute | solution.py:280
  5.1 0.0 collective-permute-done.3.m3
  5.1 0.5 collective-permute-done.2.m2
  5.7 0.5 collective-permute-done.1.m1
  6.1 0.0 collective-permute-done.t1
  6.1 1.2 %collective-permute-start.5 = (bf16[3,64,768]{2,1,0:T(8,128)(2,1)S(1)}, bf16[3,64,768]{2,1,0:T(8,128)(2,1)S(1)}, u32[]{:S(2)}, u32[]{:S(2)}) collective-permute-start(bf16[3,64,768]{2,1,0:T(8,128)(2,1)S(1)} %collective-permute-done.t1), channel_id=1, source_target_pairs={{0,2},{1,3},{2,0},{3,1},{4,5},{5,4},{6,7},{7,6},{8,10},{9,11},{10,... | collective-permute-start | bytes 884744 | tf_op jit(solution)/shard_map/ppermute | solution.py:280
  7.3 0.1 pad_add_fusion.place_ref
  7.4 0.0 copy-start
  7.4 1.2 %copy-done = bf16[768,3,192]{0,2,1:T(8,128)(2,1)S(1)} copy-done((bf16[768,3,192]{0,2,1:T(8,128)(2,1)S(1)}, bf16[768,3,192]{0,2,1:T(8,128)(2,1)}, u32[]{:S(2)}) %copy-start) | copy-done | bytes 884760
  8.6 0.0 copy-start.4
  8.6 1.0 %copy-done.4 = bf16[192,768]{1,0:T(8,128)(2,1)S(1)} copy-done((bf16[192,768]{1,0:T(8,128)(2,1)S(1)}, bf16[192,768]{1,0:T(8,128)(2,1)}, u32[]{:S(2)}) %copy-start.4) | copy-done | bytes 294936
  9.6 1.1 %split.1 = (bf16[4,96,768]{2,1,0:T(8,128)(2,1)S(1)}, bf16[4,96,768]{2,1,0:T(8,128)(2,1)S(1)}) custom-call(s32[3]{0:T(128)S(1)} %pad_add_fusion.place_ref, bf16[3,192,768]{2,1,0:T(8,128)(2,1)S(1)} %bitcast.15, bf16[192,768]{1,0:T(8,128)(2,1)S(1)} %copy-done.4), custom_call_target="tpu_custom_call" | custom-call | flops 1000 | bytes 1000 | tf_op jit(solution)/shard_map/split/pallas_call | solution.py:316
  10.7 0.0 copy-start.7
  10.7 0.1 add_multiply_fusion.base_ref
  10.8 0.0 collective-permute-done.4.t2
  10.8 0.0 copy-done.2
  10.8 0.0 copy-done.6
  10.8 0.6 %copy-done.7 = f32[768]{0:T(1024)S(1)} copy-done((f32[768]{0:T(1024)S(1)}, f32[768]{0:T(1024)}, u32[]{:S(2)}) %copy-start.7) | copy-done | bytes 3096
  11.4 1.0 %project.1 = (bf16[576,576]{1,0:T(8,128)(2,1)S(1)}, s32[3,256]{1,0:T(4,128)S(1)}) custom-call(bf16[3,64,768]{2,1,0:T(8,128)(2,1)S(1)} %bitcast.19, bf16[3,64,768]{2,1,0:T(8,128)(2,1)S(1)} %collective-permute-done.t1, bf16[3,64,768]{2,1,0:T(8,128)(2,1)S(1)} %collective-permute-done.4.t2, f32[768]{0:T(1024)S(1)} %copy-done.7, bf16[576,768]{1,0:T(8,128)(2,1)S(1)} %bitcast.22, ...), custom_call_target="tpu_custom_call" | custom-call | flops 1000 | bytes 1000 | tf_op jit(solution)/shard_map/project/pallas_call | solution.py:299
  12.4 0.0 copy-done.3
  12.4 1.3 %collective-permute-start.7 = (bf16[1,192,768]{2,1,0:T(8,128)(2,1)S(1)}, bf16[1,192,768]{2,1,0:T(8,128)(2,1)S(1)}, u32[]{:S(2)}, u32[]{:S(2)}) collective-permute-start(bf16[1,192,768]{2,1,0:T(8,128)(2,1)S(1)} %bitcast.21), channel_id=1, source_target_pairs={{0,1},{1,0},{2,3},{3,2},{4,6},{5,7},{6,4},{7,5},{8,9},{9,8},{10,11... | collective-permute-start | bytes 884744 | tf_op jit(solution)/shard_map/ppermute | solution.py:280
  13.8 0.3 collective-permute-start.15
  14.0 0.0 collective-permute-done.5.t3
  14.0 2.5 %time.1 = (bf16[3,64,192]{2,1,0:T(8,128)(2,1)S(1)}, bf16[3,64,192]{2,1,0:T(8,128)(2,1)S(1)}, bf16[6,64,192]{2,1,0:T(8,128)(2,1)S(1)}) custom-call(s32[4]{0:T(128)S(1)} %add_multiply_fusion.base_ref, bf16[576,576]{1,0:T(8,128)(2,1)S(1)} %get-tuple-element.34.early_ref, bf16[3,64,768]{2,1,0:T(8,128)(2,1)S(1)} %collective-permute-done.5.t3, ...), custom_call_target="tpu_custom_call" | custom-call | flops 10000000000 | bytes 1000 | tf_op jit(solution)/shard_map/time/pallas_call | solution.py:334
  16.5 0.9 %collective-permute-start.6 = (bf16[6,64,192]{2,1,0:T(8,128)(2,1)S(1)}, bf16[6,64,192]{2,1,0:T(8,128)(2,1)S(1)}, u32[]{:S(2)}, u32[]{:S(2)}) collective-permute-start(bf16[6,64,192]{2,1,0:T(8,128)(2,1)S(1)} %get-tuple-element.37), channel_id=1, source_target_pairs={{0,1},{1,0},{2,3},{3,2},{4,6},{5,7},{6,4},{7,5},{8,9},{9,8},{10,11... | collective-permute-start | bytes 442376 | tf_op jit(solution)/shard_map/ppermute | solution.py:280
  17.4 1.7 %collective-permute-done.7.w1 = bf16[1,192,768]{2,1,0:T(8,128)(2,1)S(1)} collective-permute-done((bf16[1,192,768]{2,1,0:T(8,128)(2,1)S(1)}, bf16[1,192,768]{2,1,0:T(8,128)(2,1)S(1)}, u32[]{:S(2)}, u32[]{:S(2)}) %collective-permute-start.7) | collective-permute-done | bytes 294944 | tf_op jit(solution)/shard_map/ppermute | solution.py:280
  19.1 3.8 %collective-permute-done.6.got = bf16[6,64,192]{2,1,0:T(8,128)(2,1)S(1)} collective-permute-done((bf16[6,64,192]{2,1,0:T(8,128)(2,1)S(1)}, bf16[6,64,192]{2,1,0:T(8,128)(2,1)S(1)}, u32[]{:S(2)}, u32[]{:S(2)}) %collective-permute-start.6) | collective-permute-done | bytes 147488 | tf_op jit(solution)/shard_map/ppermute | solution.py:280
  22.9 0.3 part.1
  23.2 0.0 copy-start.1
  23.2 1.9 %collective-permute-start.8 = (bf16[3,64,768]{2,1,0:T(8,128)(2,1)S(1)}, bf16[3,64,768]{2,1,0:T(8,128)(2,1)S(1)}, u32[]{:S(2)}, u32[]{:S(2)}) collective-permute-start(bf16[3,64,768]{2,1,0:T(8,128)(2,1)S(1)} %part.1), channel_id=1, source_target_pairs={{0,2},{1,3},{2,0},{3,1},{4,5},{5,4},{6,7},{7,6},{8,10},{9,11},{10,... | collective-permute-start | bytes 884744 | tf_op jit(solution)/shard_map/ppermute | solution.py:280
  25.1 5.8 %collective-permute-done.8.part_ref = bf16[3,64,768]{2,1,0:T(8,128)(2,1)S(1)} collective-permute-done((bf16[3,64,768]{2,1,0:T(8,128)(2,1)S(1)}, bf16[3,64,768]{2,1,0:T(8,128)(2,1)S(1)}, u32[]{:S(2)}, u32[]{:S(2)}) %collective-permute-start.8) | collective-permute-done | bytes 294944 | tf_op jit(solution)/shard_map/ppermute | solution.py:280
  30.9 0.0 copy-done.8
  30.9 1.0 %mid.1 = (bf16[3,64,768]{2,1,0:T(8,128)(2,1)S(1)}, bf16[3,64,768]{2,1,0:T(8,128)(2,1)S(1)}) custom-call(s32[3]{0:T(128)S(1)} %pad_add_fusion.place_ref, bf16[3,64,192]{2,1,0:T(8,128)(2,1)S(1)} %get-tuple-element.36.a0, bf16[6,64,192]{2,1,0:T(8,128)(2,1)S(1)} %collective-permute-done.6.got, bf16[192,768]{1,0:T(8,128)(2,1)S(1)} %copy-done.3, ...), custom_call_target="tpu_custom_call" | custom-call | flops 1000 | bytes 1000 | tf_op jit(solution)/shard_map/mid/pallas_call | solution.py:357
  31.9 0.0 copy-start.10
  32.0 0.3 collective-permute-start.10
  32.3 0.0 collective-permute-done.15.c1
  32.3 0.3 collective-permute-start.18
  32.6 3.2 %collective-permute-start.12 = (bf16[3,64,768]{2,1,0:T(8,128)(2,1)S(1)}, bf16[3,64,768]{2,1,0:T(8,128)(2,1)S(1)}, u32[]{:S(2)}, u32[]{:S(2)}) collective-permute-start(bf16[3,64,768]{2,1,0:T(8,128)(2,1)S(1)} %get-tuple-element.40.x0), channel_id=1, source_target_pairs={{8,16},{12,20},{16,8},{20,12},{9,17},{13,21},{17,9},{21,13},{10,18... | collective-permute-start | bytes 884744 | tf_op jit(solution)/shard_map/ppermute | solution.py:368
  35.8 0.1 collective-permute-start.11
  35.8 7.2 %collective-permute-start.9 = (bf16[3,64,768]{2,1,0:T(8,128)(2,1)S(1)}, bf16[3,64,768]{2,1,0:T(8,128)(2,1)S(1)}, u32[]{:S(2)}, u32[]{:S(2)}) collective-permute-start(bf16[3,64,768]{2,1,0:T(8,128)(2,1)S(1)} %get-tuple-element.40.x0), channel_id=1, source_target_pairs={{0,4},{4,0},{8,12},{12,8},{16,20},{20,16},{24,28},{28,24},{1,5},{5... | collective-permute-start | bytes 884744 | tf_op jit(solution)/shard_map/ppermute | solution.py:283
  43.0 0.0 collective-permute-done.12.got2
  43.0 4.9 %collective-permute-start.16 = (bf16[4,96,768]{2,1,0:T(8,128)(2,1)S(1)}, bf16[4,96,768]{2,1,0:T(8,128)(2,1)S(1)}, u32[]{:S(2)}, u32[]{:S(2)}) collective-permute-start(bf16[4,96,768]{2,1,0:T(8,128)(2,1)S(1)} %collective-permute-done.15.c1), channel_id=1, source_target_pairs={{0,4},{4,0},{8,12},{12,8},{16,20},{20,16},{24,28},{28,24},{1,5},{5... | collective-permute-start | bytes 1769480 | tf_op jit(solution)/shard_map/ppermute | solution.py:283
  47.9 0.0 collective-permute-done.11.got1
  47.9 0.0 collective-permute-done.10.o1
  47.9 1.7 %collective-permute-start.17 = (bf16[4,96,768]{2,1,0:T(8,128)(2,1)S(1)}, bf16[4,96,768]{2,1,0:T(8,128)(2,1)S(1)}, u32[]{:S(2)}, u32[]{:S(2)}) collective-permute-start(bf16[4,96,768]{2,1,0:T(8,128)(2,1)S(1)} %collective-permute-done.10.o1), channel_id=1, source_target_pairs={{0,4},{4,0},{8,12},{12,8},{16,20},{20,16},{24,28},{28,24},{1,5},{5... | collective-permute-start | bytes 1769480 | tf_op jit(solution)/shard_map/ppermute | solution.py:283
  49.6 0.0 collective-permute-done.18.c3
  49.6 0.1 collective-permute-start.19
  49.7 0.4 collective-permute-start.14
  50.2 0.0 collective-permute-done.9.xs
  50.2 0.1 collective-permute-start.13
  50.2 2.3 %collective-permute-done.14.swapped2 = bf16[3,64,768]{2,1,0:T(8,128)(2,1)S(1)} collective-permute-done((bf16[3,64,768]{2,1,0:T(8,128)(2,1)S(1)}, bf16[3,64,768]{2,1,0:T(8,128)(2,1)S(1)}, u32[]{:S(2)}, u32[]{:S(2)}) %collective-permute-start.14) | collective-permute-done | bytes 294944 | tf_op jit(solution)/shard_map/ppermute | solution.py:283
  52.5 0.4 collective-permute-done.13.swapped1
  53.0 0.0 collective-permute-done.16.c2
  53.0 0.0 collective-permute-done.17.o2
  53.0 0.0 collective-permute-done.19.o3
  53.0 0.0 copy-done.1
  53.0 0.0 copy-done.5
  53.0 0.0 copy-done.10
  53.0 7.7 %space.1 = bf16[3,64,768]{2,1,0:T(8,128)(2,1)} custom-call(s32[3]{0:T(128)S(1)} %pad_add_fusion.place_ref, s32[24]{0:T(128)S(1)} %copy-done.10, bf16[3,64,768]{2,1,0:T(8,128)(2,1)S(1)} %get-tuple-element.40.x0, bf16[3,64,768]{2,1,0:T(8,128)(2,1)S(1)} %collective-permute-done.9.xs, bf16[3,64,768]{2,1,0:T(8,128)(2,1)S(1)} %collective-permute-done.11.got1, ...), custom_call_target="tpu_custom_call" | custom-call | flops 1000 | bytes 1000 | tf_op jit(solution)/shard_map/space/pallas_call | solution.py:384
  (6 shorter events, 0.0 us)
Async XLA Ops:
  0.0 1.2 %copy-start.9 = (s32[64,3]{0,1:T(4,128)S(1)}, s32[64,3]{0,1:T(4,128)}, u32[]{:S(2)}) copy-start(s32[64,3]{0,1:T(4,128)} %param.10) | copy-start | bytes 2308
  0.0 6.1 %collective-permute-start = (bf16[3,64,768]{2,1,0:T(8,128)(2,1)}, bf16[3,64,768]{2,1,0:T(8,128)(2,1)S(1)}, u32[]{:S(2)}, u32[]{:S(2)}) collective-permute-start(bf16[3,64,768]{2,1,0:T(8,128)(2,1)} %bitcast.17), channel_id=1, source_target_pairs={{0,1},{1,0},{2,3},{3,2},{4,6},{5,7},{6,4},{7,5},{8,9},{9,8},{10,11... | collective-permute-start | bytes 884744 | tf_op jit(solution)/shard_map/ppermute | solution.py:280
  1.2 3.9 %collective-permute-start.3 = (s32[3,64]{1,0:T(4,128)S(1)}, s32[3,64]{1,0:T(4,128)S(1)}, u32[]{:S(2)}, u32[]{:S(2)}) collective-permute-start(s32[3,64]{1,0:T(4,128)S(1)} %bitcast.24), channel_id=1, source_target_pairs={{0,3},{1,2},{2,1},{3,0},{4,7},{5,6},{6,5},{7,4},{8,11},{9,10},{10,... | collective-permute-start | bytes 2312 | tf_op jit(solution)/shard_map/ppermute | solution.py:280
  2.9 2.8 %collective-permute-start.2 = (s32[3,64]{1,0:T(4,128)S(1)}, s32[3,64]{1,0:T(4,128)S(1)}, u32[]{:S(2)}, u32[]{:S(2)}) collective-permute-start(s32[3,64]{1,0:T(4,128)S(1)} %bitcast.25), channel_id=1, source_target_pairs={{0,2},{1,3},{2,0},{3,1},{4,5},{5,4},{6,7},{7,6},{8,10},{9,11},{10,... | collective-permute-start | bytes 2312 | tf_op jit(solution)/shard_map/ppermute | solution.py:280
  3.1 3.0 %collective-permute-start.1 = (s32[3,64]{1,0:T(4,128)S(1)}, s32[3,64]{1,0:T(4,128)S(1)}, u32[]{:S(2)}, u32[]{:S(2)}) collective-permute-start(s32[3,64]{1,0:T(4,128)S(1)} %bitcast.26), channel_id=1, source_target_pairs={{0,1},{1,0},{2,3},{3,2},{4,6},{5,7},{6,4},{7,5},{8,9},{9,8},{10,11... | collective-permute-start | bytes 2312 | tf_op jit(solution)/shard_map/ppermute | solution.py:280
  3.9 6.9 %collective-permute-start.4 = (bf16[3,64,768]{2,1,0:T(8,128)(2,1)}, bf16[3,64,768]{2,1,0:T(8,128)(2,1)S(1)}, u32[]{:S(2)}, u32[]{:S(2)}) collective-permute-start(bf16[3,64,768]{2,1,0:T(8,128)(2,1)} %bitcast.18), channel_id=1, source_target_pairs={{0,2},{1,3},{2,0},{3,1},{4,5},{5,4},{6,7},{7,6},{8,10},{9,11},{10,... | collective-permute-start | bytes 884744 | tf_op jit(solution)/shard_map/ppermute | solution.py:280
  6.1 7.9 %collective-permute-start.5 = (bf16[3,64,768]{2,1,0:T(8,128)(2,1)S(1)}, bf16[3,64,768]{2,1,0:T(8,128)(2,1)S(1)}, u32[]{:S(2)}, u32[]{:S(2)}) collective-permute-start(bf16[3,64,768]{2,1,0:T(8,128)(2,1)S(1)} %collective-permute-done.t1), channel_id=1, source_target_pairs={{0,2},{1,3},{2,0},{3,1},{4,5},{5,4},{6,7},{7,6},{8,10},{9,11},{10,... | collective-permute-start | bytes 884744 | tf_op jit(solution)/shard_map/ppermute | solution.py:280
  7.4 1.2 %copy-start = (bf16[768,3,192]{0,2,1:T(8,128)(2,1)S(1)}, bf16[768,3,192]{0,2,1:T(8,128)(2,1)}, u32[]{:S(2)}) copy-start(bf16[768,3,192]{0,2,1:T(8,128)(2,1)} %param.16) | copy-start | bytes 2654212
  8.6 1.0 %copy-start.4 = (bf16[192,768]{1,0:T(8,128)(2,1)S(1)}, bf16[192,768]{1,0:T(8,128)(2,1)}, u32[]{:S(2)}) copy-start(bf16[192,768]{1,0:T(8,128)(2,1)} %u_own.1) | copy-start | bytes 884740
  9.5 1.3 %copy-start.2 = (bf16[64,3,768]{2,0,1:T(8,128)(2,1)S(1)}, bf16[64,3,768]{2,0,1:T(8,128)(2,1)}, u32[]{:S(2)}) copy-start(bf16[64,3,768]{2,0,1:T(8,128)(2,1)} %param.9) | copy-start | bytes 884740
  9.6 1.3 %copy-start.6 = (bf16[768,3,192]{0,2,1:T(8,128)(2,1)S(1)}, bf16[768,3,192]{0,2,1:T(8,128)(2,1)}, u32[]{:S(2)}) copy-start(bf16[768,3,192]{0,2,1:T(8,128)(2,1)} %param.13) | copy-start | bytes 2654212
  10.7 0.7 %copy-start.7 = (f32[768]{0:T(1024)S(1)}, f32[768]{0:T(1024)}, u32[]{:S(2)}) copy-start(f32[768]{0:T(1024)} %gain_ref.4) | copy-start | bytes 9220
  11.4 1.0 %copy-start.3 = (bf16[192,768]{1,0:T(8,128)(2,1)S(1)}, bf16[192,768]{1,0:T(8,128)(2,1)}, u32[]{:S(2)}) copy-start(bf16[192,768]{1,0:T(8,128)(2,1)} %w0.3) | copy-start | bytes 884740
  12.4 6.7 %collective-permute-start.7 = (bf16[1,192,768]{2,1,0:T(8,128)(2,1)S(1)}, bf16[1,192,768]{2,1,0:T(8,128)(2,1)S(1)}, u32[]{:S(2)}, u32[]{:S(2)}) collective-permute-start(bf16[1,192,768]{2,1,0:T(8,128)(2,1)S(1)} %bitcast.21), channel_id=1, source_target_pairs={{0,1},{1,0},{2,3},{3,2},{4,6},{5,7},{6,4},{7,5},{8,9},{9,8},{10,11... | collective-permute-start | bytes 884744 | tf_op jit(solution)/shard_map/ppermute | solution.py:280
  13.8 18.5 %collective-permute-start.15 = (bf16[4,96,768]{2,1,0:T(8,128)(2,1)S(1)}, bf16[4,96,768]{2,1,0:T(8,128)(2,1)S(1)}, u32[]{:S(2)}, u32[]{:S(2)}) collective-permute-start(bf16[4,96,768]{2,1,0:T(8,128)(2,1)S(1)} %get-tuple-element.45), channel_id=1, source_target_pairs={{0,2},{1,3},{2,0},{3,1},{4,5},{5,4},{6,7},{7,6},{8,10},{9,11},{10,... | collective-permute-start | bytes 1769480 | tf_op jit(solution)/shard_map/ppermute | solution.py:280
  16.5 6.4 %collective-permute-start.6 = (bf16[6,64,192]{2,1,0:T(8,128)(2,1)S(1)}, bf16[6,64,192]{2,1,0:T(8,128)(2,1)S(1)}, u32[]{:S(2)}, u32[]{:S(2)}) collective-permute-start(bf16[6,64,192]{2,1,0:T(8,128)(2,1)S(1)} %get-tuple-element.37), channel_id=1, source_target_pairs={{0,1},{1,0},{2,3},{3,2},{4,6},{5,7},{6,4},{7,5},{8,9},{9,8},{10,11... | collective-permute-start | bytes 442376 | tf_op jit(solution)/shard_map/ppermute | solution.py:280
  22.9 8.0 %copy-start.8 = (f32[768]{0:T(1024)S(1)}, f32[768]{0:T(1024)}, u32[]{:S(2)}) copy-start(f32[768]{0:T(1024)} %gain_ref.5) | copy-start | bytes 9220
  23.2 29.8 %copy-start.1 = (bf16[768,3,192]{0,2,1:T(8,128)(2,1)S(1)}, bf16[768,3,192]{0,2,1:T(8,128)(2,1)}, u32[]{:S(2)}) copy-start(bf16[768,3,192]{0,2,1:T(8,128)(2,1)} %param.16) | copy-start | bytes 2654212
  23.2 7.7 %collective-permute-start.8 = (bf16[3,64,768]{2,1,0:T(8,128)(2,1)S(1)}, bf16[3,64,768]{2,1,0:T(8,128)(2,1)S(1)}, u32[]{:S(2)}, u32[]{:S(2)}) collective-permute-start(bf16[3,64,768]{2,1,0:T(8,128)(2,1)S(1)} %part.1), channel_id=1, source_target_pairs={{0,2},{1,3},{2,0},{3,1},{4,5},{5,4},{6,7},{7,6},{8,10},{9,11},{10,... | collective-permute-start | bytes 884744 | tf_op jit(solution)/shard_map/ppermute | solution.py:280
  30.9 22.1 %copy-start.5 = (bf16[192,768]{1,0:T(8,128)(2,1)S(1)}, bf16[192,768]{1,0:T(8,128)(2,1)}, u32[]{:S(2)}) copy-start(bf16[192,768]{1,0:T(8,128)(2,1)} %u_own.1) | copy-start | bytes 884740
  31.9 21.0 %copy-start.10 = (s32[24]{0:T(128)S(1)}, s32[24]{0:T(128)}, u32[]{:S(2)}) copy-start(s32[24]{0:T(128)} %ids_ref.1) | copy-start | bytes 292
  32.0 16.0 %collective-permute-start.10 = (bf16[4,96,768]{2,1,0:T(8,128)(2,1)S(1)}, bf16[4,96,768]{2,1,0:T(8,128)(2,1)S(1)}, u32[]{:S(2)}, u32[]{:S(2)}) collective-permute-start(bf16[4,96,768]{2,1,0:T(8,128)(2,1)S(1)} %get-tuple-element.42), channel_id=1, source_target_pairs={{0,2},{1,3},{2,0},{3,1},{4,5},{5,4},{6,7},{7,6},{8,10},{9,11},{10,... | collective-permute-start | bytes 1769480 | tf_op jit(solution)/shard_map/ppermute | solution.py:280
  32.3 17.4 %collective-permute-start.18 = (bf16[4,96,768]{2,1,0:T(8,128)(2,1)S(1)}, bf16[4,96,768]{2,1,0:T(8,128)(2,1)S(1)}, u32[]{:S(2)}, u32[]{:S(2)}) collective-permute-start(bf16[4,96,768]{2,1,0:T(8,128)(2,1)S(1)} %collective-permute-done.15.c1), channel_id=1, source_target_pairs={{0,1},{1,0},{2,3},{3,2},{4,6},{5,7},{6,4},{7,5},{8,9},{9,8},{10,11... | collective-permute-start | bytes 1769480 | tf_op jit(solution)/shard_map/ppermute | solution.py:280
  32.6 10.4 %collective-permute-start.12 = (bf16[3,64,768]{2,1,0:T(8,128)(2,1)S(1)}, bf16[3,64,768]{2,1,0:T(8,128)(2,1)S(1)}, u32[]{:S(2)}, u32[]{:S(2)}) collective-permute-start(bf16[3,64,768]{2,1,0:T(8,128)(2,1)S(1)} %get-tuple-element.40.x0), channel_id=1, source_target_pairs={{8,16},{12,20},{16,8},{20,12},{9,17},{13,21},{17,9},{21,13},{10,18... | collective-permute-start | bytes 884744 | tf_op jit(solution)/shard_map/ppermute | solution.py:368
  35.8 12.2 %collective-permute-start.11 = (bf16[3,64,768]{2,1,0:T(8,128)(2,1)S(1)}, bf16[3,64,768]{2,1,0:T(8,128)(2,1)S(1)}, u32[]{:S(2)}, u32[]{:S(2)}) collective-permute-start(bf16[3,64,768]{2,1,0:T(8,128)(2,1)S(1)} %get-tuple-element.40.x0), channel_id=1, source_target_pairs={{0,8},{4,12},{8,0},{12,4},{16,24},{20,28},{24,16},{28,20},{1,9},{5... | collective-permute-start | bytes 884744 | tf_op jit(solution)/shard_map/ppermute | solution.py:367
  35.8 14.3 %collective-permute-start.9 = (bf16[3,64,768]{2,1,0:T(8,128)(2,1)S(1)}, bf16[3,64,768]{2,1,0:T(8,128)(2,1)S(1)}, u32[]{:S(2)}, u32[]{:S(2)}) collective-permute-start(bf16[3,64,768]{2,1,0:T(8,128)(2,1)S(1)} %get-tuple-element.40.x0), channel_id=1, source_target_pairs={{0,4},{4,0},{8,12},{12,8},{16,20},{20,16},{24,28},{28,24},{1,5},{5... | collective-permute-start | bytes 884744 | tf_op jit(solution)/shard_map/ppermute | solution.py:283
  43.0 10.0 %collective-permute-start.16 = (bf16[4,96,768]{2,1,0:T(8,128)(2,1)S(1)}, bf16[4,96,768]{2,1,0:T(8,128)(2,1)S(1)}, u32[]{:S(2)}, u32[]{:S(2)}) collective-permute-start(bf16[4,96,768]{2,1,0:T(8,128)(2,1)S(1)} %collective-permute-done.15.c1), channel_id=1, source_target_pairs={{0,4},{4,0},{8,12},{12,8},{16,20},{20,16},{24,28},{28,24},{1,5},{5... | collective-permute-start | bytes 1769480 | tf_op jit(solution)/shard_map/ppermute | solution.py:283
  47.9 5.0 %collective-permute-start.17 = (bf16[4,96,768]{2,1,0:T(8,128)(2,1)S(1)}, bf16[4,96,768]{2,1,0:T(8,128)(2,1)S(1)}, u32[]{:S(2)}, u32[]{:S(2)}) collective-permute-start(bf16[4,96,768]{2,1,0:T(8,128)(2,1)S(1)} %collective-permute-done.10.o1), channel_id=1, source_target_pairs={{0,4},{4,0},{8,12},{12,8},{16,20},{20,16},{24,28},{28,24},{1,5},{5... | collective-permute-start | bytes 1769480 | tf_op jit(solution)/shard_map/ppermute | solution.py:283
  49.6 3.3 %collective-permute-start.19 = (bf16[4,96,768]{2,1,0:T(8,128)(2,1)S(1)}, bf16[4,96,768]{2,1,0:T(8,128)(2,1)S(1)}, u32[]{:S(2)}, u32[]{:S(2)}) collective-permute-start(bf16[4,96,768]{2,1,0:T(8,128)(2,1)S(1)} %collective-permute-done.18.c3), channel_id=1, source_target_pairs={{0,4},{4,0},{8,12},{12,8},{16,20},{20,16},{24,28},{28,24},{1,5},{5... | collective-permute-start | bytes 1769480 | tf_op jit(solution)/shard_map/ppermute | solution.py:283
  49.7 2.8 %collective-permute-start.14 = (bf16[3,64,768]{2,1,0:T(8,128)(2,1)S(1)}, bf16[3,64,768]{2,1,0:T(8,128)(2,1)S(1)}, u32[]{:S(2)}, u32[]{:S(2)}) collective-permute-start(bf16[3,64,768]{2,1,0:T(8,128)(2,1)S(1)} %collective-permute-done.12.got2), channel_id=1, source_target_pairs={{0,4},{4,0},{8,12},{12,8},{16,20},{20,16},{24,28},{28,24},{1,5},{5... | collective-permute-start | bytes 884744 | tf_op jit(solution)/shard_map/ppermute | solution.py:283
  50.2 2.8 %collective-permute-start.13 = (bf16[3,64,768]{2,1,0:T(8,128)(2,1)S(1)}, bf16[3,64,768]{2,1,0:T(8,128)(2,1)S(1)}, u32[]{:S(2)}, u32[]{:S(2)}) collective-permute-start(bf16[3,64,768]{2,1,0:T(8,128)(2,1)S(1)} %collective-permute-done.11.got1), channel_id=1, source_target_pairs={{0,4},{4,0},{8,12},{12,8},{16,20},{20,16},{24,28},{28,24},{1,5},{5... | collective-permute-start | bytes 884744 | tf_op jit(solution)/shard_map/ppermute | solution.py:283
